TPU v7x, 32 devices: a whole 2x2x4 slice. The times are simulated.
32 devices in a mesh: groups: 2 (over y), expert: 4 (over x, core), dp: 4 (over z).
Axes of the slice: x: 2, y: 2, z: 4, core: 2. Of those that a mesh axis runs over, the one named last changes fastest.
Arguments:
- tokens: bfloat16 [1024, 4096], P(('groups', 'expert'), 'dp'), parts along dimension 0, may hold values from -6 to 6
- routes: int32 [1024, 2], P(('groups', 'expert')), parts along dimension 0, may hold values from 0 to 3, all different within a row; in each aligned block of 128 rows (0 to 127, 128 to 255, ...) at most 96 rows name the same one
- router_projection_weight: bfloat16 [4096, 4], P('dp'), may hold values from -0.09375 to 0.09375
- packed_quant_codes: int32 [4, 4096, 1536], P('expert', 'dp'), may hold values from 0 to 4095
- block_absmax_scales: float32 [4, 3, 4096, 24], P('expert', None, 'dp'), may hold values from 0.01 to 0.1
- gate_up_adapter_input: bfloat16 [4, 2, 4096, 64], P('expert', None, 'dp'), may hold values from -0.09375 to 0.09375
- gate_up_adapter_output: bfloat16 [4, 2, 64, 1536], P('expert'), may hold values from -0.75 to 0.75
- down_adapter_input: bfloat16 [4, 1536, 64], P('expert'), may hold values from -0.15625 to 0.15625
- down_adapter_output: bfloat16 [4, 64, 4096], P('expert', None, 'dp'), may hold values from -0.75 to 0.75
- cotangent: bfloat16 [1024, 4096], P(('groups', 'expert'), 'dp'), parts along dimension 0, may hold values from -6 to 6
Outputs:
- out_y: bfloat16 [1024, 4096], P(('groups', 'expert'), 'dp'), parts along dimension 0
- grad_tokens: bfloat16 [1024, 4096], P(('groups', 'expert'), 'dp'), parts along dimension 0
- grad_router: float32 [8192, 4], P(('groups', 'dp')), parts along dimension 0
- grad_gate_up_a: float32 [8, 2, 4096, 64], P(('groups', 'expert'), None, 'dp'), parts along dimension 0
- grad_gate_up_b: float32 [8, 2, 64, 1536], P(('groups', 'expert'), None, None, 'dp'), parts along dimension 0
- gradient_down_input: float32 [8, 1536, 64], P(('groups', 'expert'), 'dp'), parts along dimension 0
- gradient_down_output: float32 [8, 64, 4096], P(('groups', 'expert'), None, 'dp'), parts along dimension 0
There are 2 independent parts, one for each index of `groups`. A program takes and returns all parts, laid end to end along the dimension named above; an argument that names none is the same for every part. Nothing has to cross between parts.
Inputs may be any that keep to these rules, and one draw needn't show every extreme that they name: `routes`: each row names 2 different experts. In each aligned block of 128 rows (the tokens of one index of expert) no expert is named by more than 96 rows, a bound that some block reaches. `packed_quant_codes`: each entry holds three NF4 codes: gate in the lowest four bits, up in the next four, down in the next four.
All inputs are finite; a program needn't handle non-finite values.
Results may differ from a plain program's by a relative error of at most 0.02.
Values may be sent and summed in bfloat16 or wider, within the bound.
No kernel may reach another device: no remote copies, remote signals or barrier semaphores. Data moves between devices by JAX's collectives and lax.ppermute only.
A program may use at most 128 MiB of HBM per device.

v0:
```python
import jax
import jax.numpy as jnp
from jax import lax
from jax.sharding import PartitionSpec as P

NF4_LEVELS = (
    -1.0,
    -0.6961928009986877,
    -0.5250730514526367,
    -0.39491748809814453,
    -0.28444138169288635,
    -0.18477343022823334,
    -0.09105003625154495,
    0.0,
    0.07958029955625534,
    0.16093020141124725,
    0.24611230194568634,
    0.3379152424240112,
    0.44070982933044434,
    0.5626170039176941,
    0.7229568362236023,
    1.0,
)
ADAPTER_SCALE = 0.5


def dequantize(quant_codes, scale_values):
    fields = (quant_codes % 16, quant_codes // 16 % 16, quant_codes // 256)
    feature_rows, hidden_width = quant_codes.shape
    block_count = scale_values.shape[-1]
    result = []
    for field_index in range(3):
        levels_now = jnp.zeros(quant_codes.shape, jnp.float32)
        for code_value in range(16):
            levels_now = jnp.where(
                fields[field_index] == code_value, NF4_LEVELS[code_value], levels_now
            )
        scaled = (
            levels_now.reshape(feature_rows, block_count, hidden_width // block_count)
            * scale_values[field_index][:, :, None]
        )
        result.append(scaled.reshape(feature_rows, hidden_width).astype(jnp.bfloat16))
    return result


def pre_gradient(hidden_gradient, preactivation_kept):
    sigma_gate = jax.nn.sigmoid(preactivation_kept[:, 0])
    silu_gate = preactivation_kept[:, 0] * sigma_gate
    grad_gate = (
        hidden_gradient
        * preactivation_kept[:, 1]
        * sigma_gate
        * (1.0 + preactivation_kept[:, 0] * (1.0 - sigma_gate))
    )
    grad_up = hidden_gradient * silu_gate
    return jnp.stack([grad_gate, grad_up], axis=1).astype(jnp.bfloat16)


def contract_leading(left, right):
    return lax.dot_general(
        left, right, (((0,), (0,)), ((), ())), preferred_element_type=jnp.float32
    )


def contract_trailing(left, right):
    return lax.dot_general(
        left, right, (((1,), (1,)), ((), ())), preferred_element_type=jnp.float32
    )


def shards(
    tokens,
    routes,
    router_projection_weight,
    packed_quant_codes,
    block_absmax_scales,
    gate_up_adapter_input,
    gate_up_adapter_output,
    down_adapter_input,
    down_adapter_output,
    cotangent,
):
    token_count, feature_share = tokens.shape
    slot_count = routes.shape[1]
    expert_count = router_projection_weight.shape[1]
    capacity = 3 * token_count * slot_count // (2 * expert_count)
    hidden_width = packed_quant_codes.shape[2]
    share_width = hidden_width // lax.axis_size("dp")
    share_start = lax.axis_index("dp") * share_width
    logit_terms = jnp.dot(tokens, router_projection_weight, preferred_element_type=jnp.float32)
    logits = lax.psum(logit_terms, "dp")
    expert_iota = lax.broadcasted_iota(jnp.int32, (1, 1, expert_count), 2)
    route_mask = (routes[:, :, None] == expert_iota).astype(jnp.float32)
    chosen = jnp.sum(route_mask * logits[:, None, :], axis=2)
    margin = chosen[:, 0] - chosen[:, 1]
    gates = jnp.stack([jax.nn.sigmoid(margin), jax.nn.sigmoid(-margin)], axis=1)
    slot_cotangent = (gates[:, :, None] * cotangent[:, None, :].astype(jnp.float32)).astype(
        jnp.bfloat16
    )
    flat_routes = routes.reshape(-1)
    flat_mask = (
        flat_routes[:, None] == lax.broadcasted_iota(jnp.int32, (1, expert_count), 1)
    ).astype(jnp.int32)
    position = jnp.sum((jnp.cumsum(flat_mask, axis=0) - 1) * flat_mask, axis=1)
    slot_index = flat_routes * capacity + position

    def pack_rows(rows_in):
        buffer = (
            jnp.zeros((expert_count * capacity, feature_share), jnp.bfloat16)
            .at[slot_index]
            .set(rows_in)
        )
        return buffer.reshape(expert_count, capacity, feature_share)

    def unpack_rows(buffer):
        return buffer.reshape(expert_count * capacity, feature_share)[slot_index].reshape(
            token_count, slot_count, feature_share
        )

    gate_weight, up_weight, down_flipped_matrix = dequantize(
        packed_quant_codes[0], block_absmax_scales[0]
    )
    stacked_arrays = jnp.stack([gate_weight, up_weight])
    adapter_input_map = gate_up_adapter_input[0]
    adapter_output_map = gate_up_adapter_output[0]
    down_input_map = down_adapter_input[0]
    down_output_map = down_adapter_output[0]
    token_row_block = jnp.repeat(tokens, slot_count, axis=0)
    cot_flat = slot_cotangent.reshape(token_count * slot_count, feature_share)
    arrived = lax.all_to_all(
        pack_rows(token_row_block), "expert", split_axis=0, concat_axis=0, tiled=True
    )
    input_rows = arrived.reshape(-1, feature_share)
    lowrank_terms = jnp.einsum(
        "xt,vtm->xvm", input_rows, adapter_input_map, preferred_element_type=jnp.float32
    )
    pre_terms = jnp.einsum(
        "rd,jdf->rjf", input_rows, stacked_arrays, preferred_element_type=jnp.float32
    )
    preactivation_sum = lax.psum(pre_terms.astype(jnp.bfloat16), "dp").astype(jnp.float32)
    low_sum = lax.psum(lowrank_terms.astype(jnp.bfloat16), "dp")
    adapter_input = low_sum
    preactivation_kept = preactivation_sum + ADAPTER_SCALE * jnp.einsum(
        "bvw,vwu->bvu", adapter_input, adapter_output_map, preferred_element_type=jnp.float32
    )
    sigma_full = jax.nn.sigmoid(preactivation_kept[:, 0])
    hidden_units = (preactivation_kept[:, 0] * sigma_full * preactivation_kept[:, 1]).astype(
        jnp.bfloat16
    )
    hidden_lowrank = jnp.dot(
        hidden_units, down_input_map, preferred_element_type=jnp.float32
    ).astype(jnp.bfloat16)
    expert_output = (
        contract_trailing(hidden_units, down_flipped_matrix)
        + ADAPTER_SCALE
        * jnp.dot(hidden_lowrank, down_output_map, preferred_element_type=jnp.float32)
    ).astype(jnp.bfloat16)
    saved = (input_rows, adapter_input, preactivation_kept, hidden_units, hidden_lowrank)
    saved, expert_output = (saved, expert_output.reshape(expert_count, capacity, feature_share))
    returned_out = lax.all_to_all(expert_output, "expert", split_axis=0, concat_axis=0, tiled=True)
    arrived_cot = lax.all_to_all(
        pack_rows(cot_flat), "expert", split_axis=0, concat_axis=0, tiled=True
    )
    input_rows, adapter_input, preactivation_kept, hidden_units, hidden_lowrank = saved
    slot_row_block = arrived_cot.reshape(-1, feature_share)
    cot_terms = contract_trailing(slot_row_block, down_output_map)
    grad_terms = jnp.dot(slot_row_block, down_flipped_matrix, preferred_element_type=jnp.float32)
    gradient_total = lax.psum(grad_terms.astype(jnp.bfloat16), "dp").astype(jnp.float32)
    cotangent_sum = lax.psum(cot_terms.astype(jnp.bfloat16), "dp")
    hidden_gradient = gradient_total + ADAPTER_SCALE * contract_trailing(
        cotangent_sum, down_input_map
    )
    preactivation_gradient = pre_gradient(hidden_gradient, preactivation_kept)
    preactivation_lowrank = jnp.einsum(
        "vbc,bnc->vbn",
        preactivation_gradient,
        adapter_output_map,
        preferred_element_type=jnp.float32,
    ).astype(jnp.bfloat16)
    slot_gradient = (
        jnp.einsum(
            "hyl,yxl->hx",
            preactivation_gradient,
            stacked_arrays,
            preferred_element_type=jnp.float32,
        )
        + ADAPTER_SCALE
        * jnp.einsum(
            "csa,sga->cg",
            preactivation_lowrank,
            adapter_input_map,
            preferred_element_type=jnp.float32,
        )
    ).astype(jnp.bfloat16)
    adapter_input_gradient = ADAPTER_SCALE * jnp.einsum(
        "cu,cva->vua", input_rows, preactivation_lowrank, preferred_element_type=jnp.float32
    )
    pre_grad_share = lax.dynamic_slice_in_dim(preactivation_gradient, share_start, share_width, 2)
    adapter_output_gradient = ADAPTER_SCALE * jnp.einsum(
        "doi,dol->oil", adapter_input, pre_grad_share, preferred_element_type=jnp.float32
    )
    hidden_unit_columns = lax.dynamic_slice_in_dim(hidden_units, share_start, share_width, 1)
    down_input_gradient = ADAPTER_SCALE * contract_leading(hidden_unit_columns, cotangent_sum)
    down_output_gradient = ADAPTER_SCALE * contract_leading(hidden_lowrank, slot_row_block)
    grads = (
        adapter_input_gradient[None],
        adapter_output_gradient[None],
        down_input_gradient[None],
        down_output_gradient[None],
    )
    slot_grads, grads = (slot_gradient.reshape(expert_count, capacity, feature_share), grads)
    returned_grad = lax.all_to_all(slot_grads, "expert", split_axis=0, concat_axis=0, tiled=True)
    out_rows = unpack_rows(returned_out).astype(jnp.float32)
    grad_rows = unpack_rows(returned_grad).astype(jnp.float32)
    gate_terms = jnp.sum(cotangent.astype(jnp.float32)[:, None, :] * out_rows, axis=2)
    gate_grad = lax.psum(gate_terms, "dp")
    out_y = jnp.sum(gates[:, :, None] * out_rows, axis=1).astype(jnp.bfloat16)
    logit_step = gates[:, 0] * gates[:, 1] * (gate_grad[:, 0] - gate_grad[:, 1])
    logit_grad = (logit_step[:, None] * (route_mask[:, 0] - route_mask[:, 1])).astype(jnp.bfloat16)
    router_terms = contract_leading(tokens, logit_grad)
    grad_router = lax.psum(router_terms, "expert")
    grad_tokens = (
        jnp.sum(grad_rows, axis=1) + contract_trailing(logit_grad, router_projection_weight)
    ).astype(jnp.bfloat16)
    return (out_y, grad_tokens, grad_router, grads[0], grads[1], grads[2], grads[3])


def solution(mesh):
    in_specs = (
        P(("groups", "expert"), "dp"),
        P(("groups", "expert"), None),
        P("dp", None),
        P("expert", "dp", None),
        P("expert", None, "dp", None),
        P("expert", None, "dp", None),
        P("expert", None, None, None),
        P("expert", None, None),
        P("expert", None, "dp"),
        P(("groups", "expert"), "dp"),
    )
    out_specs = (
        P(("groups", "expert"), "dp"),
        P(("groups", "expert"), "dp"),
        P(("groups", "dp"), None),
        P(("groups", "expert"), None, "dp", None),
        P(("groups", "expert"), None, None, "dp"),
        P(("groups", "expert"), "dp", None),
        P(("groups", "expert"), None, "dp"),
    )
    return jax.shard_map(shards, mesh=mesh, in_specs=in_specs, out_specs=out_specs, check_vma=False)
```

profile of v0, /device:TPU:0, one launch (start us, length us, event | category | flops | bytes accessed | tf_op | source)
XLA Modules:
  0.0 329.9 jit_solution(12455938390946149928)
XLA Ops:
  12.3 2.6 scatter_custom_fusion
  14.9 4.2 %all-to-all-start = ((bf16[4,96,1024]{2,1,0:T(8,128)(2,1)}), bf16[4,96,1024]{2,1,0:T(8,128)(2,1)S(1)}, u32[]{:S(2)}, u32[]{:S(2)}) async-start(bf16[4,96,1024]{2,1,0:T(8,128)(2,1)} %bitcast.4), calls=%async_computation | async-start | bytes 1572864 | tf_op jit(solution)/shard_map/all_to_all | solution.py:130
  19.1 6.6 %copy.79 = s32[1,1024,1536]{1,2,0:T(8,128)} copy(s32[1,1024,1536]{2,1,0:T(8,128)} %param.13) | data formatting | bytes 12582912 | tf_op args[3]
  26.4 3.4 %mul.220 = f32[1024,24,64]{0,2,1:T(8,128)} broadcast(f32[1024,24]{0,1:T(8,128)S(1)} %get-tuple-element.19), dimensions={0,1} | broadcast | bytes 6389760 | tf_op jit(solution)/shard_map/mul | solution.py:39
  29.8 6.5 %copy.77 = f32[1,1024,1536]{2,1,0:T(8,128)} copy(f32[1,1024,1536]{1,2,0:T(8,128)} %bitcast.159) | data formatting | bytes 12582912 | tf_op jit(solution)/shard_map/mul | solution.py:39
  36.4 3.4 %mul.224 = f32[1024,24,64]{0,2,1:T(8,128)} broadcast(f32[1024,24]{0,1:T(8,128)S(1)} %get-tuple-element.21), dimensions={0,1} | broadcast | bytes 6389760 | tf_op jit(solution)/shard_map/mul | solution.py:39
  39.8 6.6 %copy.78 = f32[1,1024,1536]{2,1,0:T(8,128)} copy(f32[1,1024,1536]{1,2,0:T(8,128)} %bitcast.160) | data formatting | bytes 12582912 | tf_op jit(solution)/shard_map/mul | solution.py:39
  48.5 23.9 %multiply_convert_fusion.2 = (bf16[1,1024,1536]{2,1,0:T(8,128)(2,1)}, bf16[1,1024,1536]{2,1,0:T(8,128)(2,1)}) fusion(f32[1,1024,1536]{2,1,0:T(8,128)} %copy.77, s32[1,1024,1536]{2,1,0:T(8,128)} %param.13, f32[1,1024,1536]{2,1,0:T(8,128)} %copy.78), kind=kLoop, calls=%fused_computation.23 | loop fusion | flops 154140672 | bytes 25165824 | tf_op jit(solution)/shard_map/convert_element_type | solution.py:42
  72.6 12.7 %psum.49 = f32[128,4]{0,1:T(4,128)S(1)} all-reduce(f32[128,4]{0,1:T(4,128)S(1)} %fusion.64), channel_id=1, replica_groups=mesh['groups'=2,'expert'=4,'dp'=4] {'dp'}, use_global_device_ids=true, to_apply=%region_0.0 | all-reduce | flops 512 | bytes 4096 | tf_op jit(solution)/shard_map/psum | solution.py:91
  86.2 2.7 scatter_custom_fusion.1
  88.9 3.5 %all-to-all-start.2 = ((bf16[4,96,1024]{2,1,0:T(8,128)(2,1)}), bf16[4,96,1024]{2,1,0:T(8,128)(2,1)S(1)}, u32[]{:S(2)}, u32[]{:S(2)}) async-start(bf16[4,96,1024]{2,1,0:T(8,128)(2,1)} %bitcast.168), calls=%async_computation.2 | async-start | bytes 1572864 | tf_op jit(solution)/shard_map/all_to_all | solution.py:161
  92.7 12.7 %multiply_convert_fusion = bf16[1024,24,64]{0,2,1:T(8,128)(2,1)} fusion(s32[1024,24,64]{0,2,1:T(8,128)} %bitcast.158, f32[1024,24]{0,1:T(8,128)} %get-tuple-element.20), kind=kLoop, calls=%fused_computation.19 | loop fusion | flops 77070336 | bytes 9535488 | tf_op jit(solution)/shard_map/convert_element_type | solution.py:42
  106.5 4.5 %convolution_convert_fusion = bf16[384,1536]{1,0:T(8,128)(2,1)} fusion(bf16[384,1024]{1,0:T(8,128)(2,1)S(1)} %bitcast.164, bf16[1024,1536]{0,1:T(8,128)(2,1)} %bitcast.169), kind=kOutput, calls=%fused_computation.33 | convolution fusion | flops 1208549376 | bytes 5111808 | tf_op jit(solution)/shard_map/dot_general | solution.py:167
  111.0 3.9 %fusion.7 = bf16[384,2,1536]{2,0,1:T(8,128)(2,1)} fusion(bf16[384,1024,1]{1,0,2:T(8,128)(2,1)S(1)} %bitcast.162, bf16[1,1024,1536]{2,1,0:T(8,128)(2,1)S(1)} %copy-done.5, bf16[1,1024,1536]{2,1,0:T(8,128)(2,1)S(1)} %copy-done.3), kind=kOutput, calls=%fused_computation.30 | convolution fusion | flops 2429681664 | bytes 9437184 | tf_op jit(solution)/shard_map/rd,jdf->rjf/dot_general | solution.py:137
  116.7 17.6 %psum.53 = bf16[384,64]{0,1:T(8,128)(2,1)S(1)} all-reduce(bf16[384,64]{0,1:T(8,128)(2,1)S(1)} %convolution_convert_fusion.1), channel_id=1, replica_groups=mesh['groups'=2,'expert'=4,'dp'=4] {'dp'}, use_global_device_ids=true, to_apply=%region_11.12 | all-reduce | flops 24576 | bytes 98304 | tf_op jit(solution)/shard_map/psum | solution.py:169
  134.4 118.5 %all-reduce.3.cloned.1.call-done = (bf16[384,2,1536]{2,0,1:T(8,128)(2,1)}, bf16[384,2,64]{0,2,1:T(8,128)(2,1)}, bf16[384,1536]{1,0:T(8,128)(2,1)}) async-done(((bf16[384,2,1536]{2,0,1:T(8,128)(2,1)}, bf16[384,2,64]{0,2,1:T(8,128)(2,1)}, bf16[384,1536]{1,0:T(8,128)(2,1)}), (bf16[384,2,1536]{2,0,1:T(8,128)(2,1)}, bf16[384,2,64]{0,2,1:T(8,128)(2,1)}, bf16[384,1536]{1,0:T(8,128)(2,1)})) %all-reduce.3.cloned.1.call-update) | async-done | bytes 3637264 | tf_op jit(solution)/shard_map/psum | solution.py:140
  252.9 2.5 bitcast_add_fusion
  262.9 3.7 %all-to-all-start.1 = ((bf16[4,96,1024]{2,1,0:T(8,128)(2,1)}), bf16[4,96,1024]{2,1,0:T(8,128)(2,1)S(1)}, u32[]{:S(2)}, u32[]{:S(2)}) async-start(bf16[4,96,1024]{2,1,0:T(8,128)(2,1)} %bitcast.23), calls=%async_computation.1 | async-start | bytes 1572864 | tf_op jit(solution)/shard_map/all_to_all | solution.py:160
  266.6 5.7 %fusion.25 = (bf16[384,1,1536]{2,0,1:T(8,128)(2,1)S(1)}, bf16[384,1,1536]{2,0,1:T(8,128)(2,1)S(1)}, f32[384,1536]{1,0:T(8,128)}) fusion(f32[384,2,1536]{2,0,1:T(8,128)} %copy-done.1, bf16[384,64]{0,1:T(8,128)(2,1)S(1)} %psum.53, bf16[1,1536,64]{1,2,0:T(8,128)(2,1)S(1)} %copy-done.21, bf16[384,1536]{1,0:T(8,128)(2,1)} %get-tuple-element.11), kind=kOutput, calls=%fused_computation.63 | convolution fusion | flops 84934656 | bytes 10862592 | tf_op jit(solution)/shard_map/dot_general | solution.py:66
  272.3 2.6 fusion.4
  278.0 3.5 %all-to-all-start.3 = ((bf16[4,96,1024]{2,1,0:T(8,128)(2,1)}), bf16[4,96,1024]{2,1,0:T(8,128)(2,1)S(1)}, u32[]{:S(2)}, u32[]{:S(2)}) async-start(bf16[4,96,1024]{2,1,0:T(8,128)(2,1)} %bitcast.167), calls=%async_computation.3 | async-start | bytes 1572864 | tf_op jit(solution)/shard_map/all_to_all | solution.py:212
  296.8 3.6 %multiply_reduce_fusion = (f32[128,2]{1,0:T(8,128)S(1)}, bf16[128,1024]{1,0:T(8,128)(2,1)}) fusion(f32[128,2,1024]{2,1,0:T(2,128)S(1)} %reshape.175, f32[128,1024]{1,0:T(8,128)} %convert_element_type.124, f32[128,2]{1,0:T(8,128)S(1)} %copy-done.15), kind=kLoop, calls=%fused_computation.75 | loop fusion | flops 917248 | bytes 1837056 | tf_op jit(solution)/shard_map/reduce_sum | solution.py:215
  300.5 9.5 %psum.54 = f32[128,2]{0,1:T(2,128)S(1)} all-reduce(f32[128,2]{0,1:T(2,128)S(1)} %copy.81), channel_id=1, replica_groups=mesh['groups'=2,'expert'=4,'dp'=4] {'dp'}, use_global_device_ids=true, to_apply=%region_14.15 | all-reduce | flops 256 | bytes 2048 | tf_op jit(solution)/shard_map/psum | solution.py:216
  312.4 10.7 %psum.55 = f32[1024,4]{0,1:T(4,128)} all-reduce(f32[1024,4]{0,1:T(4,128)S(1)} %convolution_bitcast_fusion), channel_id=1, replica_groups=mesh['groups'=2,'expert'=4,'dp'=4] {'expert'}, use_global_device_ids=true, to_apply=%region_15.16 | all-reduce | flops 4096 | bytes 32768 | tf_op jit(solution)/shard_map/psum | solution.py:221
  (117 shorter events, 40.1 us)
Async XLA Ops:
  7.2 245.7 %copy-start = (bf16[1,2,64,1536]{3,2,1,0:T(8,128)(2,1)S(1)}, bf16[1,2,64,1536]{3,2,1,0:T(8,128)(2,1)}, u32[]{:S(2)}) copy-start(bf16[1,2,64,1536]{3,2,1,0:T(8,128)(2,1)} %param.16) | copy-start | bytes 1179652
  14.9 74.0 %all-to-all-start = ((bf16[4,96,1024]{2,1,0:T(8,128)(2,1)}), bf16[4,96,1024]{2,1,0:T(8,128)(2,1)S(1)}, u32[]{:S(2)}, u32[]{:S(2)}) async-start(bf16[4,96,1024]{2,1,0:T(8,128)(2,1)} %bitcast.4), calls=%async_computation | async-start | bytes 1572864 | tf_op jit(solution)/shard_map/all_to_all | solution.py:130
  19.1 6.6 %copy-start.19 = (f32[1,3,1024,24]{2,3,1,0:T(8,128)S(1)}, f32[1,3,1024,24]{2,3,1,0:T(8,128)}, u32[]{:S(2)}) copy-start(f32[1,3,1024,24]{2,3,1,0:T(8,128)} %param.14) | copy-start | bytes 884740
  39.8 6.6 %copy-start.12 = (bf16[128,1024]{1,0:T(8,128)(2,1)S(1)}, bf16[128,1024]{1,0:T(8,128)(2,1)}, u32[]{:S(2)}) copy-start(bf16[128,1024]{1,0:T(8,128)(2,1)} %param.19) | copy-start | bytes 786436
  48.5 23.9 %copy-start.8 = (bf16[128,1024]{1,0:T(8,128)(2,1)S(1)}, bf16[128,1024]{1,0:T(8,128)(2,1)}, u32[]{:S(2)}) copy-start(bf16[128,1024]{1,0:T(8,128)(2,1)} %param.10) | copy-start | bytes 786436
  48.5 24.0 %copy-start.22 = (bf16[1024,4]{0,1:T(4,128)(2,1)S(1)}, bf16[1024,4]{0,1:T(4,128)(2,1)}, u32[]{:S(2)}) copy-start(bf16[1024,4]{0,1:T(4,128)(2,1)} %param.12) | copy-start | bytes 24580
  48.5 36.8 %copy-start.23 = (s32[128,2]{0,1:T(2,128)S(1)}, s32[128,2]{0,1:T(2,128)}, u32[]{:S(2)}) copy-start(s32[128,2]{0,1:T(2,128)} %param.11) | copy-start | bytes 3076
  48.5 37.7 %copy-start.2 = (f32[256,1024]{1,0:T(8,128)S(1)}, f32[256,1024]{1,0:T(8,128)}, u32[]{:S(2)}) copy-start(f32[256,1024]{1,0:T(8,128)} %mul.240) | copy-start | bytes 3145732
  86.1 19.4 %copy-start.14 = (f32[128,2]{1,0:T(8,128)}, f32[128,2]{1,0:T(8,128)S(1)}, u32[]{:S(2)}) copy-start(f32[128,2]{1,0:T(8,128)S(1)} %copy.71) | copy-start | bytes 3076
  88.9 17.5 %all-to-all-start.2 = ((bf16[4,96,1024]{2,1,0:T(8,128)(2,1)}), bf16[4,96,1024]{2,1,0:T(8,128)(2,1)S(1)}, u32[]{:S(2)}, u32[]{:S(2)}) async-start(bf16[4,96,1024]{2,1,0:T(8,128)(2,1)} %bitcast.168), calls=%async_computation.2 | async-start | bytes 1572864 | tf_op jit(solution)/shard_map/all_to_all | solution.py:161
  92.4 160.4 %all-reduce.3.cloned.1.call-start = ((), (), s32[]{:S(2)}) async-start(), calls=%async_computation.4 | async-start | bytes 7274496 | tf_op jit(solution)/shard_map/psum | solution.py:140
  92.7 12.8 %copy-start.13 = (bf16[1,2,1024,64]{2,3,1,0:T(8,128)(2,1)S(1)}, bf16[1,2,1024,64]{2,3,1,0:T(8,128)(2,1)}, u32[]{:S(2)}) copy-start(bf16[1,2,1024,64]{2,3,1,0:T(8,128)(2,1)} %param.15) | copy-start | bytes 786436
  134.3 132.3 %copy-start.20 = (bf16[384,64]{0,1:T(8,128)(2,1)}, bf16[384,64]{0,1:T(8,128)(2,1)S(1)}, u32[]{:S(2)}) copy-start(bf16[384,64]{0,1:T(8,128)(2,1)S(1)} %psum.53) | copy-start | bytes 147460
  255.4 5.6 %copy-start.1 = (f32[384,2,1536]{2,0,1:T(8,128)}, f32[384,2,1536]{2,0,1:T(8,128)S(1)}, u32[]{:S(2)}) copy-start(f32[384,2,1536]{2,0,1:T(8,128)S(1)} %bitcast_add_fusion) | copy-start | bytes 14155780
  261.6 10.8 %copy-start.17 = (bf16[384,64]{0,1:T(8,128)(2,1)}, bf16[384,64]{0,1:T(8,128)(2,1)S(1)}, u32[]{:S(2)}) copy-start(bf16[384,64]{0,1:T(8,128)(2,1)S(1)} %fusion.31) | copy-start | bytes 147460
  262.9 15.1 %all-to-all-start.1 = ((bf16[4,96,1024]{2,1,0:T(8,128)(2,1)}), bf16[4,96,1024]{2,1,0:T(8,128)(2,1)S(1)}, u32[]{:S(2)}, u32[]{:S(2)}) async-start(bf16[4,96,1024]{2,1,0:T(8,128)(2,1)} %bitcast.23), calls=%async_computation.1 | async-start | bytes 1572864 | tf_op jit(solution)/shard_map/all_to_all | solution.py:160
  266.6 5.7 %copy-start.4 = (bf16[1,1024,1536]{2,1,0:T(8,128)(2,1)S(1)}, bf16[1,1024,1536]{2,1,0:T(8,128)(2,1)}, u32[]{:S(2)}) copy-start(bf16[1,1024,1536]{2,1,0:T(8,128)(2,1)} %get-tuple-element.14) | copy-start | bytes 9437188
  266.6 5.7 %copy-start.6 = (bf16[1,1024,1536]{2,1,0:T(8,128)(2,1)S(1)}, bf16[1,1024,1536]{2,1,0:T(8,128)(2,1)}, u32[]{:S(2)}) copy-start(bf16[1,1024,1536]{2,1,0:T(8,128)(2,1)} %get-tuple-element.15) | copy-start | bytes 9437188
  275.9 13.5 %copy-start.24 = (s32[1024]{0:T(1024)S(1)}, s32[1024]{0:T(1024)}, u32[]{:S(2)}) copy-start(s32[1024]{0:T(1024)} %pad_clamp_fusion) | copy-start | bytes 12292
  278.0 15.1 %all-to-all-start.3 = ((bf16[4,96,1024]{2,1,0:T(8,128)(2,1)}), bf16[4,96,1024]{2,1,0:T(8,128)(2,1)S(1)}, u32[]{:S(2)}, u32[]{:S(2)}) async-start(bf16[4,96,1024]{2,1,0:T(8,128)(2,1)} %bitcast.167), calls=%async_computation.3 | async-start | bytes 1572864 | tf_op jit(solution)/shard_map/all_to_all | solution.py:212
  291.3 5.4 %copy-start.15 = (f32[128,2]{1,0:T(8,128)S(1)}, f32[128,2]{1,0:T(8,128)}, u32[]{:S(2)}) copy-start(f32[128,2]{1,0:T(8,128)} %copy-done.14) | copy-start | bytes 3076
  291.3 18.6 %copy-start.26 = (f32[128,1]{0,1:T(1,128)S(1)}, f32[128,1]{0,1:T(1,128)}, u32[]{:S(2)}) copy-start(f32[128,1]{0,1:T(1,128)} %copy-done.25) | copy-start | bytes 1540
  291.4 18.6 %copy-start.28 = (f32[128,1]{0,1:T(1,128)S(1)}, f32[128,1]{0,1:T(1,128)}, u32[]{:S(2)}) copy-start(f32[128,1]{0,1:T(1,128)} %copy-done.27) | copy-start | bytes 1540
  291.4 18.6 %copy-start.9 = (bf16[128,1024]{1,0:T(8,128)(2,1)S(1)}, bf16[128,1024]{1,0:T(8,128)(2,1)}, u32[]{:S(2)}) copy-start(bf16[128,1024]{1,0:T(8,128)(2,1)} %param.10) | copy-start | bytes 786436
  (10 other events, 30.7 us)
Sparse Core Ops, SparseCore 0:
  115.0 137.8 all-reduce.2
where the time goes:
time: 331 us; the launch traced here: 330 us
  waiting for transfers between devices  119 us (36%)
  other arithmetic  50.6 us (15%)
  blocking collectives  50.5 us (15%)
  local copies, waits for them, and re-layouts  45.4 us (14%)
  matrix products  34.5 us (10%)
  starting transfers between devices  15.1 us (5%)
  between operations  14.4 us (4%)
    psum x1, waiting for transfers between devices, shards(): lax.psum(pre_terms.astype(jnp.bfloat16), 'dp').astype(jnp.float32)  119 us
    convert_element_type x2, other arithmetic, dequantize(): scaled.reshape(feature_rows, hidden_width).astype(jnp.bfloat16)  36.7 us
    mul x5, local copies, waits for them, and re-layouts, dequantize(): levels_now.reshape(feature_rows, block_count, hidden_width // block_count)  20.6 us
    psum x1, blocking collectives, shards(): cotangent_sum = lax.psum(cot_terms.astype(jnp.bfloat16), 'dp')  17.6 us
    psum x1, blocking collectives, shards(): logits = lax.psum(logit_terms, 'dp')  12.7 us
    psum x1, blocking collectives, shards(): grad_router = lax.psum(router_terms, 'expert')  10.7 us
    unnamed x60, local copies, waits for them, and re-layouts  10.2 us
    psum x1, blocking collectives, shards(): gate_grad = lax.psum(gate_terms, 'dp')  9.47 us
  transfers between devices with their start and end apart: 5, of which 2 were waited for; matrix products, arithmetic and copies ran while one was open for 29% of the time, Pallas kernels for 0%

commit v1 on v0

v1 whole, which is shorter than its diff:
```python
import functools

import jax
import jax.numpy as jnp
from jax import lax
from jax.experimental import pallas as pl
from jax.experimental.pallas import tpu as pltpu
from jax.sharding import PartitionSpec as P

NF4_LEVELS = (
    -1.0,
    -0.6961928009986877,
    -0.5250730514526367,
    -0.39491748809814453,
    -0.28444138169288635,
    -0.18477343022823334,
    -0.09105003625154495,
    0.0,
    0.07958029955625534,
    0.16093020141124725,
    0.24611230194568634,
    0.3379152424240112,
    0.44070982933044434,
    0.5626170039176941,
    0.7229568362236023,
    1.0,
)
SCALE = 0.5
BF16 = jnp.bfloat16
F32 = jnp.float32
LAG = 2
INWARD = [(0, 1), (3, 2)]
MIDDLE = [(1, 2), (2, 1)]
OUTWARD = [(1, 0), (2, 3)]


def dot(left, right):
    return jnp.dot(left, right, preferred_element_type=F32)


def dot_tn(left, right):
    return lax.dot_general(left, right, (((0,), (0,)), ((), ())), preferred_element_type=F32)


def dot_nt(left, right):
    return lax.dot_general(left, right, (((1,), (1,)), ((), ())), preferred_element_type=F32)


def dequantize_kernel(code_ref, scale_ref, level_ref, spread_ref, out_ref, *, field):
    rows, width = code_ref.shape
    step = 64
    table = jnp.broadcast_to(level_ref[0:1, :], (step, 128))
    scales = scale_ref[0]
    high = scales.astype(BF16)
    rest = scales - high.astype(F32)
    middle = rest.astype(BF16)
    low = (rest - middle.astype(F32)).astype(BF16)
    for column in range(0, width, 128):
        spread = spread_ref[:, column : column + 128]
        wide = (dot(high, spread) + dot(middle, spread)) + dot(low, spread)
        for row in range(0, rows, step):
            code = (code_ref[row : row + step, column : column + 128] >> (4 * field)) & 15
            level = jnp.take_along_axis(table, code, axis=1)
            out_ref[row : row + step, column : column + 128] = (
                level * wide[row : row + step]
            ).astype(BF16)


def dequantize(codes, scales, levels, spread, field):
    features, width = codes.shape
    blocks = scales.shape[-1]
    rows = min(256, features)
    return pl.pallas_call(
        functools.partial(dequantize_kernel, field=field),
        grid=(features // rows,),
        in_specs=[
            pl.BlockSpec((rows, width), lambda i: (i, 0)),
            pl.BlockSpec((1, rows, blocks), lambda i: (field, i, 0)),
            pl.BlockSpec((8, 128), lambda i: (0, 0)),
            pl.BlockSpec((blocks, width), lambda i: (0, 0)),
        ],
        out_specs=pl.BlockSpec((rows, width), lambda i: (i, 0)),
        out_shape=jax.ShapeDtypeStruct((features, width), BF16),
        compiler_params=pltpu.CompilerParams(vmem_limit_bytes=32 * 2**20),
        cost_estimate=pl.CostEstimate(
            flops=6 * features * blocks * width, bytes_accessed=6 * features * width, transcendentals=0
        ),
    )(codes, scales, levels, spread)


def hop(value, step, count):
    return lax.ppermute(value, "expert", [(e, e ^ step) for e in range(count)])


def gather_sources(value, count):
    got = [value] + [None] * (count - 1)
    bits = [1 << b for b in range(count.bit_length() - 1)]
    for index in sorted(range(1, count), key=lambda i: bin(i).count("1")):
        low_bit = index & -index
        got[index] = hop(got[index ^ low_bit], low_bit, count)
    return got


def sum_tree(values):
    while len(values) > 1:
        values = [values[2 * i] + values[2 * i + 1] for i in range(len(values) // 2)]
    return values[0]


def sum_dp(value, parts):
    if parts & (parts - 1):
        return lax.psum(value, "dp")
    step = 1
    while step < parts:
        value = value + lax.ppermute(value, "dp", [(z, z ^ step) for z in range(parts)])
        step *= 2
    return value


def shards(
    tokens,
    routes,
    router_w,
    codes,
    scales,
    adapter_in,
    adapter_out,
    down_in,
    down_out,
    cotangent,
):
    token_count, features = tokens.shape
    slots = routes.shape[1]
    experts = router_w.shape[1]
    capacity = 3 * token_count * slots // (2 * experts)
    codes, scales = codes[0], scales[0]
    a_gate, a_up = adapter_in[0, 0], adapter_in[0, 1]
    b_gate, b_up = adapter_out[0, 0], adapter_out[0, 1]
    down_in, down_out = down_in[0], down_out[0]
    hidden_width = codes.shape[1]
    rank = a_gate.shape[1]
    blocks = scales.shape[-1]
    parts = lax.axis_size("dp")
    me = lax.axis_index("expert")
    z_index = lax.axis_index("dp")
    share = hidden_width // parts
    share_start = z_index * share

    all_tokens = gather_sources(tokens, experts)
    all_cots = gather_sources(cotangent, experts)
    routes_t = routes.T.astype(F32)
    logits = lax.dot_general(
        router_w, tokens, (((0,), (1,)), ((), ())), preferred_element_type=F32
    )
    logits = sum_dp(logits, parts)
    number = lax.broadcasted_iota(jnp.int32, (experts, 1), 0).astype(F32)
    chosen = [
        jnp.sum(jnp.where(routes_t[k : k + 1] == number, logits, 0.0), axis=0, keepdims=True)
        for k in range(2)
    ]
    margin = chosen[0] - chosen[1]
    gates = jnp.concatenate([jax.nn.sigmoid(margin), jax.nn.sigmoid(-margin)], axis=0)
    all_routes = gather_sources(routes_t, experts)
    all_gates = gather_sources(gates, experts)

    levels = jnp.zeros((8, 128), F32).at[:, :16].set(jnp.asarray(NF4_LEVELS, F32)[None])
    spread = (
        lax.broadcasted_iota(jnp.int32, (blocks, hidden_width), 0)
        == lax.broadcasted_iota(jnp.int32, (blocks, hidden_width), 1) // (hidden_width // blocks)
    ).astype(BF16)
    weights = [dequantize(codes, scales, levels, spread, field) for field in range(3)]

    me_f = me.astype(F32)
    before = (
        lax.broadcasted_iota(jnp.int32, (token_count, token_count), 0)
        < lax.broadcasted_iota(jnp.int32, (token_count, token_count), 1)
    ).astype(BF16)
    row_number = lax.broadcasted_iota(jnp.int32, (capacity, 1), 0).astype(F32)

    per_chunk = max(1, experts // 4)
    order = [list(range(i, i + per_chunk)) for i in range(0, experts, per_chunk)]
    if len(order) == 4:
        order = [order[0], order[2], order[3], order[1]]
    picks = {}
    row_gate = {}

    def build_picks(i):
        first = all_routes[i][0:1] == me_f
        second = all_routes[i][1:2] == me_f
        mine = first | second
        place = dot(jnp.broadcast_to(mine.astype(BF16), (8, token_count)), before)[0:1]
        pick = mine & (place == row_number)
        gate = jnp.where(first, all_gates[i][0:1], all_gates[i][1:2])
        picks[i] = pick
        row_gate[i] = jnp.sum(jnp.where(pick, gate, 0.0), axis=1, keepdims=True)

    chunk_x, chunk_c = {}, {}

    def unit_term(n, j):
        if j == 0:
            for i in order[n]:
                build_picks(i)
            chunk_x[n] = jnp.concatenate(
                [dot(picks[i].astype(BF16), all_tokens[i]).astype(BF16) for i in order[n]], axis=0
            )
            low = dot(chunk_x[n], jnp.concatenate([a_gate, a_up], axis=1))
            return jnp.concatenate([dot(chunk_x[n], weights[0]).astype(BF16), low.astype(BF16)], axis=1)
        if j == 1:
            return dot(chunk_x[n], weights[1]).astype(BF16)
        chunk_c[n] = jnp.concatenate(
            [dot(picks[i].astype(BF16), all_cots[i]).astype(BF16) for i in order[n]], axis=0
        )
        low = dot_nt(chunk_c[n], down_out)
        return jnp.concatenate([dot(chunk_c[n], weights[2]).astype(BF16), low.astype(BF16)], axis=1)

    saved = {}
    own_parts, back = [], {}
    gate_terms = {}

    def finish(n, sums):
        gate_sum, up_sum, grad_sum = sums
        low_gate = gate_sum[:, hidden_width : hidden_width + rank]
        low_up = gate_sum[:, hidden_width + rank :]
        cot_low = grad_sum[:, hidden_width:]
        gate_of = jnp.concatenate([row_gate[i] for i in order[n]], axis=0)
        g = gate_sum[:, :hidden_width].astype(F32) + SCALE * dot(low_gate, b_gate)
        u = up_sum.astype(F32) + SCALE * dot(low_up, b_up)
        h = grad_sum[:, :hidden_width].astype(F32) + SCALE * dot_nt(cot_low, down_in)
        sigma = jax.nn.sigmoid(g)
        silu = g * sigma
        hidden = (silu * u).astype(BF16)
        gate_grad = jnp.sum(hidden.astype(F32) * h, axis=1, keepdims=True)
        hg = h * gate_of
        grad_gate = (hg * u * sigma * (1.0 + g * (1.0 - sigma))).astype(BF16)
        grad_up = (hg * silu).astype(BF16)
        hidden_low = dot(hidden, down_in).astype(BF16)
        out = (dot_nt(hidden, weights[2]) + SCALE * dot(hidden_low, down_out)) * gate_of
        low_g = dot_nt(grad_gate, b_gate).astype(BF16)
        low_u = dot_nt(grad_up, b_up).astype(BF16)
        slot = (dot_nt(grad_gate, weights[0]) + dot_nt(grad_up, weights[1])) + SCALE * (
            dot_nt(low_g, a_gate) + dot_nt(low_u, a_up)
        )
        both = jnp.concatenate([out.astype(BF16), slot.astype(BF16)], axis=1)
        saved[n] = (
            low_gate,
            low_up,
            lax.dynamic_slice_in_dim(grad_gate, share_start, share, 1),
            lax.dynamic_slice_in_dim(grad_up, share_start, share, 1),
            lax.dynamic_slice_in_dim(hidden, share_start, share, 1),
            (cot_low.astype(F32) * gate_of).astype(BF16),
            (hidden_low.astype(F32) * gate_of).astype(BF16),
            low_g,
            low_u,
        )
        dense = []
        for at, i in enumerate(order[n]):
            rows = slice(at * capacity, (at + 1) * capacity)
            dense.append(dot_tn(picks[i].astype(BF16), both[rows]).astype(BF16))
            sign = jnp.where(all_routes[i][0:1] == me_f, 1.0, -1.0)
            gate_terms[i] = sign * jnp.sum(
                jnp.where(picks[i], gate_grad[rows], 0.0), axis=0, keepdims=True
            )
        return dense

    def send_back(n, dense):
        for at, i in enumerate(order[n]):
            back[i] = dense[at] if i == 0 else hop(dense[at], i, experts)

    chunks = len(order)
    units = [(n, j) for n in range(chunks) for j in range(3)]
    total = len(units)
    if parts == 4:
        end = (z_index == 0) | (z_index == 3)
        term, came, inner, crossed, whole, outer, done = {}, {}, {}, {}, {}, {}, {}
        ready = {}
        for t in range(total + 3 * LAG + LAG):
            ka, kb, kc, kd = t, t - LAG, t - 2 * LAG, t - 3 * LAG
            live = {}
            if ka < total:
                live["a"] = unit_term(*units[ka])
            if 0 <= kb < total:
                live["b"] = term[kb] + came[kb]
            if 0 <= kc < total:
                live["c"] = inner[kc] + crossed[kc]
            if 0 <= kd < total:
                live["d"] = jnp.where(end, outer[kd], whole[kd])
            if t in ready:
                live["r"] = ready[t][1]
            live = lax.optimization_barrier(live)
            if "a" in live:
                term[ka] = live["a"]
                came[ka] = lax.ppermute(live["a"], "dp", INWARD)
            if "b" in live:
                inner[kb] = live["b"]
                crossed[kb] = lax.ppermute(live["b"], "dp", MIDDLE)
            if "c" in live:
                whole[kc] = live["c"]
                outer[kc] = lax.ppermute(live["c"], "dp", OUTWARD)
            if "d" in live:
                done[kd] = live["d"]
                if kd % 3 == 2:
                    n = kd // 3
                    dense = finish(n, [done[3 * n + j] for j in range(3)])
                    if t + 1 < total + 3 * LAG:
                        ready[t + 1] = (n, dense)
                    else:
                        send_back(n, dense)
            if "r" in live:
                send_back(ready[t][0], live["r"])
    else:
        for n in range(chunks):
            sums = [lax.psum(unit_term(n, j), "dp") for j in range(3)]
            send_back(n, finish(n, sums))

    signed = jnp.concatenate([gate_terms[i] for i in range(experts)], axis=0)
    gathered = gather_sources(signed, experts)
    lines = []
    router_terms = []
    for i in range(experts):
        margin_grad = sum_tree([gathered[j][i ^ j : (i ^ j) + 1] for j in range(experts)])
        step = all_gates[i][0:1] * all_gates[i][1:2] * margin_grad
        line = step * (
            (all_routes[i][0:1] == number).astype(F32) - (all_routes[i][1:2] == number).astype(F32)
        )
        lines.append(line.astype(BF16))
        router_terms.append(
            lax.dot_general(
                all_tokens[i], lines[i], (((0,), (1,)), ((), ())), preferred_element_type=F32
            )
        )
    grad_router = sum_tree(router_terms)

    out_y = sum_tree([back[i][:, :features].astype(F32) for i in range(experts)]).astype(BF16)
    slot_sum = sum_tree([back[i][:, features:].astype(F32) for i in range(experts)])
    grad_tokens = (
        slot_sum
        + lax.dot_general(lines[0], router_w, (((0,), (1,)), ((), ())), preferred_element_type=F32)
    ).astype(BF16)

    def stacked(values):
        return jnp.concatenate(values, axis=0)

    s = [stacked([saved[n][f] for n in range(chunks)]) for f in range(9)]
    x_all = stacked([chunk_x[n] for n in range(chunks)])
    c_all = stacked([chunk_c[n] for n in range(chunks)])
    grad_a = SCALE * jnp.stack([dot_tn(x_all, s[7]), dot_tn(x_all, s[8])])
    grad_b = SCALE * jnp.stack([dot_tn(s[0], s[2]), dot_tn(s[1], s[3])])
    grad_di = SCALE * dot_tn(s[4], s[5])
    grad_do = SCALE * dot_tn(s[6], c_all)
    return out_y, grad_tokens, grad_router, grad_a[None], grad_b[None], grad_di[None], grad_do[None]


def solution(mesh):
    in_specs = (
        P(("groups", "expert"), "dp"),
        P(("groups", "expert"), None),
        P("dp", None),
        P("expert", "dp", None),
        P("expert", None, "dp", None),
        P("expert", None, "dp", None),
        P("expert", None, None, None),
        P("expert", None, None),
        P("expert", None, "dp"),
        P(("groups", "expert"), "dp"),
    )
    out_specs = (
        P(("groups", "expert"), "dp"),
        P(("groups", "expert"), "dp"),
        P(("groups", "dp"), None),
        P(("groups", "expert"), None, "dp", None),
        P(("groups", "expert"), None, None, "dp"),
        P(("groups", "expert"), "dp", None),
        P(("groups", "expert"), None, "dp"),
    )
    return jax.shard_map(shards, mesh=mesh, in_specs=in_specs, out_specs=out_specs, check_vma=False)
```

time: 331 us -> 249 us (0.75)
  waiting for transfers between devices: 119 us -> 42.3 us
  starting transfers between devices: 15.1 us -> 82.1 us
  blocking collectives: 50.5 us -> 0 us
  local copies, waits for them, and re-layouts: 45.4 us -> 14.9 us
  matrix products: 34.5 us -> 62 us
  other arithmetic: 50.6 us -> 28.5 us
  Pallas kernels: 0 us -> 14.4 us
  between operations: 14.4 us -> 2.92 us
    psum x1 -> x0, waiting for transfers between devices: 119 us -> none  [shards(): lax.psum(pre_terms.astype(jnp.bfloat16), 'dp').astype(jnp.float32)]
    ppermute x0 -> x56, starting transfers between devices: none -> 82.1 us  [the longest x12 44.6 us: shards(): came[ka] = lax.ppermute(live['a'], 'dp', INWARD)]
    psum x4 -> x0, blocking collectives: 50.5 us -> none  [the longest x1 17.6 us: shards(): cotangent_sum = lax.psum(cot_terms.astype(jnp.bfloat16), 'dp')]
    ppermute x0 -> x56, waiting for transfers between devices: none -> 42.3 us  [the longest x12 34.2 us: shards(): outer[kc] = lax.ppermute(live['c'], 'dp', OUTWARD)]
    convert_element_type x7 -> x9, other arithmetic: 38.2 us -> 3.14 us  [the longest x4 1.52 us: finish(): grad_up = (hg * silu).astype(BF16)]
    dot_general x18 -> x96, matrix products: 34.1 us -> 62 us  [the longest x44 33.9 us: dot(): return jnp.dot(left, right, preferred_element_type=F32)]
    mul x10 -> x0, local copies, waits for them, and re-layouts: 23.1 us -> none  [the longest x5 20.6 us: dequantize(): levels_now.reshape(feature_rows, block_count, hidden_width // block_count)]
    all_to_all x4 -> x0, starting transfers between devices: 14.9 us -> none  [the longest x1 4.21 us: shards(): lax.all_to_all(pack_rows(token_row_block), 'expert', split_axis=0, concat...]
  transfers between devices with their start and end apart: 5 -> 56, of which waited for: 2 -> 15; matrix products, arithmetic and copies ran while one was open for 29% -> 33% of each run, Pallas kernels for 0% -> 6%
where the time goes in v1:
time: 249 us; the launch traced here: 247 us
  starting transfers between devices  82.1 us (33%)
  matrix products  62 us (25%)
  waiting for transfers between devices  42.3 us (17%)
  other arithmetic  28.5 us (11%)
  local copies, waits for them, and re-layouts  14.9 us (6%)
  Pallas kernels  14.4 us (6%)
  between operations  2.92 us (1%)
    ppermute x12, starting transfers between devices, shards(): came[ka] = lax.ppermute(live['a'], 'dp', INWARD)  44.6 us
    ppermute x12, waiting for transfers between devices, shards(): outer[kc] = lax.ppermute(live['c'], 'dp', OUTWARD)  34.2 us
    dot_general x44, matrix products, dot(): return jnp.dot(left, right, preferred_element_type=F32)  33.9 us
    dot_general x36, matrix products, dot_nt(): lax.dot_general(left, right, (((1,), (1,)), ((), ())), preferred_element_...  19 us
    ppermute x12, starting transfers between devices, shards(): outer[kc] = lax.ppermute(live['c'], 'dp', OUTWARD)  15.5 us
    pallas_call x3, Pallas kernels, dequantize(): pl.pallas_call(functools.partial(dequantize_kernel, field=field), grid=(f...  14.4 us
    unnamed x169, local copies, waits for them, and re-layouts  12.4 us
    ppermute x12, starting transfers between devices, shards(): crossed[kb] = lax.ppermute(live['b'], 'dp', MIDDLE)  9.55 us
  transfers between devices with their start and end apart: 56, of which 15 were waited for; matrix products, arithmetic and copies ran while one was open for 33% of the time, Pallas kernels for 6%

profile of v1, /device:TPU:0, one launch (start us, length us, event | category | flops | bytes accessed | tf_op | source)
XLA Modules:
  0.0 247.1 jit_solution(14085737432939420150)
XLA Ops:
  1.4 2.9 %collective-permute-start.2 = (f32[2,128]{1,0:T(2,128)S(1)}, f32[2,128]{1,0:T(2,128)S(1)}, u32[]{:S(2)}, u32[]{:S(2)}) collective-permute-start(f32[2,128]{1,0:T(2,128)S(1)} %convert_bitcast_fusion), channel_id=1, source_target_pairs={{0,8},{4,12},{8,0},{12,4},{1,9},{5,13},{9,1},{13,5},{2,10},{6,14},... | collective-permute-start | bytes 3080 | tf_op jit(solution)/shard_map/ppermute | solution.py:92
  14.5 2.8 %copy-done.8 = s32[1,1024,1536]{2,1,0:T(8,128)S(1)} copy-done((s32[1,1024,1536]{2,1,0:T(8,128)S(1)}, s32[1,1024,1536]{2,1,0:T(8,128)}, u32[]{:S(2)}) %copy-start.8) | copy-done | bytes 6291480
  17.3 4.8 %shard_map.164 = bf16[1024,1536]{1,0:T(8,128)(2,1)S(1)} custom-call(s32[1024,1536]{1,0:T(8,128)S(1)} %bitcast.283, f32[3,1024,24]{2,1,0:T(8,128)S(1)} %bitcast.286, f32[8,128]{1,0:T(8,128)S(1)} %scatter.8.level_ref, bf16[24,1536]{1,0:T(8,128)(2,1)S(1)} %fusion.103.spread_ref), custom_call_target="tpu_custom_call" | custom-call | flops 226492416 | bytes 9437184 | tf_op jit(solution)/shard_map/pallas_call | solution.py:73
  26.4 4.8 %shard_map.163 = bf16[1024,1536]{1,0:T(8,128)(2,1)S(1)} custom-call(s32[1024,1536]{1,0:T(8,128)S(1)} %bitcast.284, f32[3,1024,24]{2,1,0:T(8,128)S(1)} %bitcast.287, f32[8,128]{1,0:T(8,128)S(1)} %scatter.8.level_ref, bf16[24,1536]{1,0:T(8,128)(2,1)S(1)} %fusion.103.spread_ref), custom_call_target="tpu_custom_call" | custom-call | flops 226492416 | bytes 9437184 | tf_op jit(solution)/shard_map/pallas_call | solution.py:73
  31.3 4.8 %shard_map.162 = bf16[1024,1536]{1,0:T(8,128)(2,1)S(1)} custom-call(s32[1024,1536]{1,0:T(8,128)S(1)} %bitcast.285, f32[3,1024,24]{2,1,0:T(8,128)S(1)} %bitcast.288, f32[8,128]{1,0:T(8,128)S(1)} %scatter.8.level_ref, bf16[24,1536]{1,0:T(8,128)(2,1)S(1)} %fusion.103.spread_ref), custom_call_target="tpu_custom_call" | custom-call | flops 226492416 | bytes 9437184 | tf_op jit(solution)/shard_map/pallas_call | solution.py:73
  39.3 2.8 %convolution_convert_fusion.8 = bf16[96,1536]{1,0:T(8,128)(2,1)S(1)} fusion(bf16[96,1024]{1,0:T(8,128)(2,1)} %convolution_convert_fusion.18, bf16[1024,1536]{1,0:T(8,128)(2,1)} %copy-done.5), kind=kOutput, calls=%fused_computation.27 | convolution fusion | flops 302137344 | bytes 3637248 | tf_op jit(solution)/shard_map/dot_general | solution.py:38
  49.6 2.7 %collective-permute-start.23 = (f32[4,128]{1,0:T(4,128)S(1)}, f32[4,128]{1,0:T(4,128)S(1)}, u32[]{:S(2)}, u32[]{:S(2)}) collective-permute-start(f32[4,128]{1,0:T(4,128)S(1)} %add.327), channel_id=1, source_target_pairs={{0,2},{1,3},{2,0},{3,1},{4,6},{5,7},{6,4},{7,5},{8,10},{9,11},{10,... | collective-permute-start | bytes 6152 | tf_op jit(solution)/shard_map/ppermute | solution.py:115
  55.8 2.6 %collective-permute-done.43 = f32[2,128]{1,0:T(2,128)S(1)} collective-permute-done((f32[2,128]{1,0:T(2,128)S(1)}, f32[2,128]{1,0:T(2,128)S(1)}, u32[]{:S(2)}, u32[]{:S(2)}) %collective-permute-start.43) | collective-permute-done | bytes 1056 | tf_op jit(solution)/shard_map/ppermute | solution.py:92
  60.7 4.2 %collective-permute-start.7 = (bf16[96,1536]{1,0:T(8,128)(2,1)}, bf16[96,1536]{1,0:T(8,128)(2,1)}, u32[]{:S(2)}, u32[]{:S(2)}) collective-permute-start(bf16[96,1536]{1,0:T(8,128)(2,1)} %convolution_convert_fusion.11), channel_id=1, source_target_pairs={{0,1},{3,2},{4,5},{7,6},{8,9},{11,10},{12,13},{15,14},{16,17},{19,... | collective-permute-start | bytes 884744 | tf_op jit(solution)/shard_map/ppermute | solution.py:292
  93.9 2.7 %collective-permute-start.8 = (bf16[96,1664]{1,0:T(8,128)(2,1)}, bf16[96,1664]{1,0:T(8,128)(2,1)}, u32[]{:S(2)}, u32[]{:S(2)}) collective-permute-start(bf16[96,1664]{1,0:T(8,128)(2,1)} %pad_maximum_fusion.3), channel_id=1, source_target_pairs={{0,1},{3,2},{4,5},{7,6},{8,9},{11,10},{12,13},{15,14},{16,17},{19,... | collective-permute-start | bytes 958472 | tf_op jit(solution)/shard_map/ppermute | solution.py:292
  103.7 2.8 %convolution_convert_fusion.6 = bf16[96,1536]{1,0:T(8,128)(2,1)S(1)} fusion(bf16[96,1024]{1,0:T(8,128)(2,1)} %copy-done.26, bf16[1024,1536]{1,0:T(8,128)(2,1)} %copy-done.5), kind=kOutput, calls=%fused_computation.25 | convolution fusion | flops 302137344 | bytes 3637248 | tf_op jit(solution)/shard_map/dot_general | solution.py:38
  113.0 4.6 %collective-permute-start.10 = (bf16[96,1600]{1,0:T(8,128)(2,1)S(1)}, bf16[96,1600]{1,0:T(8,128)(2,1)S(1)}, u32[]{:S(2)}, u32[]{:S(2)}) collective-permute-start(bf16[96,1600]{1,0:T(8,128)(2,1)S(1)} %copy-done.31), channel_id=1, source_target_pairs={{0,1},{3,2},{4,5},{7,6},{8,9},{11,10},{12,13},{15,14},{16,17},{19,... | collective-permute-start | bytes 921608 | tf_op jit(solution)/shard_map/ppermute | solution.py:292
  120.7 3.4 %collective-permute-start.19 = (bf16[96,1536]{1,0:T(8,128)(2,1)S(1)}, bf16[96,1536]{1,0:T(8,128)(2,1)S(1)}, u32[]{:S(2)}, u32[]{:S(2)}) collective-permute-start(bf16[96,1536]{1,0:T(8,128)(2,1)S(1)} %copy-done.33), channel_id=1, source_target_pairs={{0,1},{3,2},{4,5},{7,6},{8,9},{11,10},{12,13},{15,14},{16,17},{19,... | collective-permute-start | bytes 884744 | tf_op jit(solution)/shard_map/ppermute | solution.py:292
  126.4 4.6 %collective-permute-start.13 = (bf16[96,1536]{1,0:T(8,128)(2,1)S(1)}, bf16[96,1536]{1,0:T(8,128)(2,1)S(1)}, u32[]{:S(2)}, u32[]{:S(2)}) collective-permute-start(bf16[96,1536]{1,0:T(8,128)(2,1)S(1)} %convolution_convert_fusion.14), channel_id=1, source_target_pairs={{0,1},{3,2},{4,5},{7,6},{8,9},{11,10},{12,13},{15,14},{16,17},{19,... | collective-permute-start | bytes 884744 | tf_op jit(solution)/shard_map/ppermute | solution.py:292
  133.1 2.7 %collective-permute-done.21 = bf16[96,1664]{1,0:T(8,128)(2,1)S(1)} collective-permute-done((bf16[96,1664]{1,0:T(8,128)(2,1)S(1)}, bf16[96,1664]{1,0:T(8,128)(2,1)S(1)}, u32[]{:S(2)}, u32[]{:S(2)}) %collective-permute-start.21) | collective-permute-done | bytes 319520 | tf_op jit(solution)/shard_map/ppermute | solution.py:298
  136.7 4.4 %collective-permute-start.25 = (bf16[96,1664]{1,0:T(8,128)(2,1)S(1)}, bf16[96,1664]{1,0:T(8,128)(2,1)S(1)}, u32[]{:S(2)}, u32[]{:S(2)}) collective-permute-start(bf16[96,1664]{1,0:T(8,128)(2,1)S(1)} %pad_maximum_fusion.4), channel_id=1, source_target_pairs={{0,1},{3,2},{4,5},{7,6},{8,9},{11,10},{12,13},{15,14},{16,17},{19,... | collective-permute-start | bytes 958472 | tf_op jit(solution)/shard_map/ppermute | solution.py:292
  143.2 7.2 %collective-permute-done.27 = bf16[96,1600]{1,0:T(8,128)(2,1)S(1)} collective-permute-done((bf16[96,1600]{1,0:T(8,128)(2,1)S(1)}, bf16[96,1600]{1,0:T(8,128)(2,1)S(1)}, u32[]{:S(2)}, u32[]{:S(2)}) %collective-permute-start.27) | collective-permute-done | bytes 307232 | tf_op jit(solution)/shard_map/ppermute | solution.py:298
  159.7 6.8 %collective-permute-start.37 = (bf16[96,1600]{1,0:T(8,128)(2,1)S(1)}, bf16[96,1600]{1,0:T(8,128)(2,1)S(1)}, u32[]{:S(2)}, u32[]{:S(2)}) collective-permute-start(bf16[96,1600]{1,0:T(8,128)(2,1)S(1)} %pad_maximum_fusion.7), channel_id=1, source_target_pairs={{0,1},{3,2},{4,5},{7,6},{8,9},{11,10},{12,13},{15,14},{16,17},{19,... | collective-permute-start | bytes 921608 | tf_op jit(solution)/shard_map/ppermute | solution.py:292
  167.1 3.6 %collective-permute-start.29 = (bf16[96,1664]{1,0:T(8,128)(2,1)S(1)}, bf16[96,1664]{1,0:T(8,128)(2,1)S(1)}, u32[]{:S(2)}, u32[]{:S(2)}) collective-permute-start(bf16[96,1664]{1,0:T(8,128)(2,1)S(1)} %copy-done.29), channel_id=1, source_target_pairs={{0,1},{3,2},{4,5},{7,6},{8,9},{11,10},{12,13},{15,14},{16,17},{19,... | collective-permute-start | bytes 958472 | tf_op jit(solution)/shard_map/ppermute | solution.py:292
  173.2 6.7 %collective-permute-done.31 = bf16[96,1600]{1,0:T(8,128)(2,1)S(1)} collective-permute-done((bf16[96,1600]{1,0:T(8,128)(2,1)S(1)}, bf16[96,1600]{1,0:T(8,128)(2,1)S(1)}, u32[]{:S(2)}, u32[]{:S(2)}) %collective-permute-start.31) | collective-permute-done | bytes 307232 | tf_op jit(solution)/shard_map/ppermute | solution.py:298
  188.8 4.8 %collective-permute-start.32 = (bf16[96,1600]{1,0:T(8,128)(2,1)S(1)}, bf16[96,1600]{1,0:T(8,128)(2,1)S(1)}, u32[]{:S(2)}, u32[]{:S(2)}) collective-permute-start(bf16[96,1600]{1,0:T(8,128)(2,1)S(1)} %copy-done.28), channel_id=1, source_target_pairs={{0,1},{3,2},{4,5},{7,6},{8,9},{11,10},{12,13},{15,14},{16,17},{19,... | collective-permute-start | bytes 921608 | tf_op jit(solution)/shard_map/ppermute | solution.py:292
  204.3 7.3 %collective-permute-done.46 = bf16[96,1600]{1,0:T(8,128)(2,1)S(1)} collective-permute-done((bf16[96,1600]{1,0:T(8,128)(2,1)S(1)}, bf16[96,1600]{1,0:T(8,128)(2,1)S(1)}, u32[]{:S(2)}, u32[]{:S(2)}) %collective-permute-start.46) | collective-permute-done | bytes 307232 | tf_op jit(solution)/shard_map/ppermute | solution.py:298
  222.1 3.1 %collective-permute-done.47 = bf16[96,1536]{1,0:T(8,128)(2,1)S(1)} collective-permute-done((bf16[96,1536]{1,0:T(8,128)(2,1)S(1)}, bf16[96,1536]{1,0:T(8,128)(2,1)S(1)}, u32[]{:S(2)}, u32[]{:S(2)}) %collective-permute-start.47) | collective-permute-done | bytes 294944 | tf_op jit(solution)/shard_map/ppermute | solution.py:298
  225.3 4.1 %collective-permute-done.49 = bf16[96,1600]{1,0:T(8,128)(2,1)S(1)} collective-permute-done((bf16[96,1600]{1,0:T(8,128)(2,1)S(1)}, bf16[96,1600]{1,0:T(8,128)(2,1)S(1)}, u32[]{:S(2)}, u32[]{:S(2)}) %collective-permute-start.49) | collective-permute-done | bytes 307232 | tf_op jit(solution)/shard_map/ppermute | solution.py:298
  (461 shorter events, 143.1 us)
Async XLA Ops:
  1.4 44.5 %collective-permute-start.2 = (f32[2,128]{1,0:T(2,128)S(1)}, f32[2,128]{1,0:T(2,128)S(1)}, u32[]{:S(2)}, u32[]{:S(2)}) collective-permute-start(f32[2,128]{1,0:T(2,128)S(1)} %convert_bitcast_fusion), channel_id=1, source_target_pairs={{0,8},{4,12},{8,0},{12,4},{1,9},{5,13},{9,1},{13,5},{2,10},{6,14},... | collective-permute-start | bytes 3080 | tf_op jit(solution)/shard_map/ppermute | solution.py:92
  4.3 43.4 %collective-permute-start = (f32[2,128]{1,0:T(2,128)S(1)}, f32[2,128]{1,0:T(2,128)S(1)}, u32[]{:S(2)}, u32[]{:S(2)}) collective-permute-start(f32[2,128]{1,0:T(2,128)S(1)} %convert_bitcast_fusion), channel_id=1, source_target_pairs={{0,4},{4,0},{8,12},{12,8},{1,5},{5,1},{9,13},{13,9},{2,6},{6,2},{1... | collective-permute-start | bytes 3080 | tf_op jit(solution)/shard_map/ppermute | solution.py:92
  4.3 67.2 %collective-permute-start.6 = (bf16[128,1024]{1,0:T(8,128)(2,1)}, bf16[128,1024]{1,0:T(8,128)(2,1)}, u32[]{:S(2)}, u32[]{:S(2)}) collective-permute-start(bf16[128,1024]{1,0:T(8,128)(2,1)} %param.22), channel_id=1, source_target_pairs={{0,8},{4,12},{8,0},{12,4},{1,9},{5,13},{9,1},{13,5},{2,10},{6,14},... | collective-permute-start | bytes 786440 | tf_op jit(solution)/shard_map/ppermute | solution.py:92
  4.3 70.0 %collective-permute-start.28 = (bf16[128,1024]{1,0:T(8,128)(2,1)}, bf16[128,1024]{1,0:T(8,128)(2,1)}, u32[]{:S(2)}, u32[]{:S(2)}) collective-permute-start(bf16[128,1024]{1,0:T(8,128)(2,1)} %param.22), channel_id=1, source_target_pairs={{0,4},{4,0},{8,12},{12,8},{1,5},{5,1},{9,13},{13,9},{2,6},{6,2},{1... | collective-permute-start | bytes 786440 | tf_op jit(solution)/shard_map/ppermute | solution.py:92
  4.8 60.7 %collective-permute-start.4 = (bf16[128,1024]{1,0:T(8,128)(2,1)}, bf16[128,1024]{1,0:T(8,128)(2,1)}, u32[]{:S(2)}, u32[]{:S(2)}) collective-permute-start(bf16[128,1024]{1,0:T(8,128)(2,1)} %param.13), channel_id=1, source_target_pairs={{0,8},{4,12},{8,0},{12,4},{1,9},{5,13},{9,1},{13,5},{2,10},{6,14},... | collective-permute-start | bytes 786440 | tf_op jit(solution)/shard_map/ppermute | solution.py:92
  49.6 28.4 %collective-permute-start.1 = (bf16[128,1024]{1,0:T(8,128)(2,1)}, bf16[128,1024]{1,0:T(8,128)(2,1)S(1)}, u32[]{:S(2)}, u32[]{:S(2)}) collective-permute-start(bf16[128,1024]{1,0:T(8,128)(2,1)} %param.13), channel_id=1, source_target_pairs={{0,4},{4,0},{8,12},{12,8},{1,5},{5,1},{9,13},{13,9},{2,6},{6,2},{1... | collective-permute-start | bytes 786440 | tf_op jit(solution)/shard_map/ppermute | solution.py:92
  60.7 30.0 %collective-permute-start.7 = (bf16[96,1536]{1,0:T(8,128)(2,1)}, bf16[96,1536]{1,0:T(8,128)(2,1)}, u32[]{:S(2)}, u32[]{:S(2)}) collective-permute-start(bf16[96,1536]{1,0:T(8,128)(2,1)} %convolution_convert_fusion.11), channel_id=1, source_target_pairs={{0,1},{3,2},{4,5},{7,6},{8,9},{11,10},{12,13},{15,14},{16,17},{19,... | collective-permute-start | bytes 884744 | tf_op jit(solution)/shard_map/ppermute | solution.py:292
  65.5 31.1 %collective-permute-start.16 = (bf16[96,1664]{1,0:T(8,128)(2,1)}, bf16[96,1664]{1,0:T(8,128)(2,1)}, u32[]{:S(2)}, u32[]{:S(2)}) collective-permute-start(bf16[96,1664]{1,0:T(8,128)(2,1)} %pad_maximum_fusion.6), channel_id=1, source_target_pairs={{0,1},{3,2},{4,5},{7,6},{8,9},{11,10},{12,13},{15,14},{16,17},{19,... | collective-permute-start | bytes 958472 | tf_op jit(solution)/shard_map/ppermute | solution.py:292
  87.1 13.3 %collective-permute-start.24 = (bf16[128,1024]{1,0:T(8,128)(2,1)}, bf16[128,1024]{1,0:T(8,128)(2,1)S(1)}, u32[]{:S(2)}, u32[]{:S(2)}) collective-permute-start(bf16[128,1024]{1,0:T(8,128)(2,1)} %collective-permute-done.6), channel_id=1, source_target_pairs={{0,4},{4,0},{8,12},{12,8},{1,5},{5,1},{9,13},{13,9},{2,6},{6,2},{1... | collective-permute-start | bytes 786440 | tf_op jit(solution)/shard_map/ppermute | solution.py:92
  88.4 18.0 %collective-permute-start.5 = (bf16[128,1024]{1,0:T(8,128)(2,1)}, bf16[128,1024]{1,0:T(8,128)(2,1)}, u32[]{:S(2)}, u32[]{:S(2)}) collective-permute-start(bf16[128,1024]{1,0:T(8,128)(2,1)} %collective-permute-done.4), channel_id=1, source_target_pairs={{0,4},{4,0},{8,12},{12,8},{1,5},{5,1},{9,13},{13,9},{2,6},{6,2},{1... | collective-permute-start | bytes 786440 | tf_op jit(solution)/shard_map/ppermute | solution.py:92
  92.5 16.2 %collective-permute-start.9 = (bf16[96,1536]{1,0:T(8,128)(2,1)}, bf16[96,1536]{1,0:T(8,128)(2,1)}, u32[]{:S(2)}, u32[]{:S(2)}) collective-permute-start(bf16[96,1536]{1,0:T(8,128)(2,1)} %add.311), channel_id=1, source_target_pairs={{1,2},{2,1},{5,6},{6,5},{9,10},{10,9},{13,14},{14,13},{17,18},{18,... | collective-permute-start | bytes 884744 | tf_op jit(solution)/shard_map/ppermute | solution.py:295
  93.9 16.0 %collective-permute-start.8 = (bf16[96,1664]{1,0:T(8,128)(2,1)}, bf16[96,1664]{1,0:T(8,128)(2,1)}, u32[]{:S(2)}, u32[]{:S(2)}) collective-permute-start(bf16[96,1664]{1,0:T(8,128)(2,1)} %pad_maximum_fusion.3), channel_id=1, source_target_pairs={{0,1},{3,2},{4,5},{7,6},{8,9},{11,10},{12,13},{15,14},{16,17},{19,... | collective-permute-start | bytes 958472 | tf_op jit(solution)/shard_map/ppermute | solution.py:292
  98.4 19.9 %collective-permute-start.17 = (bf16[96,1600]{1,0:T(8,128)(2,1)}, bf16[96,1600]{1,0:T(8,128)(2,1)}, u32[]{:S(2)}, u32[]{:S(2)}) collective-permute-start(bf16[96,1600]{1,0:T(8,128)(2,1)} %pad_maximum_fusion.5), channel_id=1, source_target_pairs={{0,1},{3,2},{4,5},{7,6},{8,9},{11,10},{12,13},{15,14},{16,17},{19,... | collective-permute-start | bytes 921608 | tf_op jit(solution)/shard_map/ppermute | solution.py:292
  100.4 19.1 %collective-permute-start.18 = (bf16[96,1664]{1,0:T(8,128)(2,1)}, bf16[96,1664]{1,0:T(8,128)(2,1)}, u32[]{:S(2)}, u32[]{:S(2)}) collective-permute-start(bf16[96,1664]{1,0:T(8,128)(2,1)} %add.318), channel_id=1, source_target_pairs={{1,2},{2,1},{5,6},{6,5},{9,10},{10,9},{13,14},{14,13},{17,18},{18,... | collective-permute-start | bytes 958472 | tf_op jit(solution)/shard_map/ppermute | solution.py:295
  111.1 13.7 %collective-permute-start.12 = (bf16[96,1536]{1,0:T(8,128)(2,1)S(1)}, bf16[96,1536]{1,0:T(8,128)(2,1)S(1)}, u32[]{:S(2)}, u32[]{:S(2)}) collective-permute-start(bf16[96,1536]{1,0:T(8,128)(2,1)S(1)} %add.313), channel_id=1, source_target_pairs={{1,0},{2,3},{5,4},{6,7},{9,8},{10,11},{13,12},{14,15},{17,16},{18,... | collective-permute-start | bytes 884744 | tf_op jit(solution)/shard_map/ppermute | solution.py:298
  126.4 15.2 %collective-permute-start.13 = (bf16[96,1536]{1,0:T(8,128)(2,1)S(1)}, bf16[96,1536]{1,0:T(8,128)(2,1)S(1)}, u32[]{:S(2)}, u32[]{:S(2)}) collective-permute-start(bf16[96,1536]{1,0:T(8,128)(2,1)S(1)} %convolution_convert_fusion.14), channel_id=1, source_target_pairs={{0,1},{3,2},{4,5},{7,6},{8,9},{11,10},{12,13},{15,14},{16,17},{19,... | collective-permute-start | bytes 884744 | tf_op jit(solution)/shard_map/ppermute | solution.py:292
  136.7 13.8 %collective-permute-start.25 = (bf16[96,1664]{1,0:T(8,128)(2,1)S(1)}, bf16[96,1664]{1,0:T(8,128)(2,1)S(1)}, u32[]{:S(2)}, u32[]{:S(2)}) collective-permute-start(bf16[96,1664]{1,0:T(8,128)(2,1)S(1)} %pad_maximum_fusion.4), channel_id=1, source_target_pairs={{0,1},{3,2},{4,5},{7,6},{8,9},{11,10},{12,13},{15,14},{16,17},{19,... | collective-permute-start | bytes 958472 | tf_op jit(solution)/shard_map/ppermute | solution.py:292
  157.6 14.7 %collective-permute-start.39 = (bf16[96,1536]{1,0:T(8,128)(2,1)S(1)}, bf16[96,1536]{1,0:T(8,128)(2,1)S(1)}, u32[]{:S(2)}, u32[]{:S(2)}) collective-permute-start(bf16[96,1536]{1,0:T(8,128)(2,1)S(1)} %add.333), channel_id=1, source_target_pairs={{1,0},{2,3},{5,4},{6,7},{9,8},{10,11},{13,12},{14,15},{17,16},{18,... | collective-permute-start | bytes 884744 | tf_op jit(solution)/shard_map/ppermute | solution.py:298
  159.7 13.4 %collective-permute-start.37 = (bf16[96,1600]{1,0:T(8,128)(2,1)S(1)}, bf16[96,1600]{1,0:T(8,128)(2,1)S(1)}, u32[]{:S(2)}, u32[]{:S(2)}) collective-permute-start(bf16[96,1600]{1,0:T(8,128)(2,1)S(1)} %pad_maximum_fusion.7), channel_id=1, source_target_pairs={{0,1},{3,2},{4,5},{7,6},{8,9},{11,10},{12,13},{15,14},{16,17},{19,... | collective-permute-start | bytes 921608 | tf_op jit(solution)/shard_map/ppermute | solution.py:292
  166.4 13.4 %collective-permute-start.38 = (bf16[96,1664]{1,0:T(8,128)(2,1)S(1)}, bf16[96,1664]{1,0:T(8,128)(2,1)S(1)}, u32[]{:S(2)}, u32[]{:S(2)}) collective-permute-start(bf16[96,1664]{1,0:T(8,128)(2,1)S(1)} %add.332), channel_id=1, source_target_pairs={{1,2},{2,1},{5,6},{6,5},{9,10},{10,9},{13,14},{14,13},{17,18},{18,... | collective-permute-start | bytes 958472 | tf_op jit(solution)/shard_map/ppermute | solution.py:295
  201.4 17.2 %collective-permute-start.35 = (bf16[96,1600]{1,0:T(8,128)(2,1)S(1)}, bf16[96,1600]{1,0:T(8,128)(2,1)S(1)}, u32[]{:S(2)}, u32[]{:S(2)}) collective-permute-start(bf16[96,1600]{1,0:T(8,128)(2,1)S(1)} %add.341), channel_id=1, source_target_pairs={{1,2},{2,1},{5,6},{6,5},{9,10},{10,9},{13,14},{14,13},{17,18},{18,... | collective-permute-start | bytes 921608 | tf_op jit(solution)/shard_map/ppermute | solution.py:295
  202.1 18.0 %collective-permute-start.36 = (bf16[96,1664]{1,0:T(8,128)(2,1)S(1)}, bf16[96,1664]{1,0:T(8,128)(2,1)S(1)}, u32[]{:S(2)}, u32[]{:S(2)}) collective-permute-start(bf16[96,1664]{1,0:T(8,128)(2,1)S(1)} %add.342), channel_id=1, source_target_pairs={{1,0},{2,3},{5,4},{6,7},{9,8},{10,11},{13,12},{14,15},{17,16},{18,... | collective-permute-start | bytes 958472 | tf_op jit(solution)/shard_map/ppermute | solution.py:298
  203.4 41.7 %collective-permute-start.51 = (bf16[128,2048]{1,0:T(8,128)(2,1)S(1)}, bf16[128,2048]{1,0:T(8,128)(2,1)S(1)}, u32[]{:S(2)}, u32[]{:S(2)}) collective-permute-start(bf16[128,2048]{1,0:T(8,128)(2,1)S(1)} %convolution_convert_fusion.2), channel_id=1, source_target_pairs={{0,8},{4,12},{8,0},{12,4},{1,9},{5,13},{9,1},{13,5},{2,10},{6,14},... | collective-permute-start | bytes 1572872 | tf_op jit(solution)/shard_map/ppermute | solution.py:92
  221.8 23.3 %collective-permute-start.52 = (bf16[128,2048]{1,0:T(8,128)(2,1)S(1)}, bf16[128,2048]{1,0:T(8,128)(2,1)S(1)}, u32[]{:S(2)}, u32[]{:S(2)}) collective-permute-start(bf16[128,2048]{1,0:T(8,128)(2,1)S(1)} %convolution_convert_fusion.1), channel_id=1, source_target_pairs={{0,12},{4,8},{8,4},{12,0},{1,13},{5,9},{9,5},{13,1},{2,14},{6,10},... | collective-permute-start | bytes 1572872 | tf_op jit(solution)/shard_map/ppermute | solution.py:92
  (116 other events, 1042.5 us)

commit v2 on v1

v2 whole, which is shorter than its diff:
```python
import functools

import jax
import jax.numpy as jnp
import numpy as np
from jax import lax
from jax.experimental import pallas as pl
from jax.experimental.pallas import tpu as pltpu
from jax.sharding import PartitionSpec as P

NF4_LEVELS = (
    -1.0,
    -0.6961928009986877,
    -0.5250730514526367,
    -0.39491748809814453,
    -0.28444138169288635,
    -0.18477343022823334,
    -0.09105003625154495,
    0.0,
    0.07958029955625534,
    0.16093020141124725,
    0.24611230194568634,
    0.3379152424240112,
    0.44070982933044434,
    0.5626170039176941,
    0.7229568362236023,
    1.0,
)
SCALE = 0.5
BF16 = jnp.bfloat16
F32 = jnp.float32
LAG = 2
LAST_COST = pl.CostEstimate(flops=6 * 10**9, bytes_accessed=16 * 10**6, transcendentals=0)
NO_COST = pl.CostEstimate(flops=0, bytes_accessed=0, transcendentals=0)
INWARD = [(0, 1), (3, 2)]
MIDDLE = [(1, 2), (2, 1)]
OUTWARD = [(1, 0), (2, 3)]


def dot(left, right):
    return jnp.dot(left, right, preferred_element_type=F32)


def dot_tn(left, right):
    return lax.dot_general(left, right, (((0,), (0,)), ((), ())), preferred_element_type=F32)


def dot_nt(left, right):
    return lax.dot_general(left, right, (((1,), (1,)), ((), ())), preferred_element_type=F32)


def dequantize_kernel(code_ref, scale_ref, level_ref, spread_ref, *refs, field):
    out_ref = refs[-1]
    rows, width = code_ref.shape
    step = 64
    table = jnp.broadcast_to(level_ref[0:1, :], (step, 128))
    scales = scale_ref[0]
    high = scales.astype(BF16)
    rest = scales - high.astype(F32)
    middle = rest.astype(BF16)
    low = (rest - middle.astype(F32)).astype(BF16)
    for column in range(0, width, 128):
        spread = spread_ref[:, column : column + 128]
        wide = (dot_tn(high, spread) + dot_tn(middle, spread)) + dot_tn(low, spread)
        for row in range(0, rows, step):
            code = (code_ref[row : row + step, column : column + 128] >> (4 * field)) & 15
            level = jnp.take_along_axis(table, code, axis=1)
            out_ref[row : row + step, column : column + 128] = (
                level * wide[row : row + step]
            ).astype(BF16)


def dequantize(codes, scales, levels, spread, field, *after):
    features, width = codes.shape
    blocks = scales.shape[1]
    rows = min(256, features)
    return pl.pallas_call(
        functools.partial(dequantize_kernel, field=field),
        grid=(features // rows,),
        in_specs=[
            pl.BlockSpec((rows, width), lambda i: (i, 0)),
            pl.BlockSpec((1, blocks, rows), lambda i: (field, 0, i)),
            pl.BlockSpec((8, 128), lambda i: (0, 0)),
            pl.BlockSpec((blocks, width), lambda i: (0, 0)),
        ]
        + [pl.BlockSpec(memory_space=pl.ANY)] * len(after),
        out_specs=pl.BlockSpec((rows, width), lambda i: (i, 0)),
        out_shape=jax.ShapeDtypeStruct((features, width), BF16),
        compiler_params=pltpu.CompilerParams(vmem_limit_bytes=(12 if after else 56) * 2**20),
        cost_estimate=NO_COST,
    )(codes, scales, levels, spread, *after)


def call(body, args, after, shapes, piped=False):
    smem = pl.BlockSpec(memory_space=pltpu.SMEM)
    count = len(args)
    extra = len(after)

    def whole(shape):
        if piped:
            return pl.BlockSpec(shape, lambda i: (0,) * len(shape))
        return pl.BlockSpec(memory_space=pltpu.VMEM)

    def kernel(*refs):
        body(list(refs[:count]), list(refs[count + extra :]))

    out = pl.pallas_call(
        kernel,
        grid=(1,) if piped else (),
        in_specs=[smem if a.dtype == jnp.int32 else whole(a.shape) for a in args]
        + [pl.BlockSpec(memory_space=pl.ANY)] * extra,
        out_specs=[whole(shape) for shape, _ in shapes],
        out_shape=[jax.ShapeDtypeStruct(shape, dtype) for shape, dtype in shapes],
        compiler_params=pltpu.CompilerParams(vmem_limit_bytes=(24 if piped else 10) * 2**20),
        cost_estimate=NO_COST,
    )(*args, *after)
    return list(out)


def run_step(end, kind, unit, pairs, pack, logits_of, after):
    args, shapes, count = [end], [], 0
    if kind is not None:
        rows, blocks, weight, low = unit
        if kind == 1:
            args.append(rows)
            count = rows.shape[0]
        else:
            features = weight.shape[0]
            count = sum(pick.shape[0] for pick, _, _ in blocks)
            for pick, block, _ in blocks:
                args += [pick, block]
            shapes.append(((count, features), BF16))
        args += [weight, low]
        shapes.append(((count, weight.shape[1] + low.shape[-2]), BF16))
    for name in pairs:
        args += list(pairs[name])
        shapes.append((pairs[name][0].shape, BF16))
    if pack is not None:
        args += list(pack)
        tokens, _, routes = pack
        shapes.append(((tokens.shape[0] + routes.shape[0], 2 * tokens.shape[1]), BF16))
    if logits_of is not None:
        router, packs = logits_of
        token_count = packs[0].shape[0] - 16
        args += [router] + packs
        shapes.append(((router.shape[0], token_count * len(packs)), F32))

    def body(ins, outs):
        is_end = ins.pop(0)[0]
        term = None
        if kind is not None:
            if kind == 1:
                rows_ref = ins.pop(0)
            else:
                rows_ref = outs.pop(0)
                found = []
                for pick, block, at in blocks:
                    pick_ref, block_ref = ins.pop(0), ins.pop(0)
                    found.append(
                        dot(pick_ref[...], block_ref[: pick.shape[1], at : at + rows_ref.shape[1]])
                    )
                rows_ref[...] = (jnp.concatenate(found, axis=0) if len(found) > 1 else found[0]).astype(
                    BF16
                )
            weight_ref, low_ref = ins.pop(0), ins.pop(0)
            term = outs.pop(0)
            width = weight_ref.shape[1]
            for column in range(0, width, 512):
                tile = slice(column, column + 512)
                term[:, tile] = dot(rows_ref[...], weight_ref[:, tile]).astype(BF16)
            low_map = low_ref[...] if kind == 2 else low_ref[kind]
            term[:, width:] = dot_nt(rows_ref[...], low_map).astype(BF16)
        for name in pairs:
            left, right, out = ins.pop(0), ins.pop(0), outs.pop(0)
            if name == "b" or (name == "c" and term is None):
                out[...] = (left[...].astype(F32) + right[...].astype(F32)).astype(BF16)
            elif name == "c":

                @pl.when(is_end == 1)
                def _(out=out):
                    out[...] = term[...]

                @pl.when(is_end == 0)
                def _(out=out, left=left, right=right):
                    out[...] = (left[...].astype(F32) + right[...].astype(F32)).astype(BF16)

            else:

                @pl.when(is_end == 1)
                def _(out=out, right=right):
                    out[...] = right[...]

                @pl.when(is_end == 0)
                def _(out=out, left=left):
                    out[...] = left[...]

        if pack is not None:
            tokens_ref, cots_ref, routes_ref, out = ins.pop(0), ins.pop(0), ins.pop(0), outs.pop(0)
            top, left = tokens_ref.shape
            out[:top, :left] = tokens_ref[...]
            out[:top, left:] = cots_ref[...]
            out[top:, : routes_ref.shape[1]] = routes_ref[...]
        if logits_of is not None:
            router_ref, out = ins.pop(0), outs.pop(0)
            features = router_ref.shape[1]
            for number in range(len(packs)):
                block = ins.pop(0)
                out[:, number * token_count : (number + 1) * token_count] = dot_nt(
                    router_ref[...], block[:token_count, :features]
                )

    return call(body, args, after, shapes)


def middle_shapes(rows, hidden_width, rank, sources, tokens):
    wide, low = ((rows, hidden_width), BF16), ((rows, rank), BF16)
    return [wide, wide, wide] + [low] * 7 + [((rows, 1), F32), ((sources, tokens), F32)]


def middle_body(ins, outs):
    gate_ref, up_ref, cot_ref, gates_ref, signs_ref, maps, down_ref = ins[:7]
    picks_ref = ins[7:]
    sources = len(picks_ref)
    rows = gate_ref.shape[0]
    cap = rows // sources
    hidden_width = maps.shape[2]
    hidden_ref, grad_gate_ref, grad_up_ref, hl_ref, lg_ref, lu_ref, hlg_ref, clg_ref = outs[:8]
    ag_ref, au_ref, gate_out, signed_ref = outs[8:]
    ag_ref[...] = gate_ref[:, hidden_width:]
    au_ref[...] = up_ref[:, hidden_width:]
    chosen = [pick[...].astype(F32) for pick in picks_ref]
    gate = [jnp.sum(chosen[i] * gates_ref[i : i + 1, :], axis=1, keepdims=True) for i in range(sources)]
    gate = jnp.concatenate(gate, axis=0) if sources > 1 else gate[0]
    gate_out[...] = gate
    cot_low = cot_ref[:, hidden_width:]
    total = jnp.zeros((rows, 1), F32)
    step = 512
    for column in range(0, hidden_width, step):
        tile = slice(column, column + step)
        g = gate_ref[:, tile].astype(F32) + SCALE * dot(gate_ref[:, hidden_width:], maps[0, :, tile])
        u = up_ref[:, tile].astype(F32) + SCALE * dot(up_ref[:, hidden_width:], maps[1, :, tile])
        h = cot_ref[:, tile].astype(F32) + SCALE * dot(cot_low, down_ref[:, tile])
        sigma = jax.nn.sigmoid(g)
        silu = g * sigma
        hidden = (silu * u).astype(BF16)
        total = total + jnp.sum(hidden.astype(F32) * h, axis=1, keepdims=True)
        h = h * gate
        hidden_ref[:, tile] = hidden
        grad_gate_ref[:, tile] = (h * u * sigma * (1.0 + g * (1.0 - sigma))).astype(BF16)
        grad_up_ref[:, tile] = (h * silu).astype(BF16)
    hidden_low = dot_nt(hidden_ref[...], down_ref[...]).astype(BF16)
    hl_ref[...] = hidden_low
    hlg_ref[...] = (hidden_low.astype(F32) * gate).astype(BF16)
    clg_ref[...] = (cot_low.astype(F32) * gate).astype(BF16)
    lg_ref[...] = dot_nt(grad_gate_ref[...], maps[0]).astype(BF16)
    lu_ref[...] = dot_nt(grad_up_ref[...], maps[1]).astype(BF16)
    for i in range(sources):
        line = jnp.sum(chosen[i] * total[i * cap : (i + 1) * cap], axis=0, keepdims=True)
        signed_ref[i : i + 1, :] = line * signs_ref[i : i + 1, :]


def run_middle(head, picks, after):
    rows, maps = head[0].shape[0], head[5]
    shapes = middle_shapes(rows, maps.shape[2], maps.shape[1], len(picks), picks[0].shape[1])
    return call(middle_body, head + picks, after, shapes)


def run_back(share_start, share, head, mid, rows_x, rows_c, weights, adapter_in_t, down_out, picks, totals, after, cost):
    rows, hidden_width = rows_x.shape[0], weights[0].shape[1]
    rank, features = down_out.shape
    sources = len(picks)
    cap = rows // sources
    width = hidden_width if share % 128 else share
    tile = min(256, features)
    tokens = picks[0].shape[1]

    def fixed(value):
        return pl.BlockSpec(value.shape, lambda i, n=value.ndim: (0,) * n)

    last = pl.BlockSpec((rows, tile), lambda i: (0, i))
    lines = pl.BlockSpec((tile, hidden_width), lambda i: (i, 0))
    low = pl.BlockSpec((rank, tile), lambda i: (0, i))
    pair = pl.BlockSpec((2, rank, tile), lambda i: (0, 0, i))
    total_specs = [
        pair,
        pl.BlockSpec((2, rank, width), lambda i: (0, 0, 0)),
        pl.BlockSpec((rank, width), lambda i: (0, 0)),
        low,
    ]
    fused = mid is None
    lead = head if fused else list(mid)
    inner = middle_shapes(rows, hidden_width, rank, sources, tokens)
    args = [share_start] + lead + [rows_x, rows_c] + list(weights) + [adapter_in_t, down_out]
    args += picks + totals + after
    specs = [pl.BlockSpec(memory_space=pltpu.SMEM)] + [fixed(value) for value in lead]
    specs += [last, last, lines, lines, lines, pair, low] + [fixed(pick) for pick in picks]
    specs += total_specs[: len(totals)] + [pl.BlockSpec(memory_space=pl.ANY)] * len(after)
    shapes = [((2, tokens, features), BF16)] * sources
    shapes += [((2, rank, features), F32), ((2, rank, width), F32), ((rank, width), F32), ((rank, features), F32)]
    out_specs = [pl.BlockSpec((2, tokens, tile), lambda i: (0, 0, i))] * sources + total_specs
    if fused:
        shapes.append(inner[-1])
        out_specs.append(pl.BlockSpec(inner[-1][0], lambda i: (0, 0)))
    given = len(totals)
    led = 1 + len(lead)

    def body(*refs):
        start = pl.multiple_of(refs[0][0], 128) if share % 128 == 0 else 0
        x_ref, c_ref, wg, wu, wd, maps, down_ref = refs[led : led + 7]
        picks_ref = refs[led + 7 : led + 7 + sources]
        old = refs[led + 7 + sources : led + 7 + sources + given]
        outs = refs[len(args) :]
        backs, new = outs[:sources], outs[sources : sources + 4]
        middle = refs[1:led]
        if fused:
            middle = outs[sources + 5 :]

            @pl.when(pl.program_id(0) == 0)
            def _():
                middle_body(list(refs[1:led]) + list(picks_ref), list(middle) + [outs[sources + 4]])

        h_ref, gg_ref, gu_ref, hl_ref, lg_ref, lu_ref, hlg_ref, clg_ref, ag_ref, au_ref, gate_ref = middle
        out = dot_nt(h_ref[...], wd[...]) + SCALE * dot(hl_ref[...], down_ref[...])
        slot = (dot_nt(gg_ref[...], wg[...]) + dot_nt(gu_ref[...], wu[...])) + SCALE * (
            dot(lg_ref[...], maps[0]) + dot(lu_ref[...], maps[1])
        )
        for which, value in enumerate((out * gate_ref[...], slot)):
            for i in range(sources):
                part = value[i * cap : (i + 1) * cap].astype(BF16)
                backs[i][which] = dot_tn(picks_ref[i][...], part).astype(BF16)

        def add(which, index, value):
            value = SCALE * value
            if given:
                value = value + old[which][index]
            new[which][index] = value

        add(0, 0, dot_tn(lg_ref[...], x_ref[...]))
        add(0, 1, dot_tn(lu_ref[...], x_ref[...]))
        add(3, ..., dot_tn(hlg_ref[...], c_ref[...]))

        @pl.when(pl.program_id(0) == 0)
        def _():
            columns = pl.ds(start, width)
            add(1, 0, dot_tn(ag_ref[...], gg_ref[:, columns]))
            add(1, 1, dot_tn(au_ref[...], gu_ref[:, columns]))
            add(2, ..., dot_tn(clg_ref[...], h_ref[:, columns]))

    out = pl.pallas_call(
        body,
        grid=(features // tile,),
        in_specs=specs,
        out_specs=out_specs,
        out_shape=[jax.ShapeDtypeStruct(shape, dtype) for shape, dtype in shapes],
        scratch_shapes=[pltpu.VMEM(shape, dtype) for shape, dtype in inner[:-1]] if fused else [],
        compiler_params=pltpu.CompilerParams(vmem_limit_bytes=20 * 2**20),
        cost_estimate=cost,
    )(*args)
    return list(out[:sources]), list(out[sources : sources + 4]), list(out[sources + 4 :])


def run_end(backs, packs, gathered, gates, routes, router_t, after):
    token_count = backs[0].shape[1]
    experts, features = router_t.shape
    args = backs + packs + gathered + [gates, routes, router_t]
    shapes = [((token_count, features), BF16), ((token_count, features), BF16), ((experts, features), F32)]

    def body(ins, outs):
        backs_ref, packs_ref, gathered_ref = ins[:experts], ins[experts : 2 * experts], ins[2 * experts : 3 * experts]
        gates_ref, routes_ref, router_ref = ins[3 * experts :]
        number = lax.broadcasted_iota(jnp.int32, (experts, 1), 0).astype(F32)
        terms, first_line = [], None
        for i in range(experts):
            at = slice(i * token_count, (i + 1) * token_count)
            margin = sum_tree([gathered_ref[j][i ^ j : (i ^ j) + 1, :] for j in range(experts)])
            step = gates_ref[0:1, at] * gates_ref[1:2, at] * margin
            line = step * (
                (routes_ref[0:1, at] == number).astype(F32) - (routes_ref[1:2, at] == number).astype(F32)
            )
            line = line.astype(BF16)
            first_line = line if i == 0 else first_line
            terms.append(dot(line, packs_ref[i][:token_count, :features]))
        outs[2][...] = sum_tree(terms)
        outs[0][...] = sum_tree([back[0].astype(F32) for back in backs_ref]).astype(BF16)
        outs[1][...] = (
            sum_tree([back[1].astype(F32) for back in backs_ref])
            + dot_tn(first_line, router_ref[...])
        ).astype(BF16)

    return call(body, args, after, shapes, True)


def hop(value, step, count):
    return lax.ppermute(value, "expert", [(e, e ^ step) for e in range(count)])


def gather_direct(value, count):
    return [value] + [hop(value, step, count) for step in range(1, count)]


def gather_sources(value, count):
    got = [value] + [None] * (count - 1)
    bits = [1 << b for b in range(count.bit_length() - 1)]
    for index in sorted(range(1, count), key=lambda i: bin(i).count("1")):
        low_bit = index & -index
        got[index] = hop(got[index ^ low_bit], low_bit, count)
    return got


def sum_tree(values):
    while len(values) > 1:
        values = [values[2 * i] + values[2 * i + 1] for i in range(len(values) // 2)]
    return values[0]


def sum_dp(value, parts):
    if parts & (parts - 1):
        return lax.psum(value, "dp")
    step = 1
    while step < parts:
        value = value + lax.ppermute(value, "dp", [(z, z ^ step) for z in range(parts)])
        step *= 2
    return value


def shards(
    tokens,
    routes,
    router_w,
    codes,
    scales,
    adapter_in,
    adapter_out,
    down_in,
    down_out,
    cotangent,
):
    token_count, features = tokens.shape
    slots = routes.shape[1]
    experts = router_w.shape[1]
    capacity = 3 * token_count * slots // (2 * experts)
    codes, scales_t = codes[0], jnp.swapaxes(scales[0], 1, 2)
    adapter_in_t = jnp.swapaxes(adapter_in[0], 1, 2)
    adapter_out, down_out = adapter_out[0], down_out[0]
    down_in_t = down_in[0].T
    router_t = router_w.T
    hidden_width = codes.shape[1]
    blocks = scales_t.shape[1]
    parts = lax.axis_size("dp")
    me = lax.axis_index("expert").astype(F32)
    z_index = lax.axis_index("dp")
    share = hidden_width // parts
    share_start = (z_index * share).astype(jnp.int32).reshape(1)
    end = ((z_index == 0) | (z_index == parts - 1)).astype(jnp.int32).reshape(1)
    number = lax.broadcasted_iota(jnp.int32, (experts, 1), 0).astype(F32)

    table = np.zeros((8, 128), np.float32)
    table[:, :16] = np.asarray(NF4_LEVELS, np.float32)
    levels = jnp.asarray(table)
    block_of = np.arange(hidden_width) // (hidden_width // blocks)
    spread = jnp.asarray(np.arange(blocks)[:, None] == block_of[None, :], BF16)
    before = jnp.asarray(np.arange(token_count)[:, None] < np.arange(token_count)[None, :], BF16)
    row_number = jnp.asarray(np.arange(capacity)[:, None], F32)
    weights = [dequantize(codes, scales_t, levels, spread, 0), None, None]

    per_chunk = max(1, experts // 4)
    order = [list(range(i, i + per_chunk)) for i in range(0, experts, per_chunk)]
    if len(order) == 4:
        order = [order[0], order[2], order[3], order[1]]

    def picks_of(first, second):
        mine = (first == me) | (second == me)
        pad = jnp.concatenate([mine, mine, mine, mine, mine, mine, mine, mine], axis=0)
        place = dot(pad[: max(8, mine.shape[0])].astype(BF16), before)
        return [
            (mine[i : i + 1] & (place[i : i + 1] == row_number)).astype(BF16) for i in range(mine.shape[0])
        ]

    routes_t = routes.T.astype(F32)
    picks = picks_of(routes_t[0:1], routes_t[1:2])
    routes_pad = jnp.pad(routes_t.astype(BF16), ((0, 14), (0, 0)))
    packs, chunk_x, chunk_c, shared = [], {}, {}, {}

    def spread_start(packed):
        packs[:] = gather_sources(packed, experts)
        rows = [pack[token_count : token_count + 2, :token_count].astype(F32) for pack in packs]
        shared["routes"] = jnp.concatenate(rows, axis=1)
        if experts > 1:
            first = jnp.concatenate([row[0:1] for row in rows[1:]], axis=0)
            second = jnp.concatenate([row[1:2] for row in rows[1:]], axis=0)
            picks[1:] = picks_of(first, second)

    def settle_gates(logits):
        logits = sum_dp(logits, parts)
        all_routes = shared["routes"]
        chosen = [
            jnp.sum(jnp.where(all_routes[k : k + 1] == number, logits, 0.0), axis=0, keepdims=True)
            for k in range(2)
        ]
        margin = chosen[0] - chosen[1]
        gates = jnp.concatenate([jax.nn.sigmoid(margin), jax.nn.sigmoid(-margin)], axis=0)
        shared["gates"] = gates
        first = all_routes[0:1] == me
        shared["mine"] = jnp.where(first, gates[0:1], gates[1:2]).reshape(experts, token_count)
        shared["signs"] = jnp.where(first, 1.0, -1.0).reshape(experts, token_count)

    def step(n, j, pairs, after, logits=False):
        kind, unit, pack = None, None, None
        if n is not None:
            kind = j
            if weights[j] is None:
                weights[j] = dequantize(codes, scales_t, levels, spread, j, *after)
            early = not packs
            if j == 0:
                taken = [(picks[i], tokens if early else packs[i], 0) for i in order[n]]
                unit = (None, taken, weights[0], adapter_in_t)
            elif j == 1:
                unit = (chunk_x[n], None, weights[1], adapter_in_t)
            else:
                unit = (None, [(picks[i], packs[i], features) for i in order[n]], weights[2], down_out)
            if early:
                pack = (tokens, cotangent, routes_pad)
        logits_of = (router_t, packs) if logits else None
        out = run_step(end, kind, unit, pairs, pack, logits_of, after)
        if logits:
            settle_gates(out.pop())
        if pack is not None:
            spread_start(out.pop())
        term = None
        if kind is not None:
            if kind == 0:
                chunk_x[n] = out.pop(0)
            elif kind == 2:
                chunk_c[n] = out.pop(0)
            term = out.pop(0)
        return term, dict(zip(pairs, out))

    back, totals, signed = {}, [], {}

    def finish(n, sums, after, split=False):
        chosen = [picks[i] for i in order[n]]
        gates = jnp.concatenate([shared["mine"][i : i + 1] for i in order[n]], axis=0)
        signs = jnp.concatenate([shared["signs"][i : i + 1] for i in order[n]], axis=0)
        head = list(sums) + [gates, signs, adapter_out, down_in_t]
        mid, cost = None, NO_COST
        if split:
            mid = run_middle(head, chosen, after)
            lines, after, cost = [mid.pop()], [mid[0]], LAST_COST
        dense, new, extra = run_back(
            share_start,
            share,
            head,
            mid,
            chunk_x[n],
            chunk_c[n],
            weights,
            adapter_in_t,
            down_out,
            chosen,
            totals,
            after,
            cost,
        )
        lines = lines if split else extra
        totals[:] = new
        for at, i in enumerate(order[n]):
            signed[i] = lines[0][at : at + 1]
            back[i] = dense[at] if i == 0 else hop(dense[at], i, experts)
        return [new[0]]

    chunks = len(order)
    units = [(n, j) for n in range(chunks) for j in range(3)]
    total = len(units)
    after = []
    if parts == 4 and per_chunk == 1:
        term, near, inner, far, carried, final = {}, {}, {}, {}, {}, {}
        for t in range(total + 3 * LAG):
            old = t - LAG
            pairs = {}
            if 0 <= t - LAG < total:
                pairs["b"] = (term[old], near[old])
            if 0 <= t - 2 * LAG < total:
                pairs["c"] = (inner[old], far[old])
            if 0 <= t - 3 * LAG < total:
                pairs["d"] = (carried[old], near[old])
            n, j = units[t] if t < total else (None, None)
            new, sums = step(n, j, pairs, after, logits=t == 4)
            if new is not None:
                term[t] = new
            if "c" in sums:
                carried[t] = sums["c"]
                way = (INWARD if new is not None else []) + OUTWARD
                near[t] = lax.ppermute(carried[t], "dp", way)
            elif new is not None:
                near[t] = lax.ppermute(new, "dp", INWARD)
            if "b" in sums:
                inner[t] = sums["b"]
                far[t] = lax.ppermute(inner[t], "dp", MIDDLE)
            after = [new if new is not None else list(sums.values())[0]]
            if "d" in sums:
                unit = t - 3 * LAG
                final[unit] = sums["d"]
                if unit % 3 == 2:
                    m = unit // 3
                    after = finish(m, [final[3 * m + f] for f in range(3)], after, m == chunks - 1)
    else:
        top = jnp.concatenate([tokens, cotangent], axis=1)
        low = jnp.pad(routes_pad, ((0, 0), (0, 2 * features - token_count)))
        spread_start(jnp.concatenate([top, low], axis=0))
        sums = {}
        for n, j in units:
            new = step(n, j, {}, after)[0]
            after = [new]
            sums[n, j] = lax.psum(new, "dp")
        step(None, None, {}, after, logits=True)
        for n in range(chunks):
            after = finish(n, [sums[n, j] for j in range(3)], after)

    gathered = gather_direct(jnp.concatenate([signed[i] for i in range(experts)], axis=0), experts)
    out_y, grad_tokens, grad_router = run_end(
        [back[i] for i in range(experts)], packs, gathered, shared["gates"], shared["routes"], router_t, after
    )
    grad_a, grad_b, grad_di, grad_do = totals
    if share % 128:
        grad_b = lax.dynamic_slice_in_dim(grad_b, z_index * share, share, 2)
        grad_di = lax.dynamic_slice_in_dim(grad_di, z_index * share, share, 1)
    return (
        out_y,
        grad_tokens,
        grad_router.T,
        jnp.swapaxes(grad_a, 1, 2)[None],
        grad_b[None],
        grad_di.T[None],
        grad_do[None],
    )


def solution(mesh):
    in_specs = (
        P(("groups", "expert"), "dp"),
        P(("groups", "expert"), None),
        P("dp", None),
        P("expert", "dp", None),
        P("expert", None, "dp", None),
        P("expert", None, "dp", None),
        P("expert", None, None, None),
        P("expert", None, None),
        P("expert", None, "dp"),
        P(("groups", "expert"), "dp"),
    )
    out_specs = (
        P(("groups", "expert"), "dp"),
        P(("groups", "expert"), "dp"),
        P(("groups", "dp"), None),
        P(("groups", "expert"), None, "dp", None),
        P(("groups", "expert"), None, None, "dp"),
        P(("groups", "expert"), "dp", None),
        P(("groups", "expert"), None, "dp"),
    )
    return jax.shard_map(shards, mesh=mesh, in_specs=in_specs, out_specs=out_specs, check_vma=False)
```

time: 249 us -> 174 us (0.70)
  matrix products: 62 us -> 1.01 us
  Pallas kernels: 14.4 us -> 67.4 us
  other arithmetic: 28.5 us -> 2.98 us
  starting transfers between devices: 82.1 us -> 63 us
  waiting for transfers between devices: 42.3 us -> 27.2 us
  local copies, waits for them, and re-layouts: 14.9 us -> 9.26 us
    pallas_call x0 -> x24, Pallas kernels: none -> 49.3 us  [the longest x4 25 us: run_back(): pl.pallas_call(body, grid=(features // tile,), in_specs=specs, out_specs=...]
    dot_general x44 -> x2, matrix products: 33.9 us -> 1.01 us  [dot(): return jnp.dot(left, right, preferred_element_type=F32)]
    dot_general x52 -> x0, matrix products: 28 us -> none  [the longest x36 19 us: dot_nt(): lax.dot_general(left, right, (((1,), (1,)), ((), ())), preferred_element_...]
    ppermute x36 -> x28, starting transfers between devices: 69.6 us -> 52.5 us  [the longest x12 33.8 us: shards(): near[t] = lax.ppermute(carried[t], 'dp', way)]
    ppermute x36 -> x28, waiting for transfers between devices: 34.9 us -> 19.5 us  [the longest x12 19.5 us: shards(): near[t] = lax.ppermute(carried[t], 'dp', way)]
    add x24 -> x0, other arithmetic: 9.66 us -> none  [the longest x12 6.51 us: shards(): live['b'] = term[kb] + came[kb]]
    concatenate x10 -> x3, other arithmetic: 8.59 us -> 0.02 us  [the longest x1 0.01 us: shards(): jnp.concatenate([signed[i] for i in range(experts)], axis=0)]
    pallas_call x3, Pallas kernels: 14.4 us -> 18.2 us  [dequantize(): pl.pallas_call(functools.partial(dequantize_kernel, field=field), grid=(f...]
  transfers between devices with their start and end apart: 56 -> 39, of which waited for: 15 -> 9; matrix products, arithmetic and copies ran while one was open for 33% -> 1% of each run, Pallas kernels for 6% -> 32%
where the time goes in v2:
time: 174 us; the launch traced here: 172 us
  Pallas kernels  67.4 us (39%)
  starting transfers between devices  63 us (36%)
  waiting for transfers between devices  27.2 us (16%)
  local copies, waits for them, and re-layouts  9.26 us (5%)
  other arithmetic  2.98 us (2%)
    ppermute x12, starting transfers between devices, shards(): near[t] = lax.ppermute(carried[t], 'dp', way)  33.8 us
    pallas_call x4, Pallas kernels, run_back(): pl.pallas_call(body, grid=(features // tile,), in_specs=specs, out_specs=...  25 us
    pallas_call x20, Pallas kernels, call(): pl.pallas_call(kernel, grid=(1,) if piped else (), in_specs=[smem if a.dt...  24.3 us
    ppermute x12, waiting for transfers between devices, shards(): near[t] = lax.ppermute(carried[t], 'dp', way)  19.5 us
    pallas_call x3, Pallas kernels, dequantize(): pl.pallas_call(functools.partial(dequantize_kernel, field=field), grid=(f...  18.2 us
    ppermute x4, starting transfers between devices, shards(): near[t] = lax.ppermute(new, 'dp', INWARD)  10.5 us
    unnamed x50, local copies, waits for them, and re-layouts  9.22 us
    ppermute x12, starting transfers between devices, shards(): far[t] = lax.ppermute(inner[t], 'dp', MIDDLE)  8.26 us
  transfers between devices with their start and end apart: 39, of which 9 were waited for; matrix products, arithmetic and copies ran while one was open for 1% of the time, Pallas kernels for 32%

profile of v2, /device:TPU:0, one launch (start us, length us, event | category | flops | bytes accessed | tf_op | source)
XLA Modules:
  0.0 172.4 jit_solution(9509768805213016859)
XLA Ops:
  2.4 8.1 %shard_map.189.refs_3_.refs_10_.refs_14_ = bf16[1024,1536]{1,0:T(8,128)(2,1)} custom-call(s32[1024,1536]{1,0:T(8,128)} %bitcast.51, f32[3,24,1024]{2,1,0:T(8,128)} %bitcast.82, f32[8,128]{1,0:T(8,128)} %constant.30.clone.level_ref, bf16[24,1536]{1,0:T(8,128)(2,1)} %constant.31.clone.spread_ref), custom_call_target="tpu_custom_call" | custom-call | tf_op jit(solution)/shard_map/pallas_call | solution.py:77
  14.1 2.9 %collective-permute-start.1 = (bf16[144,2048]{1,0:T(8,128)(2,1)}, bf16[144,2048]{1,0:T(8,128)(2,1)}, u32[]{:S(2)}, u32[]{:S(2)}) collective-permute-start(bf16[144,2048]{1,0:T(8,128)(2,1)} %get-tuple-element.100.refs_2_.refs_9_.refs_4_), channel_id=1, source_target_pairs={{0,8},{4,12},{8,0},{12,4},{1,9},{5,13},{9,1},{13,5},{2,10},{6,14},... | collective-permute-start | bytes 1769480 | tf_op jit(solution)/shard_map/ppermute | solution.py:394
  17.0 4.2 %collective-permute-start.4 = (bf16[96,1600]{1,0:T(8,128)(2,1)}, bf16[96,1600]{1,0:T(8,128)(2,1)}, u32[]{:S(2)}, u32[]{:S(2)}) collective-permute-start(bf16[96,1600]{1,0:T(8,128)(2,1)} %get-tuple-element.102.refs_0_.refs_4_.refs_5_), channel_id=1, source_target_pairs={{0,1},{3,2},{4,5},{7,6},{8,9},{11,10},{12,13},{15,14},{16,17},{19,... | collective-permute-start | bytes 921608 | tf_op jit(solution)/shard_map/ppermute | solution.py:595
  21.2 5.0 %shard_map.191.refs_2_.refs_11_.refs_15_ = bf16[1024,1536]{1,0:T(8,128)(2,1)S(1)} custom-call(s32[1024,1536]{1,0:T(8,128)S(1)} %bitcast.52, f32[3,24,1024]{2,1,0:T(8,128)S(1)} %bitcast.83, f32[8,128]{1,0:T(8,128)S(1)} %copy-done.22, bf16[24,1536]{1,0:T(8,128)(2,1)S(1)} %copy-done.16, bf16[96,1600]{1,0:T(8,128)(2,1)} %get-tuple-element.102.refs_0_.refs_4_.refs_5_), custom_call_target="tpu_custom_call" | custom-call | tf_op jit(solution)/shard_map/pallas_call | solution.py:77
  32.1 5.0 %shard_map.193.refs_3_.refs_12_.refs_16_ = bf16[1024,1536]{1,0:T(8,128)(2,1)S(1)} custom-call(s32[1024,1536]{1,0:T(8,128)S(1)} %bitcast.53, f32[3,24,1024]{2,1,0:T(8,128)S(1)} %bitcast.84, f32[8,128]{1,0:T(8,128)S(1)} %copy-done.22, bf16[24,1536]{1,0:T(8,128)(2,1)S(1)} %copy-done.16, bf16[96,1600]{1,0:T(8,128)(2,1)} %shard_map.192.refs_0_.refs_7_.refs_5_), custom_call_target="tpu_custom_call" | custom-call | tf_op jit(solution)/shard_map/pallas_call | solution.py:77
  41.6 2.2 %shard_map.194 = (bf16[96,1024]{1,0:T(8,128)(2,1)S(1)}, bf16[96,1600]{1,0:T(8,128)(2,1)S(1)}, bf16[96,1600]{1,0:T(8,128)(2,1)S(1)}) custom-call(s32[1]{0:T(128)} %bitcast.1.refs_0_, bf16[96,128]{1,0:T(8,128)(2,1)S(1)} %copy-done.19, bf16[144,2048]{1,0:T(8,128)(2,1)} %get-tuple-element.100.refs_2_.refs_9_.refs_4_, bf16[1024,1536]{1,0:T(8,128)(2,1)S(1)} %copy-done.5, ...), custom_call_target="tpu_custom_call" | custom-call | tf_op jit(solution)/shard_map/pallas_call | solution.py:107
  48.7 2.2 %shard_map.195 = (bf16[96,1024]{1,0:T(8,128)(2,1)S(1)}, bf16[96,1600]{1,0:T(8,128)(2,1)S(1)}, bf16[96,1600]{1,0:T(8,128)(2,1)S(1)}) custom-call(s32[1]{0:T(128)} %bitcast.1.refs_0_, bf16[96,128]{1,0:T(8,128)(2,1)S(1)} %fusion.5.refs_1_.refs_15_, bf16[144,2048]{1,0:T(8,128)(2,1)} %collective-permute-done.1.refs_2_.refs_11_.refs_6_, ...), custom_call_target="tpu_custom_call" | custom-call | tf_op jit(solution)/shard_map/pallas_call | solution.py:107
  50.8 2.7 %collective-permute-start.9 = (bf16[96,1600]{1,0:T(8,128)(2,1)S(1)}, bf16[96,1600]{1,0:T(8,128)(2,1)S(1)}, u32[]{:S(2)}, u32[]{:S(2)}) collective-permute-start(bf16[96,1600]{1,0:T(8,128)(2,1)S(1)} %get-tuple-element.106.refs_13_.refs_5_), channel_id=1, source_target_pairs={{0,1},{3,2},{4,5},{7,6},{8,9},{11,10},{12,13},{15,14},{16,17},{19,... | collective-permute-start | bytes 921608 | tf_op jit(solution)/shard_map/ppermute | solution.py:595
  53.6 2.8 %shard_map.196 = (bf16[96,1600]{1,0:T(8,128)(2,1)S(1)}, bf16[96,1600]{1,0:T(8,128)(2,1)S(1)}, bf16[96,1600]{1,0:T(8,128)(2,1)S(1)}, f32[4,512]{1,0:T(4,128)S(1)}) custom-call(s32[1]{0:T(128)} %bitcast.1.refs_0_, bf16[96,1024]{1,0:T(8,128)(2,1)S(1)} %get-tuple-element.104.refs_1_.refs_8_, bf16[1024,1536]{1,0:T(8,128)(2,1)S(1)} %copy-done.3, ...), custom_call_target="tpu_custom_call" | custom-call | tf_op jit(solution)/shard_map/pallas_call | solution.py:107
  58.9 2.9 %collective-permute-start.7 = (bf16[96,1600]{1,0:T(8,128)(2,1)S(1)}, bf16[96,1600]{1,0:T(8,128)(2,1)S(1)}, u32[]{:S(2)}, u32[]{:S(2)}) collective-permute-start(bf16[96,1600]{1,0:T(8,128)(2,1)S(1)} %get-tuple-element.108.refs_9_), channel_id=1, source_target_pairs={{0,1},{3,2},{1,0},{2,3},{4,5},{7,6},{5,4},{6,7},{8,9},{11,10},{9,8... | collective-permute-start | bytes 921608 | tf_op jit(solution)/shard_map/ppermute | solution.py:593
  62.7 2.8 %collective-permute-start.16 = (f32[4,512]{1,0:T(4,128)S(1)}, f32[4,512]{1,0:T(4,128)S(1)}, u32[]{:S(2)}, u32[]{:S(2)}) collective-permute-start(f32[4,512]{1,0:T(4,128)S(1)} %add.34), channel_id=1, source_target_pairs={{0,2},{1,3},{2,0},{3,1},{4,6},{5,7},{6,4},{7,5},{8,10},{9,11},{10,... | collective-permute-start | bytes 24584 | tf_op jit(solution)/shard_map/ppermute | solution.py:421
  67.5 5.5 %collective-permute-start.11 = (bf16[96,1600]{1,0:T(8,128)(2,1)S(1)}, bf16[96,1600]{1,0:T(8,128)(2,1)S(1)}, u32[]{:S(2)}, u32[]{:S(2)}) collective-permute-start(bf16[96,1600]{1,0:T(8,128)(2,1)S(1)} %get-tuple-element.114.refs_8_), channel_id=1, source_target_pairs={{0,1},{3,2},{1,0},{2,3},{4,5},{7,6},{5,4},{6,7},{8,9},{11,10},{9,8... | collective-permute-start | bytes 921608 | tf_op jit(solution)/shard_map/ppermute | solution.py:593
  73.6 3.7 %collective-permute-done.16 = f32[4,512]{1,0:T(4,128)S(1)} collective-permute-done((f32[4,512]{1,0:T(4,128)S(1)}, f32[4,512]{1,0:T(4,128)S(1)}, u32[]{:S(2)}, u32[]{:S(2)}) %collective-permute-start.16) | collective-permute-done | bytes 8224 | tf_op jit(solution)/shard_map/ppermute | solution.py:421
  80.3 5.6 %collective-permute-start.17 = (bf16[96,1600]{1,0:T(8,128)(2,1)S(1)}, bf16[96,1600]{1,0:T(8,128)(2,1)S(1)}, u32[]{:S(2)}, u32[]{:S(2)}) collective-permute-start(bf16[96,1600]{1,0:T(8,128)(2,1)S(1)} %get-tuple-element.126.refs_9_), channel_id=1, source_target_pairs={{0,1},{3,2},{1,0},{2,3},{4,5},{7,6},{5,4},{6,7},{8,9},{11,10},{9,8... | collective-permute-start | bytes 921608 | tf_op jit(solution)/shard_map/ppermute | solution.py:593
  88.4 5.5 %collective-permute-start.21 = (bf16[96,1600]{1,0:T(8,128)(2,1)S(1)}, bf16[96,1600]{1,0:T(8,128)(2,1)S(1)}, u32[]{:S(2)}, u32[]{:S(2)}) collective-permute-start(bf16[96,1600]{1,0:T(8,128)(2,1)S(1)} %get-tuple-element.133.refs_8_), channel_id=1, source_target_pairs={{0,1},{3,2},{1,0},{2,3},{4,5},{7,6},{5,4},{6,7},{8,9},{11,10},{9,8... | collective-permute-start | bytes 921608 | tf_op jit(solution)/shard_map/ppermute | solution.py:593
  94.6 6.2 %shard_map.201 = (bf16[2,128,1024]{2,1,0:T(8,128)(2,1)S(1)}, f32[2,64,1024]{2,1,0:T(8,128)S(1)}, f32[2,64,384]{2,1,0:T(8,128)S(1)}, f32[64,384]{1,0:T(8,128)S(1)...) custom-call(s32[1]{0:T(128)} %bitcast.refs_0_, bf16[96,1600]{1,0:T(8,128)(2,1)S(1)} %get-tuple-element.112.refs_1_, ...), custom_call_target="tpu_custom_call" | custom-call | tf_op jit(solution)/shard_map/pallas_call | solution.py:349
  102.9 2.9 %collective-permute-start.19 = (bf16[96,1600]{1,0:T(8,128)(2,1)S(1)}, bf16[96,1600]{1,0:T(8,128)(2,1)S(1)}, u32[]{:S(2)}, u32[]{:S(2)}) collective-permute-start(bf16[96,1600]{1,0:T(8,128)(2,1)S(1)} %get-tuple-element.130.refs_9_), channel_id=1, source_target_pairs={{0,1},{3,2},{1,0},{2,3},{4,5},{7,6},{5,4},{6,7},{8,9},{11,10},{9,8... | collective-permute-start | bytes 921608 | tf_op jit(solution)/shard_map/ppermute | solution.py:593
  114.0 3.8 %collective-permute-start.23 = (bf16[96,1600]{1,0:T(8,128)(2,1)S(1)}, bf16[96,1600]{1,0:T(8,128)(2,1)S(1)}, u32[]{:S(2)}, u32[]{:S(2)}) collective-permute-start(bf16[96,1600]{1,0:T(8,128)(2,1)S(1)} %get-tuple-element.137.refs_5_), channel_id=1, source_target_pairs={{0,1},{3,2},{1,0},{2,3},{4,5},{7,6},{5,4},{6,7},{8,9},{11,10},{9,8... | collective-permute-start | bytes 921608 | tf_op jit(solution)/shard_map/ppermute | solution.py:593
  118.4 6.4 %shard_map.205 = (bf16[2,128,1024]{2,1,0:T(8,128)(2,1)S(1)}, f32[2,64,1024]{2,1,0:T(8,128)S(1)}, f32[2,64,384]{2,1,0:T(8,128)S(1)}, f32[64,384]{1,0:T(8,128)S(1)...) custom-call(s32[1]{0:T(128)} %bitcast.refs_0_, bf16[96,1600]{1,0:T(8,128)(2,1)S(1)} %get-tuple-element.141.refs_1_, ...), custom_call_target="tpu_custom_call" | custom-call | tf_op jit(solution)/shard_map/pallas_call | solution.py:349
  129.2 9.9 %collective-permute-done.30.refs_4_ = bf16[96,1600]{1,0:T(8,128)(2,1)S(1)} collective-permute-done((bf16[96,1600]{1,0:T(8,128)(2,1)S(1)}, bf16[96,1600]{1,0:T(8,128)(2,1)S(1)}, u32[]{:S(2)}, u32[]{:S(2)}) %collective-permute-start.30) | collective-permute-done | bytes 307232 | tf_op jit(solution)/shard_map/ppermute | solution.py:593
  140.5 6.3 %shard_map.209 = (bf16[2,128,1024]{2,1,0:T(8,128)(2,1)S(1)}, f32[2,64,1024]{2,1,0:T(8,128)S(1)}, f32[2,64,384]{2,1,0:T(8,128)S(1)}, f32[64,384]{1,0:T(8,128)S(1)...) custom-call(s32[1]{0:T(128)} %bitcast.refs_0_, bf16[96,1600]{1,0:T(8,128)(2,1)S(1)} %get-tuple-element.152.refs_1_, ...), custom_call_target="tpu_custom_call" | custom-call | tf_op jit(solution)/shard_map/pallas_call | solution.py:349
  149.4 6.5 %collective-permute-done.32.refs_2_ = bf16[96,1600]{1,0:T(8,128)(2,1)S(1)} collective-permute-done((bf16[96,1600]{1,0:T(8,128)(2,1)S(1)}, bf16[96,1600]{1,0:T(8,128)(2,1)S(1)}, u32[]{:S(2)}, u32[]{:S(2)}) %collective-permute-start.32) | collective-permute-done | bytes 307232 | tf_op jit(solution)/shard_map/ppermute | solution.py:593
  157.1 6.1 %shard_map.214 = (bf16[2,128,1024]{2,1,0:T(8,128)(2,1)S(1)}, f32[2,64,1024]{2,1,0:T(8,128)}, f32[2,64,384]{2,1,0:T(8,128)}, f32[64,384]{1,0:T(8,128)}, f32[64,1024]{1,0:T(8,128)}) custom-call(s32[1]{0:T(128)} %bitcast.refs_0_, bf16[96,1536]{1,0:T(8,128)(2,1)S(1)} %get-tuple-element.164.refs_1_.refs_24_, bf16[96,1536]{1,0:T(8,128)(2,1)S(1)} %get-tuple-element.165.refs_2_, ...), custom_call_target="tpu_custom_call" | custom-call | flops 6000000000 | bytes 16000000 | tf_op jit(solution)/shard_map/pallas_call | solution.py:349
  169.7 2.7 %shard_map.215 = (bf16[128,1024]{1,0:T(8,128)(2,1)}, bf16[128,1024]{1,0:T(8,128)(2,1)}, f32[4,1024]{1,0:T(4,128)}) custom-call(bf16[2,128,1024]{2,1,0:T(8,128)(2,1)S(1)} %get-tuple-element.125.refs_0_, bf16[2,128,1024]{2,1,0:T(8,128)(2,1)S(1)} %collective-permute-done.33.refs_1_, bf16[2,128,1024]{2,1,0:T(8,128)(2,1)S(1)} %collective-permute-done.34.refs_2_, ...), custom_call_target="tpu_custom_call" | custom-call | tf_op jit(solution)/shard_map/pallas_call | solution.py:107
  (161 shorter events, 59.1 us)
Async XLA Ops:
  14.1 32.1 %collective-permute-start.1 = (bf16[144,2048]{1,0:T(8,128)(2,1)}, bf16[144,2048]{1,0:T(8,128)(2,1)}, u32[]{:S(2)}, u32[]{:S(2)}) collective-permute-start(bf16[144,2048]{1,0:T(8,128)(2,1)} %get-tuple-element.100.refs_2_.refs_9_.refs_4_), channel_id=1, source_target_pairs={{0,8},{4,12},{8,0},{12,4},{1,9},{5,13},{9,1},{13,5},{2,10},{6,14},... | collective-permute-start | bytes 1769480 | tf_op jit(solution)/shard_map/ppermute | solution.py:394
  17.0 30.1 %collective-permute-start = (bf16[144,2048]{1,0:T(8,128)(2,1)}, bf16[144,2048]{1,0:T(8,128)(2,1)}, u32[]{:S(2)}, u32[]{:S(2)}) collective-permute-start(bf16[144,2048]{1,0:T(8,128)(2,1)} %get-tuple-element.100.refs_2_.refs_9_.refs_4_), channel_id=1, source_target_pairs={{0,4},{4,0},{8,12},{12,8},{1,5},{5,1},{9,13},{13,9},{2,6},{6,2},{1... | collective-permute-start | bytes 1769480 | tf_op jit(solution)/shard_map/ppermute | solution.py:394
  17.0 21.8 %collective-permute-start.4 = (bf16[96,1600]{1,0:T(8,128)(2,1)}, bf16[96,1600]{1,0:T(8,128)(2,1)}, u32[]{:S(2)}, u32[]{:S(2)}) collective-permute-start(bf16[96,1600]{1,0:T(8,128)(2,1)} %get-tuple-element.102.refs_0_.refs_4_.refs_5_), channel_id=1, source_target_pairs={{0,1},{3,2},{4,5},{7,6},{8,9},{11,10},{12,13},{15,14},{16,17},{19,... | collective-permute-start | bytes 921608 | tf_op jit(solution)/shard_map/ppermute | solution.py:595
  29.4 19.3 %collective-permute-start.3 = (bf16[96,1600]{1,0:T(8,128)(2,1)}, bf16[96,1600]{1,0:T(8,128)(2,1)}, u32[]{:S(2)}, u32[]{:S(2)}) collective-permute-start(bf16[96,1600]{1,0:T(8,128)(2,1)} %shard_map.192.refs_0_.refs_7_.refs_5_), channel_id=1, source_target_pairs={{0,1},{3,2},{4,5},{7,6},{8,9},{11,10},{12,13},{15,14},{16,17},{19,... | collective-permute-start | bytes 921608 | tf_op jit(solution)/shard_map/ppermute | solution.py:595
  43.9 9.7 %collective-permute-start.5 = (bf16[96,1600]{1,0:T(8,128)(2,1)S(1)}, bf16[96,1600]{1,0:T(8,128)(2,1)S(1)}, u32[]{:S(2)}, u32[]{:S(2)}) collective-permute-start(bf16[96,1600]{1,0:T(8,128)(2,1)S(1)} %get-tuple-element.103.refs_7_.refs_4_), channel_id=1, source_target_pairs={{0,1},{3,2},{4,5},{7,6},{8,9},{11,10},{12,13},{15,14},{16,17},{19,... | collective-permute-start | bytes 921608 | tf_op jit(solution)/shard_map/ppermute | solution.py:595
  50.8 14.6 %collective-permute-start.9 = (bf16[96,1600]{1,0:T(8,128)(2,1)S(1)}, bf16[96,1600]{1,0:T(8,128)(2,1)S(1)}, u32[]{:S(2)}, u32[]{:S(2)}) collective-permute-start(bf16[96,1600]{1,0:T(8,128)(2,1)S(1)} %get-tuple-element.106.refs_13_.refs_5_), channel_id=1, source_target_pairs={{0,1},{3,2},{4,5},{7,6},{8,9},{11,10},{12,13},{15,14},{16,17},{19,... | collective-permute-start | bytes 921608 | tf_op jit(solution)/shard_map/ppermute | solution.py:595
  58.9 18.5 %collective-permute-start.7 = (bf16[96,1600]{1,0:T(8,128)(2,1)S(1)}, bf16[96,1600]{1,0:T(8,128)(2,1)S(1)}, u32[]{:S(2)}, u32[]{:S(2)}) collective-permute-start(bf16[96,1600]{1,0:T(8,128)(2,1)S(1)} %get-tuple-element.108.refs_9_), channel_id=1, source_target_pairs={{0,1},{3,2},{1,0},{2,3},{4,5},{7,6},{5,4},{6,7},{8,9},{11,10},{9,8... | collective-permute-start | bytes 921608 | tf_op jit(solution)/shard_map/ppermute | solution.py:593
  61.9 15.6 %collective-permute-start.8 = (bf16[96,1600]{1,0:T(8,128)(2,1)S(1)}, bf16[96,1600]{1,0:T(8,128)(2,1)S(1)}, u32[]{:S(2)}, u32[]{:S(2)}) collective-permute-start(bf16[96,1600]{1,0:T(8,128)(2,1)S(1)} %get-tuple-element.109.refs_7_), channel_id=1, source_target_pairs={{1,2},{2,1},{5,6},{6,5},{9,10},{10,9},{13,14},{14,13},{17,18},{18,... | collective-permute-start | bytes 921608 | tf_op jit(solution)/shard_map/ppermute | solution.py:598
  62.7 14.7 %collective-permute-start.16 = (f32[4,512]{1,0:T(4,128)S(1)}, f32[4,512]{1,0:T(4,128)S(1)}, u32[]{:S(2)}, u32[]{:S(2)}) collective-permute-start(f32[4,512]{1,0:T(4,128)S(1)} %add.34), channel_id=1, source_target_pairs={{0,2},{1,3},{2,0},{3,1},{4,6},{5,7},{6,4},{7,5},{8,10},{9,11},{10,... | collective-permute-start | bytes 24584 | tf_op jit(solution)/shard_map/ppermute | solution.py:421
  67.5 12.0 %collective-permute-start.11 = (bf16[96,1600]{1,0:T(8,128)(2,1)S(1)}, bf16[96,1600]{1,0:T(8,128)(2,1)S(1)}, u32[]{:S(2)}, u32[]{:S(2)}) collective-permute-start(bf16[96,1600]{1,0:T(8,128)(2,1)S(1)} %get-tuple-element.114.refs_8_), channel_id=1, source_target_pairs={{0,1},{3,2},{1,0},{2,3},{4,5},{7,6},{5,4},{6,7},{8,9},{11,10},{9,8... | collective-permute-start | bytes 921608 | tf_op jit(solution)/shard_map/ppermute | solution.py:593
  80.3 20.5 %collective-permute-start.17 = (bf16[96,1600]{1,0:T(8,128)(2,1)S(1)}, bf16[96,1600]{1,0:T(8,128)(2,1)S(1)}, u32[]{:S(2)}, u32[]{:S(2)}) collective-permute-start(bf16[96,1600]{1,0:T(8,128)(2,1)S(1)} %get-tuple-element.126.refs_9_), channel_id=1, source_target_pairs={{0,1},{3,2},{1,0},{2,3},{4,5},{7,6},{5,4},{6,7},{8,9},{11,10},{9,8... | collective-permute-start | bytes 921608 | tf_op jit(solution)/shard_map/ppermute | solution.py:593
  85.9 14.9 %collective-permute-start.18 = (bf16[96,1600]{1,0:T(8,128)(2,1)S(1)}, bf16[96,1600]{1,0:T(8,128)(2,1)S(1)}, u32[]{:S(2)}, u32[]{:S(2)}) collective-permute-start(bf16[96,1600]{1,0:T(8,128)(2,1)S(1)} %get-tuple-element.127.refs_7_), channel_id=1, source_target_pairs={{1,2},{2,1},{5,6},{6,5},{9,10},{10,9},{13,14},{14,13},{17,18},{18,... | collective-permute-start | bytes 921608 | tf_op jit(solution)/shard_map/ppermute | solution.py:598
  88.4 18.1 %collective-permute-start.21 = (bf16[96,1600]{1,0:T(8,128)(2,1)S(1)}, bf16[96,1600]{1,0:T(8,128)(2,1)S(1)}, u32[]{:S(2)}, u32[]{:S(2)}) collective-permute-start(bf16[96,1600]{1,0:T(8,128)(2,1)S(1)} %get-tuple-element.133.refs_8_), channel_id=1, source_target_pairs={{0,1},{3,2},{1,0},{2,3},{4,5},{7,6},{5,4},{6,7},{8,9},{11,10},{9,8... | collective-permute-start | bytes 921608 | tf_op jit(solution)/shard_map/ppermute | solution.py:593
  93.9 12.6 %collective-permute-start.22 = (bf16[96,1600]{1,0:T(8,128)(2,1)S(1)}, bf16[96,1600]{1,0:T(8,128)(2,1)S(1)}, u32[]{:S(2)}, u32[]{:S(2)}) collective-permute-start(bf16[96,1600]{1,0:T(8,128)(2,1)S(1)} %get-tuple-element.134.refs_6_), channel_id=1, source_target_pairs={{1,2},{2,1},{5,6},{6,5},{9,10},{10,9},{13,14},{14,13},{17,18},{18,... | collective-permute-start | bytes 921608 | tf_op jit(solution)/shard_map/ppermute | solution.py:598
  107.3 17.5 %collective-permute-start.25 = (bf16[96,1600]{1,0:T(8,128)(2,1)S(1)}, bf16[96,1600]{1,0:T(8,128)(2,1)S(1)}, u32[]{:S(2)}, u32[]{:S(2)}) collective-permute-start(bf16[96,1600]{1,0:T(8,128)(2,1)S(1)} %get-tuple-element.139.refs_5_), channel_id=1, source_target_pairs={{0,1},{3,2},{1,0},{2,3},{4,5},{7,6},{5,4},{6,7},{8,9},{11,10},{9,8... | collective-permute-start | bytes 921608 | tf_op jit(solution)/shard_map/ppermute | solution.py:593
  109.4 15.4 %collective-permute-start.26 = (bf16[96,1600]{1,0:T(8,128)(2,1)S(1)}, bf16[96,1600]{1,0:T(8,128)(2,1)S(1)}, u32[]{:S(2)}, u32[]{:S(2)}) collective-permute-start(bf16[96,1600]{1,0:T(8,128)(2,1)S(1)} %get-tuple-element.140.refs_3_), channel_id=1, source_target_pairs={{1,2},{2,1},{5,6},{6,5},{9,10},{10,9},{13,14},{14,13},{17,18},{18,... | collective-permute-start | bytes 921608 | tf_op jit(solution)/shard_map/ppermute | solution.py:598
  114.0 13.0 %collective-permute-start.23 = (bf16[96,1600]{1,0:T(8,128)(2,1)S(1)}, bf16[96,1600]{1,0:T(8,128)(2,1)S(1)}, u32[]{:S(2)}, u32[]{:S(2)}) collective-permute-start(bf16[96,1600]{1,0:T(8,128)(2,1)S(1)} %get-tuple-element.137.refs_5_), channel_id=1, source_target_pairs={{0,1},{3,2},{1,0},{2,3},{4,5},{7,6},{5,4},{6,7},{8,9},{11,10},{9,8... | collective-permute-start | bytes 921608 | tf_op jit(solution)/shard_map/ppermute | solution.py:593
  117.7 9.3 %collective-permute-start.24 = (bf16[96,1600]{1,0:T(8,128)(2,1)S(1)}, bf16[96,1600]{1,0:T(8,128)(2,1)S(1)}, u32[]{:S(2)}, u32[]{:S(2)}) collective-permute-start(bf16[96,1600]{1,0:T(8,128)(2,1)S(1)} %get-tuple-element.138.refs_3_), channel_id=1, source_target_pairs={{1,2},{2,1},{5,6},{6,5},{9,10},{10,9},{13,14},{14,13},{17,18},{18,... | collective-permute-start | bytes 921608 | tf_op jit(solution)/shard_map/ppermute | solution.py:598
  125.7 13.4 %collective-permute-start.30 = (bf16[96,1600]{1,0:T(8,128)(2,1)S(1)}, bf16[96,1600]{1,0:T(8,128)(2,1)S(1)}, u32[]{:S(2)}, u32[]{:S(2)}) collective-permute-start(bf16[96,1600]{1,0:T(8,128)(2,1)S(1)} %get-tuple-element.154.refs_3_), channel_id=1, source_target_pairs={{1,0},{2,3},{5,4},{6,7},{9,8},{10,11},{13,12},{14,15},{17,16},{18,... | collective-permute-start | bytes 921608 | tf_op jit(solution)/shard_map/ppermute | solution.py:593
  127.2 19.7 %collective-permute-start.27 = (bf16[96,1600]{1,0:T(8,128)(2,1)S(1)}, bf16[96,1600]{1,0:T(8,128)(2,1)S(1)}, u32[]{:S(2)}, u32[]{:S(2)}) collective-permute-start(bf16[96,1600]{1,0:T(8,128)(2,1)S(1)} %get-tuple-element.150.refs_5_.refs_1_), channel_id=1, source_target_pairs={{1,2},{2,1},{5,6},{6,5},{9,10},{10,9},{13,14},{14,13},{17,18},{18,... | collective-permute-start | bytes 921608 | tf_op jit(solution)/shard_map/ppermute | solution.py:598
  127.9 19.0 %collective-permute-start.28 = (bf16[96,1600]{1,0:T(8,128)(2,1)S(1)}, bf16[96,1600]{1,0:T(8,128)(2,1)S(1)}, u32[]{:S(2)}, u32[]{:S(2)}) collective-permute-start(bf16[96,1600]{1,0:T(8,128)(2,1)S(1)} %get-tuple-element.151.refs_3_), channel_id=1, source_target_pairs={{1,0},{2,3},{5,4},{6,7},{9,8},{10,11},{13,12},{14,15},{17,16},{18,... | collective-permute-start | bytes 921608 | tf_op jit(solution)/shard_map/ppermute | solution.py:593
  139.2 10.2 %collective-permute-start.31 = (bf16[96,1600]{1,0:T(8,128)(2,1)S(1)}, bf16[96,1600]{1,0:T(8,128)(2,1)S(1)}, u32[]{:S(2)}, u32[]{:S(2)}) collective-permute-start(bf16[96,1600]{1,0:T(8,128)(2,1)S(1)} %get-tuple-element.160.refs_20_.refs_1_), channel_id=1, source_target_pairs={{1,0},{2,3},{5,4},{6,7},{9,8},{10,11},{13,12},{14,15},{17,16},{18,... | collective-permute-start | bytes 921608 | tf_op jit(solution)/shard_map/ppermute | solution.py:593
  148.3 16.0 %collective-permute-start.34 = (bf16[2,128,1024]{2,1,0:T(8,128)(2,1)S(1)}, bf16[2,128,1024]{2,1,0:T(8,128)(2,1)S(1)}, u32[]{:S(2)}, u32[]{:S(2)}) collective-permute-start(bf16[2,128,1024]{2,1,0:T(8,128)(2,1)S(1)} %get-tuple-element.180), channel_id=1, source_target_pairs={{0,8},{4,12},{8,0},{12,4},{1,9},{5,13},{9,1},{13,5},{2,10},{6,14},... | collective-permute-start | bytes 1572872 | tf_op jit(solution)/shard_map/ppermute | solution.py:394
  148.7 18.0 %collective-permute-start.35 = (bf16[2,128,1024]{2,1,0:T(8,128)(2,1)S(1)}, bf16[2,128,1024]{2,1,0:T(8,128)(2,1)S(1)}, u32[]{:S(2)}, u32[]{:S(2)}) collective-permute-start(bf16[2,128,1024]{2,1,0:T(8,128)(2,1)S(1)} %get-tuple-element.181), channel_id=1, source_target_pairs={{0,12},{4,8},{8,4},{12,0},{1,13},{5,9},{9,5},{13,1},{2,14},{6,10},... | collective-permute-start | bytes 1572872 | tf_op jit(solution)/shard_map/ppermute | solution.py:394
  (40 other events, 335.9 us)

commit v3 on v2

--- a/solution.py
+++ b/solution.py
@@ -134,7 +134,7 @@
         shapes.append(((count, weight.shape[1] + low.shape[-2]), BF16))
     for name in pairs:
         args += list(pairs[name])
-        shapes.append((pairs[name][0].shape, BF16))
+        shapes.append((pairs[name][0].shape, pairs[name][0].dtype))
     if pack is not None:
         args += list(pack)
         tokens, _, routes = pack
@@ -172,8 +172,8 @@
             term[:, width:] = dot_nt(rows_ref[...], low_map).astype(BF16)
         for name in pairs:
             left, right, out = ins.pop(0), ins.pop(0), outs.pop(0)
-            if name == "b" or (name == "c" and term is None):
-                out[...] = (left[...].astype(F32) + right[...].astype(F32)).astype(BF16)
+            if name in "be" or (name == "c" and term is None):
+                out[...] = (left[...].astype(F32) + right[...].astype(F32)).astype(out.dtype)
             elif name == "c":
 
                 @pl.when(is_end == 1)
@@ -278,7 +278,6 @@
         return pl.BlockSpec(value.shape, lambda i, n=value.ndim: (0,) * n)
 
     last = pl.BlockSpec((rows, tile), lambda i: (0, i))
-    lines = pl.BlockSpec((tile, hidden_width), lambda i: (i, 0))
     low = pl.BlockSpec((rank, tile), lambda i: (0, i))
     pair = pl.BlockSpec((2, rank, tile), lambda i: (0, 0, i))
     total_specs = [
@@ -293,7 +292,8 @@
     args = [share_start] + lead + [rows_x, rows_c] + list(weights) + [adapter_in_t, down_out]
     args += picks + totals + after
     specs = [pl.BlockSpec(memory_space=pltpu.SMEM)] + [fixed(value) for value in lead]
-    specs += [last, last, lines, lines, lines, pair, low] + [fixed(pick) for pick in picks]
+    resident = pl.BlockSpec(memory_space=pltpu.VMEM)
+    specs += [last, last, resident, resident, resident, pair, low] + [fixed(pick) for pick in picks]
     specs += total_specs[: len(totals)] + [pl.BlockSpec(memory_space=pl.ANY)] * len(after)
     shapes = [((2, tokens, features), BF16)] * sources
     shapes += [((2, rank, features), F32), ((2, rank, width), F32), ((rank, width), F32), ((rank, features), F32)]
@@ -320,8 +320,9 @@
                 middle_body(list(refs[1:led]) + list(picks_ref), list(middle) + [outs[sources + 4]])
 
         h_ref, gg_ref, gu_ref, hl_ref, lg_ref, lu_ref, hlg_ref, clg_ref, ag_ref, au_ref, gate_ref = middle
-        out = dot_nt(h_ref[...], wd[...]) + SCALE * dot(hl_ref[...], down_ref[...])
-        slot = (dot_nt(gg_ref[...], wg[...]) + dot_nt(gu_ref[...], wu[...])) + SCALE * (
+        lines = pl.ds(pl.multiple_of(pl.program_id(0) * tile, tile), tile)
+        out = dot_nt(h_ref[...], wd[lines, :]) + SCALE * dot(hl_ref[...], down_ref[...])
+        slot = (dot_nt(gg_ref[...], wg[lines, :]) + dot_nt(gu_ref[...], wu[lines, :])) + SCALE * (
             dot(lg_ref[...], maps[0]) + dot(lu_ref[...], maps[1])
         )
         for which, value in enumerate((out * gate_ref[...], slot)):
@@ -490,19 +491,31 @@
             second = jnp.concatenate([row[1:2] for row in rows[1:]], axis=0)
             picks[1:] = picks_of(first, second)
 
-    def settle_gates(logits):
-        logits = sum_dp(logits, parts)
-        all_routes = shared["routes"]
-        chosen = [
-            jnp.sum(jnp.where(all_routes[k : k + 1] == number, logits, 0.0), axis=0, keepdims=True)
-            for k in range(2)
-        ]
-        margin = chosen[0] - chosen[1]
-        gates = jnp.concatenate([jax.nn.sigmoid(margin), jax.nn.sigmoid(-margin)], axis=0)
-        shared["gates"] = gates
-        first = all_routes[0:1] == me
-        shared["mine"] = jnp.where(first, gates[0:1], gates[1:2]).reshape(experts, token_count)
-        shared["signs"] = jnp.where(first, 1.0, -1.0).reshape(experts, token_count)
+    def settle_gates(logits, more, after):
+        first = (shared["routes"][0:1] == me).astype(F32)
+        args = [logits] + ([more] if more is not None else []) + [shared["routes"], first]
+        row = ((1, first.shape[1]), F32)
+
+        def body(ins, outs):
+            total = ins[0][...] + (ins[1][...] if more is not None else 0.0)
+            routes_ref, first_ref = ins[-2:]
+            which = lax.broadcasted_iota(jnp.int32, (experts, 1), 0).astype(F32)
+            chosen = [
+                jnp.sum(jnp.where(routes_ref[k : k + 1, :] == which, total, 0.0), axis=0, keepdims=True)
+                for k in range(2)
+            ]
+            margin = chosen[0] - chosen[1]
+            gate, other = jax.nn.sigmoid(margin), jax.nn.sigmoid(-margin)
+            outs[0][0:1, :] = gate
+            outs[0][1:2, :] = other
+            mine = first_ref[...] > 0.5
+            outs[1][...] = jnp.where(mine, gate, other)
+            outs[2][...] = jnp.where(mine, 1.0, -1.0)
+
+        out = call(body, args, after, [((2, first.shape[1]), F32), row, row])
+        shared["gates"] = out[0]
+        shared["mine"] = out[1].reshape(experts, token_count)
+        shared["signs"] = out[2].reshape(experts, token_count)
 
     def step(n, j, pairs, after, logits=False):
         kind, unit, pack = None, None, None
@@ -510,20 +523,19 @@
             kind = j
             if weights[j] is None:
                 weights[j] = dequantize(codes, scales_t, levels, spread, j, *after)
-            early = not packs
             if j == 0:
-                taken = [(picks[i], tokens if early else packs[i], 0) for i in order[n]]
+                taken = [(picks[i], packs[i] if packs else tokens, 0) for i in order[n]]
                 unit = (None, taken, weights[0], adapter_in_t)
             elif j == 1:
                 unit = (chunk_x[n], None, weights[1], adapter_in_t)
             else:
                 unit = (None, [(picks[i], packs[i], features) for i in order[n]], weights[2], down_out)
-            if early:
+            if j == 0 and not packs:
                 pack = (tokens, cotangent, routes_pad)
         logits_of = (router_t, packs) if logits else None
         out = run_step(end, kind, unit, pairs, pack, logits_of, after)
         if logits:
-            settle_gates(out.pop())
+            shared["logits"] = out.pop()
         if pack is not None:
             spread_start(out.pop())
         term = None
@@ -535,7 +547,7 @@
             term = out.pop(0)
         return term, dict(zip(pairs, out))
 
-    back, totals, signed = {}, [], {}
+    back, totals, signed, waiting = {}, [], {}, {}
 
     def finish(n, sums, after, split=False):
         chosen = [picks[i] for i in order[n]]
@@ -565,8 +577,15 @@
         totals[:] = new
         for at, i in enumerate(order[n]):
             signed[i] = lines[0][at : at + 1]
-            back[i] = dense[at] if i == 0 else hop(dense[at], i, experts)
+            waiting[i] = dense[at]
         return [new[0]]
+
+    def send_back(n):
+        for i in order[n]:
+            value = waiting[i]
+            if i:
+                value = hop(value, i, experts)
+            back[i] = value
 
     chunks = len(order)
     units = [(n, j) for n in range(chunks) for j in range(3)]
@@ -584,7 +603,14 @@
             if 0 <= t - 3 * LAG < total:
                 pairs["d"] = (carried[old], near[old])
             n, j = units[t] if t < total else (None, None)
-            new, sums = step(n, j, pairs, after, logits=t == 4)
+            if t == 8:
+                pairs["e"] = (shared["logits"], nearby)
+            new, sums = step(n, j, pairs, after, logits=t == 6)
+            if t == 6:
+                nearby = lax.ppermute(shared["logits"], "dp", [(z, z ^ 1) for z in range(4)])
+            if t == 8:
+                shared["logits"] = sums.pop("e")
+                distant = lax.ppermute(shared["logits"], "dp", [(z, z ^ 2) for z in range(4)])
             if new is not None:
                 term[t] = new
             if "c" in sums:
@@ -598,11 +624,15 @@
                 far[t] = lax.ppermute(inner[t], "dp", MIDDLE)
             after = [new if new is not None else list(sums.values())[0]]
             if "d" in sums:
-                unit = t - 3 * LAG
-                final[unit] = sums["d"]
-                if unit % 3 == 2:
-                    m = unit // 3
-                    after = finish(m, [final[3 * m + f] for f in range(3)], after, m == chunks - 1)
+                final[t - 3 * LAG] = sums["d"]
+            for m in range(chunks):
+                wait = 2 if m < chunks - 2 else (1 if m < chunks - 1 else 0)
+                if t == 3 * m + 2 + 3 * LAG + wait:
+                    if m == 0:
+                        settle_gates(shared["logits"], distant, after)
+                    last = m == chunks - 1
+                    after = finish(m, [final[3 * m + f] for f in range(3)], after, last)
+                    send_back(m)
     else:
         top = jnp.concatenate([tokens, cotangent], axis=1)
         low = jnp.pad(routes_pad, ((0, 0), (0, 2 * features - token_count)))
@@ -613,8 +643,10 @@
             after = [new]
             sums[n, j] = lax.psum(new, "dp")
         step(None, None, {}, after, logits=True)
+        settle_gates(sum_dp(shared["logits"], parts), None, [])
         for n in range(chunks):
             after = finish(n, [sums[n, j] for j in range(3)], after)
+            send_back(n)
 
     gathered = gather_direct(jnp.concatenate([signed[i] for i in range(experts)], axis=0), experts)
     out_y, grad_tokens, grad_router = run_end(

time: 174 us -> 162 us (0.931)
  starting transfers between devices: 63 us -> 56.8 us
  Pallas kernels: 67.4 us -> 61.7 us
  local copies, waits for them, and re-layouts: 9.26 us -> 12.6 us
    ppermute x12, starting transfers between devices: 33.8 us -> 22.6 us  [shards(): near[t] = lax.ppermute(carried[t], 'dp', way)]
    ppermute x4, waiting for transfers between devices: 0.01 us -> 6.28 us  [shards(): near[t] = lax.ppermute(new, 'dp', INWARD)]
    pallas_call x20 -> x21, Pallas kernels: 24.3 us -> 18.3 us  [call(): pl.pallas_call(kernel, grid=(1,) if piped else (), in_specs=[smem if a.dt...]
    ppermute x12, waiting for transfers between devices: 19.5 us -> 14.7 us  [shards(): near[t] = lax.ppermute(carried[t], 'dp', way)]
    ppermute x2, waiting for transfers between devices: 3.71 us -> 0.01 us  [the longest x1 0.01 us: shards(): lax.ppermute(shared['logits'], 'dp', [(z, z ^ 2) for z in range(4)])]
    unnamed x50 -> x124, local copies, waits for them, and re-layouts: 9.22 us -> 11.4 us
where the time goes in v3:
time: 162 us; the launch traced here: 161 us
  Pallas kernels  61.7 us (38%)
  starting transfers between devices  56.8 us (35%)
  waiting for transfers between devices  25.9 us (16%)
  local copies, waits for them, and re-layouts  12.6 us (8%)
  between operations  1.92 us (1%)
    pallas_call x4, Pallas kernels, run_back(): pl.pallas_call(body, grid=(features // tile,), in_specs=specs, out_specs=...  25.1 us
    ppermute x12, starting transfers between devices, shards(): near[t] = lax.ppermute(carried[t], 'dp', way)  22.6 us
    pallas_call x21, Pallas kernels, call(): pl.pallas_call(kernel, grid=(1,) if piped else (), in_specs=[smem if a.dt...  18.3 us
    pallas_call x3, Pallas kernels, dequantize(): pl.pallas_call(functools.partial(dequantize_kernel, field=field), grid=(f...  18.2 us
    ppermute x12, waiting for transfers between devices, shards(): near[t] = lax.ppermute(carried[t], 'dp', way)  14.7 us
    ppermute x4, starting transfers between devices, shards(): near[t] = lax.ppermute(new, 'dp', INWARD)  12 us
    unnamed x124, local copies, waits for them, and re-layouts  11.4 us
    ppermute x12, starting transfers between devices, shards(): far[t] = lax.ppermute(inner[t], 'dp', MIDDLE)  9.7 us
  transfers between devices with their start and end apart: 39, of which 9 were waited for; matrix products, arithmetic and copies ran while one was open for 1% of the time, Pallas kernels for 32%

profile of v3, /device:TPU:0, one launch (start us, length us, event | category | flops | bytes accessed | tf_op | source)
XLA Modules:
  0.0 161.3 jit_solution(4760304344200798172)
XLA Ops:
  2.4 8.1 %shard_map.189.refs_3_.refs_10_.refs_14_ = bf16[1024,1536]{1,0:T(8,128)(2,1)} custom-call(s32[1024,1536]{1,0:T(8,128)} %bitcast.47, f32[3,24,1024]{2,1,0:T(8,128)} %bitcast.78, f32[8,128]{1,0:T(8,128)} %constant.23.clone.level_ref, bf16[24,1536]{1,0:T(8,128)(2,1)} %constant.24.clone.spread_ref), custom_call_target="tpu_custom_call" | custom-call | tf_op jit(solution)/shard_map/pallas_call | solution.py:77
  13.3 3.0 %collective-permute-start.1 = (bf16[144,2048]{1,0:T(8,128)(2,1)S(1)}, bf16[144,2048]{1,0:T(8,128)(2,1)S(1)}, u32[]{:S(2)}, u32[]{:S(2)}) collective-permute-start(bf16[144,2048]{1,0:T(8,128)(2,1)S(1)} %get-tuple-element.104.refs_2_.refs_12_.refs_4_), channel_id=1, source_target_pairs={{0,8},{4,12},{8,0},{12,4},{1,9},{5,13},{9,1},{13,5},{2,10},{6,14},... | collective-permute-start | bytes 1769480 | tf_op jit(solution)/shard_map/ppermute | solution.py:395
  16.3 3.5 %collective-permute-start.4 = (bf16[96,1600]{1,0:T(8,128)(2,1)S(1)}, bf16[96,1600]{1,0:T(8,128)(2,1)S(1)}, u32[]{:S(2)}, u32[]{:S(2)}) collective-permute-start(bf16[96,1600]{1,0:T(8,128)(2,1)S(1)} %get-tuple-element.106.refs_0_.refs_4_.refs_5_), channel_id=1, source_target_pairs={{0,1},{3,2},{4,5},{7,6},{8,9},{11,10},{12,13},{15,14},{16,17},{19,... | collective-permute-start | bytes 921608 | tf_op jit(solution)/shard_map/ppermute | solution.py:621
  19.9 5.0 %shard_map.191.refs_2_.refs_11_.refs_15_ = bf16[1024,1536]{1,0:T(8,128)(2,1)S(1)} custom-call(s32[1024,1536]{1,0:T(8,128)S(1)} %bitcast.48, f32[3,24,1024]{2,1,0:T(8,128)S(1)} %bitcast.79, f32[8,128]{1,0:T(8,128)S(1)} %copy-done.50, bf16[24,1536]{1,0:T(8,128)(2,1)S(1)} %copy-done.34, bf16[96,1600]{1,0:T(8,128)(2,1)S(1)} %get-tuple-element.106.refs_0_.refs_4_.refs_5_), custom_call_target="tpu_custom_call" | custom-call | tf_op jit(solution)/shard_map/pallas_call | solution.py:77
  27.1 5.0 %shard_map.193.refs_3_.refs_12_.refs_16_ = bf16[1024,1536]{1,0:T(8,128)(2,1)S(1)} custom-call(s32[1024,1536]{1,0:T(8,128)S(1)} %bitcast.49, f32[3,24,1024]{2,1,0:T(8,128)S(1)} %bitcast.80, f32[8,128]{1,0:T(8,128)S(1)} %copy-done.50, bf16[24,1536]{1,0:T(8,128)(2,1)S(1)} %copy-done.34, bf16[96,1600]{1,0:T(8,128)(2,1)S(1)} %shard_map.192.refs_0_.refs_7_.refs_5_), custom_call_target="tpu_custom_call" | custom-call | tf_op jit(solution)/shard_map/pallas_call | solution.py:77
  41.1 5.7 %collective-permute-start.9 = (bf16[96,1600]{1,0:T(8,128)(2,1)S(1)}, bf16[96,1600]{1,0:T(8,128)(2,1)S(1)}, u32[]{:S(2)}, u32[]{:S(2)}) collective-permute-start(bf16[96,1600]{1,0:T(8,128)(2,1)S(1)} %get-tuple-element.110.refs_8_.refs_5_), channel_id=1, source_target_pairs={{0,1},{3,2},{4,5},{7,6},{8,9},{11,10},{12,13},{15,14},{16,17},{19,... | collective-permute-start | bytes 921608 | tf_op jit(solution)/shard_map/ppermute | solution.py:621
  48.3 6.3 %collective-permute-done.9.refs_6_ = bf16[96,1600]{1,0:T(8,128)(2,1)S(1)} collective-permute-done((bf16[96,1600]{1,0:T(8,128)(2,1)S(1)}, bf16[96,1600]{1,0:T(8,128)(2,1)S(1)}, u32[]{:S(2)}, u32[]{:S(2)}) %collective-permute-start.9) | collective-permute-done | bytes 307232 | tf_op jit(solution)/shard_map/ppermute | solution.py:621
  57.0 2.5 %collective-permute-start.11 = (bf16[96,1600]{1,0:T(8,128)(2,1)}, bf16[96,1600]{1,0:T(8,128)(2,1)}, u32[]{:S(2)}, u32[]{:S(2)}) collective-permute-start(bf16[96,1600]{1,0:T(8,128)(2,1)} %get-tuple-element.118.refs_8_), channel_id=1, source_target_pairs={{0,1},{3,2},{1,0},{2,3},{4,5},{7,6},{5,4},{6,7},{8,9},{11,10},{9,8... | collective-permute-start | bytes 921608 | tf_op jit(solution)/shard_map/ppermute | solution.py:619
  61.5 2.1 %shard_map.198 = (bf16[96,1024]{1,0:T(8,128)(2,1)S(1)}, bf16[96,1600]{1,0:T(8,128)(2,1)S(1)}, bf16[96,1600]{1,0:T(8,128)(2,1)}, bf16[96,1600]{1,0:T(8,128)(2,1)}...) custom-call(s32[1]{0:T(128)} %bitcast.1.refs_0_, bf16[96,128]{1,0:T(8,128)(2,1)S(1)} %fusion.3.refs_1_.refs_15_, ...), custom_call_target="tpu_custom_call" | custom-call | tf_op jit(solution)/shard_map/pallas_call | solution.py:107
  65.8 2.5 %collective-permute-start.13 = (bf16[96,1600]{1,0:T(8,128)(2,1)}, bf16[96,1600]{1,0:T(8,128)(2,1)}, u32[]{:S(2)}, u32[]{:S(2)}) collective-permute-start(bf16[96,1600]{1,0:T(8,128)(2,1)} %get-tuple-element.122.refs_9_), channel_id=1, source_target_pairs={{0,1},{3,2},{1,0},{2,3},{4,5},{7,6},{5,4},{6,7},{8,9},{11,10},{9,8... | collective-permute-start | bytes 921608 | tf_op jit(solution)/shard_map/ppermute | solution.py:619
  70.2 2.1 %collective-permute-start.15 = (f32[4,512]{1,0:T(4,128)S(1)}, f32[4,512]{1,0:T(4,128)S(1)}, u32[]{:S(2)}, u32[]{:S(2)}) collective-permute-start(f32[4,512]{1,0:T(4,128)S(1)} %get-tuple-element.124.refs_11_), channel_id=1, source_target_pairs={{0,1},{1,0},{2,3},{3,2},{4,5},{5,4},{6,7},{7,6},{8,9},{9,8},{10,11... | collective-permute-start | bytes 24584 | tf_op jit(solution)/shard_map/ppermute | solution.py:610
  77.1 2.3 %shard_map.199 = (bf16[96,1600]{1,0:T(8,128)(2,1)S(1)}, bf16[96,1600]{1,0:T(8,128)(2,1)S(1)}, bf16[96,1600]{1,0:T(8,128)(2,1)S(1)}, bf16[96,1600]{1,0:T(8,128)(2,1)S(1)}) custom-call(s32[1]{0:T(128)} %bitcast.1.refs_0_, bf16[96,1024]{1,0:T(8,128)(2,1)S(1)} %copy-done.30, bf16[1024,1536]{1,0:T(8,128)(2,1)S(1)} %copy-done.5, ...), custom_call_target="tpu_custom_call" | custom-call | tf_op jit(solution)/shard_map/pallas_call | solution.py:107
  80.7 2.3 %shard_map.200 = (bf16[96,1024]{1,0:T(8,128)(2,1)S(1)}, bf16[96,1600]{1,0:T(8,128)(2,1)S(1)}, bf16[96,1600]{1,0:T(8,128)(2,1)S(1)}, bf16[96,1600]{1,0:T(8,128)(2...) custom-call(s32[1]{0:T(128)} %bitcast.1.refs_0_, bf16[96,128]{1,0:T(8,128)(2,1)S(1)} %copy-done.39, ...), custom_call_target="tpu_custom_call" | custom-call | tf_op jit(solution)/shard_map/pallas_call | solution.py:107
  83.1 3.6 %collective-permute-start.19 = (bf16[96,1600]{1,0:T(8,128)(2,1)S(1)}, bf16[96,1600]{1,0:T(8,128)(2,1)S(1)}, u32[]{:S(2)}, u32[]{:S(2)}) collective-permute-start(bf16[96,1600]{1,0:T(8,128)(2,1)S(1)} %get-tuple-element.132.refs_8_), channel_id=1, source_target_pairs={{0,1},{3,2},{1,0},{2,3},{4,5},{7,6},{5,4},{6,7},{8,9},{11,10},{9,8... | collective-permute-start | bytes 921608 | tf_op jit(solution)/shard_map/ppermute | solution.py:619
  87.4 3.0 %collective-permute-start.16 = (f32[4,512]{1,0:T(4,128)S(1)}, f32[4,512]{1,0:T(4,128)S(1)}, u32[]{:S(2)}, u32[]{:S(2)}) collective-permute-start(f32[4,512]{1,0:T(4,128)S(1)} %get-tuple-element.127.refs_0_), channel_id=1, source_target_pairs={{0,2},{1,3},{2,0},{3,1},{4,6},{5,7},{6,4},{7,5},{8,10},{9,11},{10,... | collective-permute-start | bytes 24584 | tf_op jit(solution)/shard_map/ppermute | solution.py:613
  96.1 4.2 %collective-permute-start.25 = (bf16[96,1600]{1,0:T(8,128)(2,1)S(1)}, bf16[96,1600]{1,0:T(8,128)(2,1)S(1)}, u32[]{:S(2)}, u32[]{:S(2)}) collective-permute-start(bf16[96,1600]{1,0:T(8,128)(2,1)S(1)} %get-tuple-element.146.refs_5_), channel_id=1, source_target_pairs={{0,1},{3,2},{1,0},{2,3},{4,5},{7,6},{5,4},{6,7},{8,9},{11,10},{9,8... | collective-permute-start | bytes 921608 | tf_op jit(solution)/shard_map/ppermute | solution.py:619
  101.1 6.3 %shard_map.204 = (bf16[2,128,1024]{2,1,0:T(8,128)(2,1)S(1)}, f32[2,64,1024]{2,1,0:T(8,128)S(1)}, f32[2,64,384]{2,1,0:T(8,128)S(1)}, f32[64,384]{1,0:T(8,128)S(1)...) custom-call(s32[1]{0:T(128)} %bitcast.refs_0_, bf16[96,1600]{1,0:T(8,128)(2,1)S(1)} %copy-done.44, ...), custom_call_target="tpu_custom_call" | custom-call | tf_op jit(solution)/shard_map/pallas_call | solution.py:350
  108.4 2.1 %collective-permute-start.23 = (bf16[96,1600]{1,0:T(8,128)(2,1)S(1)}, bf16[96,1600]{1,0:T(8,128)(2,1)S(1)}, u32[]{:S(2)}, u32[]{:S(2)}) collective-permute-start(bf16[96,1600]{1,0:T(8,128)(2,1)S(1)} %get-tuple-element.144.refs_5_), channel_id=1, source_target_pairs={{0,1},{3,2},{1,0},{2,3},{4,5},{7,6},{5,4},{6,7},{8,9},{11,10},{9,8... | collective-permute-start | bytes 921608 | tf_op jit(solution)/shard_map/ppermute | solution.py:619
  113.4 3.8 %collective-permute-done.23.refs_2_.refs_6_ = bf16[96,1600]{1,0:T(8,128)(2,1)S(1)} collective-permute-done((bf16[96,1600]{1,0:T(8,128)(2,1)S(1)}, bf16[96,1600]{1,0:T(8,128)(2,1)S(1)}, u32[]{:S(2)}, u32[]{:S(2)}) %collective-permute-start.23) | collective-permute-done | bytes 307232 | tf_op jit(solution)/shard_map/ppermute | solution.py:619
  119.4 6.4 %shard_map.208 = (bf16[2,128,1024]{2,1,0:T(8,128)(2,1)S(1)}, f32[2,64,1024]{2,1,0:T(8,128)S(1)}, f32[2,64,384]{2,1,0:T(8,128)S(1)}, f32[64,384]{1,0:T(8,128)S(1)...) custom-call(s32[1]{0:T(128)} %bitcast.refs_0_, bf16[96,1600]{1,0:T(8,128)(2,1)S(1)} %get-tuple-element.152.refs_1_, ...), custom_call_target="tpu_custom_call" | custom-call | tf_op jit(solution)/shard_map/pallas_call | solution.py:350
  127.7 8.4 %collective-permute-done.28.refs_4_ = bf16[96,1600]{1,0:T(8,128)(2,1)S(1)} collective-permute-done((bf16[96,1600]{1,0:T(8,128)(2,1)S(1)}, bf16[96,1600]{1,0:T(8,128)(2,1)S(1)}, u32[]{:S(2)}, u32[]{:S(2)}) %collective-permute-start.28) | collective-permute-done | bytes 307232 | tf_op jit(solution)/shard_map/ppermute | solution.py:619
  138.1 6.4 %shard_map.211 = (bf16[2,128,1024]{2,1,0:T(8,128)(2,1)S(1)}, f32[2,64,1024]{2,1,0:T(8,128)S(1)}, f32[2,64,384]{2,1,0:T(8,128)S(1)}, f32[64,384]{1,0:T(8,128)S(1)...) custom-call(s32[1]{0:T(128)} %bitcast.refs_0_, bf16[96,1600]{1,0:T(8,128)(2,1)S(1)} %get-tuple-element.162.refs_1_, ...), custom_call_target="tpu_custom_call" | custom-call | tf_op jit(solution)/shard_map/pallas_call | solution.py:350
  146.4 6.0 %shard_map.215 = (bf16[2,128,1024]{2,1,0:T(8,128)(2,1)S(1)}, f32[2,64,1024]{2,1,0:T(8,128)}, f32[2,64,384]{2,1,0:T(8,128)}, f32[64,384]{1,0:T(8,128)}, f32[64,1024]{1,0:T(8,128)}) custom-call(s32[1]{0:T(128)} %bitcast.refs_0_, bf16[96,1536]{1,0:T(8,128)(2,1)S(1)} %get-tuple-element.171.refs_1_.refs_24_, bf16[96,1536]{1,0:T(8,128)(2,1)S(1)} %get-tuple-element.172.refs_2_, ...), custom_call_target="tpu_custom_call" | custom-call | flops 6000000000 | bytes 16000000 | tf_op jit(solution)/shard_map/pallas_call | solution.py:350
  155.6 3.3 %collective-permute-done.37.refs_10_ = f32[4,128]{1,0:T(4,128)S(1)} collective-permute-done((f32[4,128]{1,0:T(4,128)S(1)}, f32[4,128]{1,0:T(4,128)S(1)}, u32[]{:S(2)}, u32[]{:S(2)}) %collective-permute-start.37) | collective-permute-done | bytes 2080 | tf_op jit(solution)/shard_map/ppermute | solution.py:395
  (229 shorter events, 55.2 us)
Async XLA Ops:
  13.3 22.7 %collective-permute-start.1 = (bf16[144,2048]{1,0:T(8,128)(2,1)S(1)}, bf16[144,2048]{1,0:T(8,128)(2,1)S(1)}, u32[]{:S(2)}, u32[]{:S(2)}) collective-permute-start(bf16[144,2048]{1,0:T(8,128)(2,1)S(1)} %get-tuple-element.104.refs_2_.refs_12_.refs_4_), channel_id=1, source_target_pairs={{0,8},{4,12},{8,0},{12,4},{1,9},{5,13},{9,1},{13,5},{2,10},{6,14},... | collective-permute-start | bytes 1769480 | tf_op jit(solution)/shard_map/ppermute | solution.py:395
  16.3 16.0 %collective-permute-start.4 = (bf16[96,1600]{1,0:T(8,128)(2,1)S(1)}, bf16[96,1600]{1,0:T(8,128)(2,1)S(1)}, u32[]{:S(2)}, u32[]{:S(2)}) collective-permute-start(bf16[96,1600]{1,0:T(8,128)(2,1)S(1)} %get-tuple-element.106.refs_0_.refs_4_.refs_5_), channel_id=1, source_target_pairs={{0,1},{3,2},{4,5},{7,6},{8,9},{11,10},{12,13},{15,14},{16,17},{19,... | collective-permute-start | bytes 921608 | tf_op jit(solution)/shard_map/ppermute | solution.py:621
  19.8 16.7 %collective-permute-start = (bf16[144,2048]{1,0:T(8,128)(2,1)S(1)}, bf16[144,2048]{1,0:T(8,128)(2,1)S(1)}, u32[]{:S(2)}, u32[]{:S(2)}) collective-permute-start(bf16[144,2048]{1,0:T(8,128)(2,1)S(1)} %get-tuple-element.104.refs_2_.refs_12_.refs_4_), channel_id=1, source_target_pairs={{0,4},{4,0},{8,12},{12,8},{1,5},{5,1},{9,13},{13,9},{2,6},{6,2},{1... | collective-permute-start | bytes 1769480 | tf_op jit(solution)/shard_map/ppermute | solution.py:395
  25.7 13.7 %collective-permute-start.3 = (bf16[96,1600]{1,0:T(8,128)(2,1)S(1)}, bf16[96,1600]{1,0:T(8,128)(2,1)S(1)}, u32[]{:S(2)}, u32[]{:S(2)}) collective-permute-start(bf16[96,1600]{1,0:T(8,128)(2,1)S(1)} %shard_map.192.refs_0_.refs_7_.refs_5_), channel_id=1, source_target_pairs={{0,1},{3,2},{4,5},{7,6},{8,9},{11,10},{12,13},{15,14},{16,17},{19,... | collective-permute-start | bytes 921608 | tf_op jit(solution)/shard_map/ppermute | solution.py:621
  33.8 12.9 %collective-permute-start.5 = (bf16[96,1600]{1,0:T(8,128)(2,1)S(1)}, bf16[96,1600]{1,0:T(8,128)(2,1)S(1)}, u32[]{:S(2)}, u32[]{:S(2)}) collective-permute-start(bf16[96,1600]{1,0:T(8,128)(2,1)S(1)} %get-tuple-element.107.refs_7_.refs_4_), channel_id=1, source_target_pairs={{0,1},{3,2},{4,5},{7,6},{8,9},{11,10},{12,13},{15,14},{16,17},{19,... | collective-permute-start | bytes 921608 | tf_op jit(solution)/shard_map/ppermute | solution.py:621
  35.2 11.5 %collective-permute-start.6 = (bf16[96,1600]{1,0:T(8,128)(2,1)S(1)}, bf16[96,1600]{1,0:T(8,128)(2,1)S(1)}, u32[]{:S(2)}, u32[]{:S(2)}) collective-permute-start(bf16[96,1600]{1,0:T(8,128)(2,1)S(1)} %get-tuple-element.109.refs_6_), channel_id=1, source_target_pairs={{1,2},{2,1},{5,6},{6,5},{9,10},{10,9},{13,14},{14,13},{17,18},{18,... | collective-permute-start | bytes 921608 | tf_op jit(solution)/shard_map/ppermute | solution.py:624
  41.1 13.6 %collective-permute-start.9 = (bf16[96,1600]{1,0:T(8,128)(2,1)S(1)}, bf16[96,1600]{1,0:T(8,128)(2,1)S(1)}, u32[]{:S(2)}, u32[]{:S(2)}) collective-permute-start(bf16[96,1600]{1,0:T(8,128)(2,1)S(1)} %get-tuple-element.110.refs_8_.refs_5_), channel_id=1, source_target_pairs={{0,1},{3,2},{4,5},{7,6},{8,9},{11,10},{12,13},{15,14},{16,17},{19,... | collective-permute-start | bytes 921608 | tf_op jit(solution)/shard_map/ppermute | solution.py:621
  47.6 13.9 %collective-permute-start.7 = (bf16[96,1600]{1,0:T(8,128)(2,1)S(1)}, bf16[96,1600]{1,0:T(8,128)(2,1)S(1)}, u32[]{:S(2)}, u32[]{:S(2)}) collective-permute-start(bf16[96,1600]{1,0:T(8,128)(2,1)S(1)} %get-tuple-element.112.refs_9_), channel_id=1, source_target_pairs={{0,1},{3,2},{1,0},{2,3},{4,5},{7,6},{5,4},{6,7},{8,9},{11,10},{9,8... | collective-permute-start | bytes 921608 | tf_op jit(solution)/shard_map/ppermute | solution.py:619
  47.6 13.8 %collective-permute-start.8 = (bf16[96,1600]{1,0:T(8,128)(2,1)S(1)}, bf16[96,1600]{1,0:T(8,128)(2,1)S(1)}, u32[]{:S(2)}, u32[]{:S(2)}) collective-permute-start(bf16[96,1600]{1,0:T(8,128)(2,1)S(1)} %get-tuple-element.113.refs_7_), channel_id=1, source_target_pairs={{1,2},{2,1},{5,6},{6,5},{9,10},{10,9},{13,14},{14,13},{17,18},{18,... | collective-permute-start | bytes 921608 | tf_op jit(solution)/shard_map/ppermute | solution.py:624
  57.0 15.3 %collective-permute-start.11 = (bf16[96,1600]{1,0:T(8,128)(2,1)}, bf16[96,1600]{1,0:T(8,128)(2,1)}, u32[]{:S(2)}, u32[]{:S(2)}) collective-permute-start(bf16[96,1600]{1,0:T(8,128)(2,1)} %get-tuple-element.118.refs_8_), channel_id=1, source_target_pairs={{0,1},{3,2},{1,0},{2,3},{4,5},{7,6},{5,4},{6,7},{8,9},{11,10},{9,8... | collective-permute-start | bytes 921608 | tf_op jit(solution)/shard_map/ppermute | solution.py:619
  59.6 12.8 %collective-permute-start.12 = (bf16[96,1600]{1,0:T(8,128)(2,1)}, bf16[96,1600]{1,0:T(8,128)(2,1)}, u32[]{:S(2)}, u32[]{:S(2)}) collective-permute-start(bf16[96,1600]{1,0:T(8,128)(2,1)} %get-tuple-element.119.refs_6_), channel_id=1, source_target_pairs={{1,2},{2,1},{5,6},{6,5},{9,10},{10,9},{13,14},{14,13},{17,18},{18,... | collective-permute-start | bytes 921608 | tf_op jit(solution)/shard_map/ppermute | solution.py:624
  65.8 14.9 %collective-permute-start.13 = (bf16[96,1600]{1,0:T(8,128)(2,1)}, bf16[96,1600]{1,0:T(8,128)(2,1)}, u32[]{:S(2)}, u32[]{:S(2)}) collective-permute-start(bf16[96,1600]{1,0:T(8,128)(2,1)} %get-tuple-element.122.refs_9_), channel_id=1, source_target_pairs={{0,1},{3,2},{1,0},{2,3},{4,5},{7,6},{5,4},{6,7},{8,9},{11,10},{9,8... | collective-permute-start | bytes 921608 | tf_op jit(solution)/shard_map/ppermute | solution.py:619
  68.3 12.4 %collective-permute-start.14 = (bf16[96,1600]{1,0:T(8,128)(2,1)}, bf16[96,1600]{1,0:T(8,128)(2,1)}, u32[]{:S(2)}, u32[]{:S(2)}) collective-permute-start(bf16[96,1600]{1,0:T(8,128)(2,1)} %get-tuple-element.123.refs_7_), channel_id=1, source_target_pairs={{1,2},{2,1},{5,6},{6,5},{9,10},{10,9},{13,14},{14,13},{17,18},{18,... | collective-permute-start | bytes 921608 | tf_op jit(solution)/shard_map/ppermute | solution.py:624
  83.1 12.2 %collective-permute-start.19 = (bf16[96,1600]{1,0:T(8,128)(2,1)S(1)}, bf16[96,1600]{1,0:T(8,128)(2,1)S(1)}, u32[]{:S(2)}, u32[]{:S(2)}) collective-permute-start(bf16[96,1600]{1,0:T(8,128)(2,1)S(1)} %get-tuple-element.132.refs_8_), channel_id=1, source_target_pairs={{0,1},{3,2},{1,0},{2,3},{4,5},{7,6},{5,4},{6,7},{8,9},{11,10},{9,8... | collective-permute-start | bytes 921608 | tf_op jit(solution)/shard_map/ppermute | solution.py:619
  87.4 13.6 %collective-permute-start.16 = (f32[4,512]{1,0:T(4,128)S(1)}, f32[4,512]{1,0:T(4,128)S(1)}, u32[]{:S(2)}, u32[]{:S(2)}) collective-permute-start(f32[4,512]{1,0:T(4,128)S(1)} %get-tuple-element.127.refs_0_), channel_id=1, source_target_pairs={{0,2},{1,3},{2,0},{3,1},{4,6},{5,7},{6,4},{7,5},{8,10},{9,11},{10,... | collective-permute-start | bytes 24584 | tf_op jit(solution)/shard_map/ppermute | solution.py:613
  91.4 15.9 %collective-permute-start.21 = (bf16[96,1600]{1,0:T(8,128)(2,1)S(1)}, bf16[96,1600]{1,0:T(8,128)(2,1)S(1)}, u32[]{:S(2)}, u32[]{:S(2)}) collective-permute-start(bf16[96,1600]{1,0:T(8,128)(2,1)S(1)} %get-tuple-element.140.refs_9_), channel_id=1, source_target_pairs={{0,1},{3,2},{1,0},{2,3},{4,5},{7,6},{5,4},{6,7},{8,9},{11,10},{9,8... | collective-permute-start | bytes 921608 | tf_op jit(solution)/shard_map/ppermute | solution.py:619
  93.4 14.0 %collective-permute-start.22 = (bf16[96,1600]{1,0:T(8,128)(2,1)S(1)}, bf16[96,1600]{1,0:T(8,128)(2,1)S(1)}, u32[]{:S(2)}, u32[]{:S(2)}) collective-permute-start(bf16[96,1600]{1,0:T(8,128)(2,1)S(1)} %get-tuple-element.141.refs_7_), channel_id=1, source_target_pairs={{1,2},{2,1},{5,6},{6,5},{9,10},{10,9},{13,14},{14,13},{17,18},{18,... | collective-permute-start | bytes 921608 | tf_op jit(solution)/shard_map/ppermute | solution.py:624
  96.1 15.1 %collective-permute-start.25 = (bf16[96,1600]{1,0:T(8,128)(2,1)S(1)}, bf16[96,1600]{1,0:T(8,128)(2,1)S(1)}, u32[]{:S(2)}, u32[]{:S(2)}) collective-permute-start(bf16[96,1600]{1,0:T(8,128)(2,1)S(1)} %get-tuple-element.146.refs_5_), channel_id=1, source_target_pairs={{0,1},{3,2},{1,0},{2,3},{4,5},{7,6},{5,4},{6,7},{8,9},{11,10},{9,8... | collective-permute-start | bytes 921608 | tf_op jit(solution)/shard_map/ppermute | solution.py:619
  111.4 14.4 %collective-permute-start.29 = (bf16[96,1600]{1,0:T(8,128)(2,1)S(1)}, bf16[96,1600]{1,0:T(8,128)(2,1)S(1)}, u32[]{:S(2)}, u32[]{:S(2)}) collective-permute-start(bf16[96,1600]{1,0:T(8,128)(2,1)S(1)} %get-tuple-element.148.refs_7_.refs_1_), channel_id=1, source_target_pairs={{1,2},{2,1},{5,6},{6,5},{9,10},{10,9},{13,14},{14,13},{17,18},{18,... | collective-permute-start | bytes 921608 | tf_op jit(solution)/shard_map/ppermute | solution.py:624
  112.1 14.2 %collective-permute-start.30 = (bf16[96,1600]{1,0:T(8,128)(2,1)S(1)}, bf16[96,1600]{1,0:T(8,128)(2,1)S(1)}, u32[]{:S(2)}, u32[]{:S(2)}) collective-permute-start(bf16[96,1600]{1,0:T(8,128)(2,1)S(1)} %get-tuple-element.151.refs_3_), channel_id=1, source_target_pairs={{1,0},{2,3},{5,4},{6,7},{9,8},{10,11},{13,12},{14,15},{17,16},{18,... | collective-permute-start | bytes 921608 | tf_op jit(solution)/shard_map/ppermute | solution.py:619
  118.1 18.0 %collective-permute-start.28 = (bf16[96,1600]{1,0:T(8,128)(2,1)S(1)}, bf16[96,1600]{1,0:T(8,128)(2,1)S(1)}, u32[]{:S(2)}, u32[]{:S(2)}) collective-permute-start(bf16[96,1600]{1,0:T(8,128)(2,1)S(1)} %get-tuple-element.150.refs_3_), channel_id=1, source_target_pairs={{1,0},{2,3},{5,4},{6,7},{9,8},{10,11},{13,12},{14,15},{17,16},{18,... | collective-permute-start | bytes 921608 | tf_op jit(solution)/shard_map/ppermute | solution.py:619
  126.4 18.2 %collective-permute-start.31 = (bf16[96,1600]{1,0:T(8,128)(2,1)S(1)}, bf16[96,1600]{1,0:T(8,128)(2,1)S(1)}, u32[]{:S(2)}, u32[]{:S(2)}) collective-permute-start(bf16[96,1600]{1,0:T(8,128)(2,1)S(1)} %get-tuple-element.160.refs_5_.refs_1_), channel_id=1, source_target_pairs={{1,0},{2,3},{5,4},{6,7},{9,8},{10,11},{13,12},{14,15},{17,16},{18,... | collective-permute-start | bytes 921608 | tf_op jit(solution)/shard_map/ppermute | solution.py:619
  137.5 16.8 %collective-permute-start.34 = (bf16[2,128,1024]{2,1,0:T(8,128)(2,1)S(1)}, bf16[2,128,1024]{2,1,0:T(8,128)(2,1)S(1)}, u32[]{:S(2)}, u32[]{:S(2)}) collective-permute-start(bf16[2,128,1024]{2,1,0:T(8,128)(2,1)S(1)} %get-tuple-element.187), channel_id=1, source_target_pairs={{0,8},{4,12},{8,0},{12,4},{1,9},{5,13},{9,1},{13,5},{2,10},{6,14},... | collective-permute-start | bytes 1572872 | tf_op jit(solution)/shard_map/ppermute | solution.py:395
  144.5 14.4 %collective-permute-start.35 = (bf16[2,128,1024]{2,1,0:T(8,128)(2,1)S(1)}, bf16[2,128,1024]{2,1,0:T(8,128)(2,1)S(1)}, u32[]{:S(2)}, u32[]{:S(2)}) collective-permute-start(bf16[2,128,1024]{2,1,0:T(8,128)(2,1)S(1)} %get-tuple-element.188), channel_id=1, source_target_pairs={{0,12},{4,8},{8,4},{12,0},{1,13},{5,9},{9,5},{13,1},{2,14},{6,10},... | collective-permute-start | bytes 1572872 | tf_op jit(solution)/shard_map/ppermute | solution.py:395
  (77 other events, 718.1 us)

commit v4 on v3

--- a/solution.py
+++ b/solution.py
@@ -49,6 +49,14 @@
     return lax.dot_general(left, right, (((1,), (1,)), ((), ())), preferred_element_type=F32)
 
 
+def select_level(code):
+    found = list(NF4_LEVELS)
+    for bit in range(4):
+        odd = (code & (1 << bit)) != 0
+        found = [jnp.where(odd, found[2 * i + 1], found[2 * i]) for i in range(len(found) // 2)]
+    return found[0]
+
+
 def dequantize_kernel(code_ref, scale_ref, level_ref, spread_ref, *refs, field):
     out_ref = refs[-1]
     rows, width = code_ref.shape
@@ -64,7 +72,10 @@
         wide = (dot_tn(high, spread) + dot_tn(middle, spread)) + dot_tn(low, spread)
         for row in range(0, rows, step):
             code = (code_ref[row : row + step, column : column + 128] >> (4 * field)) & 15
-            level = jnp.take_along_axis(table, code, axis=1)
+            if column // 128 % 3 == 1:
+                level = select_level(code)
+            else:
+                level = jnp.take_along_axis(table, code, axis=1)
             out_ref[row : row + step, column : column + 128] = (
                 level * wide[row : row + step]
             ).astype(BF16)
@@ -91,7 +102,7 @@
     )(codes, scales, levels, spread, *after)
 
 
-def call(body, args, after, shapes, piped=False):
+def call(body, args, after, shapes, piped=False, limit=24):
     smem = pl.BlockSpec(memory_space=pltpu.SMEM)
     count = len(args)
     extra = len(after)
@@ -111,7 +122,7 @@
         + [pl.BlockSpec(memory_space=pl.ANY)] * extra,
         out_specs=[whole(shape) for shape, _ in shapes],
         out_shape=[jax.ShapeDtypeStruct(shape, dtype) for shape, dtype in shapes],
-        compiler_params=pltpu.CompilerParams(vmem_limit_bytes=(24 if piped else 10) * 2**20),
+        compiler_params=pltpu.CompilerParams(vmem_limit_bytes=(limit if piped else 10) * 2**20),
         cost_estimate=NO_COST,
     )(*args, *after)
     return list(out)
@@ -626,7 +637,7 @@
             if "d" in sums:
                 final[t - 3 * LAG] = sums["d"]
             for m in range(chunks):
-                wait = 2 if m < chunks - 2 else (1 if m < chunks - 1 else 0)
+                wait = (2, 3, 1, 0)[m]
                 if t == 3 * m + 2 + 3 * LAG + wait:
                     if m == 0:
                         settle_gates(shared["logits"], distant, after)

time: 162 us -> 160 us (0.988)
  no operation moved by 1% of the time
where the time goes in v4:
time: 160 us; the launch traced here: 159 us
  Pallas kernels  60.3 us (38%)
  starting transfers between devices  56.5 us (35%)
  waiting for transfers between devices  25 us (16%)
  local copies, waits for them, and re-layouts  12.6 us (8%)
  between operations  1.92 us (1%)
    pallas_call x4, Pallas kernels, run_back(): pl.pallas_call(body, grid=(features // tile,), in_specs=specs, out_specs=...  25.1 us
    ppermute x12, starting transfers between devices, shards(): near[t] = lax.ppermute(carried[t], 'dp', way)  22.5 us
    pallas_call x21, Pallas kernels, call(): pl.pallas_call(kernel, grid=(1,) if piped else (), in_specs=[smem if a.dt...  18.5 us
    pallas_call x3, Pallas kernels, dequantize(): pl.pallas_call(functools.partial(dequantize_kernel, field=field), grid=(f...  16.7 us
    ppermute x12, waiting for transfers between devices, shards(): near[t] = lax.ppermute(carried[t], 'dp', way)  13.8 us
    ppermute x4, starting transfers between devices, shards(): near[t] = lax.ppermute(new, 'dp', INWARD)  12 us
    unnamed x124, local copies, waits for them, and re-layouts  11.4 us
    ppermute x12, starting transfers between devices, shards(): far[t] = lax.ppermute(inner[t], 'dp', MIDDLE)  9.52 us
  transfers between devices with their start and end apart: 39, of which 9 were waited for; matrix products, arithmetic and copies ran while one was open for 1% of the time, Pallas kernels for 32%

profile of v4, /device:TPU:0, one launch (start us, length us, event | category | flops | bytes accessed | tf_op | source)
XLA Modules:
  0.0 158.7 jit_solution(7966763985998296371)
XLA Ops:
  2.4 8.0 %shard_map.189.refs_3_.refs_10_.refs_14_ = bf16[1024,1536]{1,0:T(8,128)(2,1)} custom-call(s32[1024,1536]{1,0:T(8,128)} %bitcast.47, f32[3,24,1024]{2,1,0:T(8,128)} %bitcast.78, f32[8,128]{1,0:T(8,128)} %constant.23.clone.level_ref, bf16[24,1536]{1,0:T(8,128)(2,1)} %constant.24.clone.spread_ref), custom_call_target="tpu_custom_call" | custom-call | tf_op jit(solution)/shard_map/pallas_call | solution.py:88
  13.1 3.0 %collective-permute-start.1 = (bf16[144,2048]{1,0:T(8,128)(2,1)S(1)}, bf16[144,2048]{1,0:T(8,128)(2,1)S(1)}, u32[]{:S(2)}, u32[]{:S(2)}) collective-permute-start(bf16[144,2048]{1,0:T(8,128)(2,1)S(1)} %get-tuple-element.104.refs_2_.refs_12_.refs_4_), channel_id=1, source_target_pairs={{0,8},{4,12},{8,0},{12,4},{1,9},{5,13},{9,1},{13,5},{2,10},{6,14},... | collective-permute-start | bytes 1769480 | tf_op jit(solution)/shard_map/ppermute | solution.py:406
  16.1 3.5 %collective-permute-start.4 = (bf16[96,1600]{1,0:T(8,128)(2,1)S(1)}, bf16[96,1600]{1,0:T(8,128)(2,1)S(1)}, u32[]{:S(2)}, u32[]{:S(2)}) collective-permute-start(bf16[96,1600]{1,0:T(8,128)(2,1)S(1)} %get-tuple-element.106.refs_0_.refs_4_.refs_5_), channel_id=1, source_target_pairs={{0,1},{3,2},{4,5},{7,6},{8,9},{11,10},{12,13},{15,14},{16,17},{19,... | collective-permute-start | bytes 921608 | tf_op jit(solution)/shard_map/ppermute | solution.py:632
  19.7 4.4 %shard_map.191.refs_2_.refs_11_.refs_15_ = bf16[1024,1536]{1,0:T(8,128)(2,1)S(1)} custom-call(s32[1024,1536]{1,0:T(8,128)S(1)} %bitcast.48, f32[3,24,1024]{2,1,0:T(8,128)S(1)} %bitcast.79, f32[8,128]{1,0:T(8,128)S(1)} %copy-done.50, bf16[24,1536]{1,0:T(8,128)(2,1)S(1)} %copy-done.34, bf16[96,1600]{1,0:T(8,128)(2,1)S(1)} %get-tuple-element.106.refs_0_.refs_4_.refs_5_), custom_call_target="tpu_custom_call" | custom-call | tf_op jit(solution)/shard_map/pallas_call | solution.py:88
  26.3 4.3 %shard_map.193.refs_3_.refs_12_.refs_16_ = bf16[1024,1536]{1,0:T(8,128)(2,1)S(1)} custom-call(s32[1024,1536]{1,0:T(8,128)S(1)} %bitcast.49, f32[3,24,1024]{2,1,0:T(8,128)S(1)} %bitcast.80, f32[8,128]{1,0:T(8,128)S(1)} %copy-done.50, bf16[24,1536]{1,0:T(8,128)(2,1)S(1)} %copy-done.34, bf16[96,1600]{1,0:T(8,128)(2,1)S(1)} %shard_map.192.refs_0_.refs_7_.refs_5_), custom_call_target="tpu_custom_call" | custom-call | tf_op jit(solution)/shard_map/pallas_call | solution.py:88
  39.5 5.6 %collective-permute-start.9 = (bf16[96,1600]{1,0:T(8,128)(2,1)S(1)}, bf16[96,1600]{1,0:T(8,128)(2,1)S(1)}, u32[]{:S(2)}, u32[]{:S(2)}) collective-permute-start(bf16[96,1600]{1,0:T(8,128)(2,1)S(1)} %get-tuple-element.110.refs_8_.refs_5_), channel_id=1, source_target_pairs={{0,1},{3,2},{4,5},{7,6},{8,9},{11,10},{12,13},{15,14},{16,17},{19,... | collective-permute-start | bytes 921608 | tf_op jit(solution)/shard_map/ppermute | solution.py:632
  46.8 6.3 %collective-permute-done.9.refs_6_ = bf16[96,1600]{1,0:T(8,128)(2,1)S(1)} collective-permute-done((bf16[96,1600]{1,0:T(8,128)(2,1)S(1)}, bf16[96,1600]{1,0:T(8,128)(2,1)S(1)}, u32[]{:S(2)}, u32[]{:S(2)}) %collective-permute-start.9) | collective-permute-done | bytes 307232 | tf_op jit(solution)/shard_map/ppermute | solution.py:632
  55.5 2.5 %collective-permute-start.11 = (bf16[96,1600]{1,0:T(8,128)(2,1)}, bf16[96,1600]{1,0:T(8,128)(2,1)}, u32[]{:S(2)}, u32[]{:S(2)}) collective-permute-start(bf16[96,1600]{1,0:T(8,128)(2,1)} %get-tuple-element.118.refs_8_), channel_id=1, source_target_pairs={{0,1},{3,2},{1,0},{2,3},{4,5},{7,6},{5,4},{6,7},{8,9},{11,10},{9,8... | collective-permute-start | bytes 921608 | tf_op jit(solution)/shard_map/ppermute | solution.py:630
  59.9 2.1 %shard_map.198 = (bf16[96,1024]{1,0:T(8,128)(2,1)S(1)}, bf16[96,1600]{1,0:T(8,128)(2,1)S(1)}, bf16[96,1600]{1,0:T(8,128)(2,1)}, bf16[96,1600]{1,0:T(8,128)(2,1)}...) custom-call(s32[1]{0:T(128)} %bitcast.1.refs_0_, bf16[96,128]{1,0:T(8,128)(2,1)S(1)} %fusion.3.refs_1_.refs_15_, ...), custom_call_target="tpu_custom_call" | custom-call | tf_op jit(solution)/shard_map/pallas_call | solution.py:118
  64.2 2.5 %collective-permute-start.13 = (bf16[96,1600]{1,0:T(8,128)(2,1)}, bf16[96,1600]{1,0:T(8,128)(2,1)}, u32[]{:S(2)}, u32[]{:S(2)}) collective-permute-start(bf16[96,1600]{1,0:T(8,128)(2,1)} %get-tuple-element.122.refs_9_), channel_id=1, source_target_pairs={{0,1},{3,2},{1,0},{2,3},{4,5},{7,6},{5,4},{6,7},{8,9},{11,10},{9,8... | collective-permute-start | bytes 921608 | tf_op jit(solution)/shard_map/ppermute | solution.py:630
  68.6 2.1 %collective-permute-start.15 = (f32[4,512]{1,0:T(4,128)S(1)}, f32[4,512]{1,0:T(4,128)S(1)}, u32[]{:S(2)}, u32[]{:S(2)}) collective-permute-start(f32[4,512]{1,0:T(4,128)S(1)} %get-tuple-element.124.refs_11_), channel_id=1, source_target_pairs={{0,1},{1,0},{2,3},{3,2},{4,5},{5,4},{6,7},{7,6},{8,9},{9,8},{10,11... | collective-permute-start | bytes 24584 | tf_op jit(solution)/shard_map/ppermute | solution.py:621
  75.5 2.3 %shard_map.199 = (bf16[96,1600]{1,0:T(8,128)(2,1)S(1)}, bf16[96,1600]{1,0:T(8,128)(2,1)S(1)}, bf16[96,1600]{1,0:T(8,128)(2,1)S(1)}, bf16[96,1600]{1,0:T(8,128)(2,1)S(1)}) custom-call(s32[1]{0:T(128)} %bitcast.1.refs_0_, bf16[96,1024]{1,0:T(8,128)(2,1)S(1)} %copy-done.30, bf16[1024,1536]{1,0:T(8,128)(2,1)S(1)} %copy-done.5, ...), custom_call_target="tpu_custom_call" | custom-call | tf_op jit(solution)/shard_map/pallas_call | solution.py:118
  79.0 2.5 %shard_map.200 = (bf16[96,1024]{1,0:T(8,128)(2,1)S(1)}, bf16[96,1600]{1,0:T(8,128)(2,1)S(1)}, bf16[96,1600]{1,0:T(8,128)(2,1)S(1)}, bf16[96,1600]{1,0:T(8,128)(2...) custom-call(s32[1]{0:T(128)} %bitcast.1.refs_0_, bf16[96,128]{1,0:T(8,128)(2,1)S(1)} %copy-done.39, ...), custom_call_target="tpu_custom_call" | custom-call | tf_op jit(solution)/shard_map/pallas_call | solution.py:118
  81.5 3.6 %collective-permute-start.19 = (bf16[96,1600]{1,0:T(8,128)(2,1)S(1)}, bf16[96,1600]{1,0:T(8,128)(2,1)S(1)}, u32[]{:S(2)}, u32[]{:S(2)}) collective-permute-start(bf16[96,1600]{1,0:T(8,128)(2,1)S(1)} %get-tuple-element.132.refs_8_), channel_id=1, source_target_pairs={{0,1},{3,2},{1,0},{2,3},{4,5},{7,6},{5,4},{6,7},{8,9},{11,10},{9,8... | collective-permute-start | bytes 921608 | tf_op jit(solution)/shard_map/ppermute | solution.py:630
  85.8 3.0 %collective-permute-start.16 = (f32[4,512]{1,0:T(4,128)S(1)}, f32[4,512]{1,0:T(4,128)S(1)}, u32[]{:S(2)}, u32[]{:S(2)}) collective-permute-start(f32[4,512]{1,0:T(4,128)S(1)} %get-tuple-element.127.refs_0_), channel_id=1, source_target_pairs={{0,2},{1,3},{2,0},{3,1},{4,6},{5,7},{6,4},{7,5},{8,10},{9,11},{10,... | collective-permute-start | bytes 24584 | tf_op jit(solution)/shard_map/ppermute | solution.py:624
  94.5 4.3 %collective-permute-start.25 = (bf16[96,1600]{1,0:T(8,128)(2,1)S(1)}, bf16[96,1600]{1,0:T(8,128)(2,1)S(1)}, u32[]{:S(2)}, u32[]{:S(2)}) collective-permute-start(bf16[96,1600]{1,0:T(8,128)(2,1)S(1)} %get-tuple-element.146.refs_5_), channel_id=1, source_target_pairs={{0,1},{3,2},{1,0},{2,3},{4,5},{7,6},{5,4},{6,7},{8,9},{11,10},{9,8... | collective-permute-start | bytes 921608 | tf_op jit(solution)/shard_map/ppermute | solution.py:630
  99.6 6.3 %shard_map.204 = (bf16[2,128,1024]{2,1,0:T(8,128)(2,1)S(1)}, f32[2,64,1024]{2,1,0:T(8,128)S(1)}, f32[2,64,384]{2,1,0:T(8,128)S(1)}, f32[64,384]{1,0:T(8,128)S(1)...) custom-call(s32[1]{0:T(128)} %bitcast.refs_0_, bf16[96,1600]{1,0:T(8,128)(2,1)S(1)} %copy-done.44, ...), custom_call_target="tpu_custom_call" | custom-call | tf_op jit(solution)/shard_map/pallas_call | solution.py:361
  106.8 2.1 %collective-permute-start.23 = (bf16[96,1600]{1,0:T(8,128)(2,1)S(1)}, bf16[96,1600]{1,0:T(8,128)(2,1)S(1)}, u32[]{:S(2)}, u32[]{:S(2)}) collective-permute-start(bf16[96,1600]{1,0:T(8,128)(2,1)S(1)} %get-tuple-element.144.refs_5_), channel_id=1, source_target_pairs={{0,1},{3,2},{1,0},{2,3},{4,5},{7,6},{5,4},{6,7},{8,9},{11,10},{9,8... | collective-permute-start | bytes 921608 | tf_op jit(solution)/shard_map/ppermute | solution.py:630
  111.8 3.8 %collective-permute-done.23.refs_2_.refs_6_ = bf16[96,1600]{1,0:T(8,128)(2,1)S(1)} collective-permute-done((bf16[96,1600]{1,0:T(8,128)(2,1)S(1)}, bf16[96,1600]{1,0:T(8,128)(2,1)S(1)}, u32[]{:S(2)}, u32[]{:S(2)}) %collective-permute-start.23) | collective-permute-done | bytes 307232 | tf_op jit(solution)/shard_map/ppermute | solution.py:630
  117.8 6.8 %collective-permute-done.30.refs_4_ = bf16[96,1600]{1,0:T(8,128)(2,1)S(1)} collective-permute-done((bf16[96,1600]{1,0:T(8,128)(2,1)S(1)}, bf16[96,1600]{1,0:T(8,128)(2,1)S(1)}, u32[]{:S(2)}, u32[]{:S(2)}) %collective-permute-start.30) | collective-permute-done | bytes 307232 | tf_op jit(solution)/shard_map/ppermute | solution.py:630
  126.1 6.4 %shard_map.209 = (bf16[2,128,1024]{2,1,0:T(8,128)(2,1)S(1)}, f32[2,64,1024]{2,1,0:T(8,128)S(1)}, f32[2,64,384]{2,1,0:T(8,128)S(1)}, f32[64,384]{1,0:T(8,128)S(1)...) custom-call(s32[1]{0:T(128)} %bitcast.refs_0_, bf16[96,1600]{1,0:T(8,128)(2,1)S(1)} %get-tuple-element.151.refs_1_, ...), custom_call_target="tpu_custom_call" | custom-call | tf_op jit(solution)/shard_map/pallas_call | solution.py:361
  135.6 6.4 %shard_map.211 = (bf16[2,128,1024]{2,1,0:T(8,128)(2,1)S(1)}, f32[2,64,1024]{2,1,0:T(8,128)S(1)}, f32[2,64,384]{2,1,0:T(8,128)S(1)}, f32[64,384]{1,0:T(8,128)S(1)...) custom-call(s32[1]{0:T(128)} %bitcast.refs_0_, bf16[96,1600]{1,0:T(8,128)(2,1)S(1)} %get-tuple-element.162.refs_1_, ...), custom_call_target="tpu_custom_call" | custom-call | tf_op jit(solution)/shard_map/pallas_call | solution.py:361
  143.9 6.1 %shard_map.215 = (bf16[2,128,1024]{2,1,0:T(8,128)(2,1)S(1)}, f32[2,64,1024]{2,1,0:T(8,128)}, f32[2,64,384]{2,1,0:T(8,128)}, f32[64,384]{1,0:T(8,128)}, f32[64,1024]{1,0:T(8,128)}) custom-call(s32[1]{0:T(128)} %bitcast.refs_0_, bf16[96,1536]{1,0:T(8,128)(2,1)S(1)} %get-tuple-element.171.refs_1_.refs_24_, bf16[96,1536]{1,0:T(8,128)(2,1)S(1)} %get-tuple-element.172.refs_2_, ...), custom_call_target="tpu_custom_call" | custom-call | flops 6000000000 | bytes 16000000 | tf_op jit(solution)/shard_map/pallas_call | solution.py:361
  153.0 3.3 %collective-permute-done.37.refs_10_ = f32[4,128]{1,0:T(4,128)S(1)} collective-permute-done((f32[4,128]{1,0:T(4,128)S(1)}, f32[4,128]{1,0:T(4,128)S(1)}, u32[]{:S(2)}, u32[]{:S(2)}) %collective-permute-start.37) | collective-permute-done | bytes 2080 | tf_op jit(solution)/shard_map/ppermute | solution.py:406
  (229 shorter events, 55.6 us)
Async XLA Ops:
  13.1 21.3 %collective-permute-start.1 = (bf16[144,2048]{1,0:T(8,128)(2,1)S(1)}, bf16[144,2048]{1,0:T(8,128)(2,1)S(1)}, u32[]{:S(2)}, u32[]{:S(2)}) collective-permute-start(bf16[144,2048]{1,0:T(8,128)(2,1)S(1)} %get-tuple-element.104.refs_2_.refs_12_.refs_4_), channel_id=1, source_target_pairs={{0,8},{4,12},{8,0},{12,4},{1,9},{5,13},{9,1},{13,5},{2,10},{6,14},... | collective-permute-start | bytes 1769480 | tf_op jit(solution)/shard_map/ppermute | solution.py:406
  16.1 14.6 %collective-permute-start.4 = (bf16[96,1600]{1,0:T(8,128)(2,1)S(1)}, bf16[96,1600]{1,0:T(8,128)(2,1)S(1)}, u32[]{:S(2)}, u32[]{:S(2)}) collective-permute-start(bf16[96,1600]{1,0:T(8,128)(2,1)S(1)} %get-tuple-element.106.refs_0_.refs_4_.refs_5_), channel_id=1, source_target_pairs={{0,1},{3,2},{4,5},{7,6},{8,9},{11,10},{12,13},{15,14},{16,17},{19,... | collective-permute-start | bytes 921608 | tf_op jit(solution)/shard_map/ppermute | solution.py:632
  19.6 15.4 %collective-permute-start = (bf16[144,2048]{1,0:T(8,128)(2,1)S(1)}, bf16[144,2048]{1,0:T(8,128)(2,1)S(1)}, u32[]{:S(2)}, u32[]{:S(2)}) collective-permute-start(bf16[144,2048]{1,0:T(8,128)(2,1)S(1)} %get-tuple-element.104.refs_2_.refs_12_.refs_4_), channel_id=1, source_target_pairs={{0,4},{4,0},{8,12},{12,8},{1,5},{5,1},{9,13},{13,9},{2,6},{6,2},{1... | collective-permute-start | bytes 1769480 | tf_op jit(solution)/shard_map/ppermute | solution.py:406
  24.8 13.1 %collective-permute-start.3 = (bf16[96,1600]{1,0:T(8,128)(2,1)S(1)}, bf16[96,1600]{1,0:T(8,128)(2,1)S(1)}, u32[]{:S(2)}, u32[]{:S(2)}) collective-permute-start(bf16[96,1600]{1,0:T(8,128)(2,1)S(1)} %shard_map.192.refs_0_.refs_7_.refs_5_), channel_id=1, source_target_pairs={{0,1},{3,2},{4,5},{7,6},{8,9},{11,10},{12,13},{15,14},{16,17},{19,... | collective-permute-start | bytes 921608 | tf_op jit(solution)/shard_map/ppermute | solution.py:632
  32.3 12.9 %collective-permute-start.5 = (bf16[96,1600]{1,0:T(8,128)(2,1)S(1)}, bf16[96,1600]{1,0:T(8,128)(2,1)S(1)}, u32[]{:S(2)}, u32[]{:S(2)}) collective-permute-start(bf16[96,1600]{1,0:T(8,128)(2,1)S(1)} %get-tuple-element.107.refs_7_.refs_4_), channel_id=1, source_target_pairs={{0,1},{3,2},{4,5},{7,6},{8,9},{11,10},{12,13},{15,14},{16,17},{19,... | collective-permute-start | bytes 921608 | tf_op jit(solution)/shard_map/ppermute | solution.py:632
  33.7 11.5 %collective-permute-start.6 = (bf16[96,1600]{1,0:T(8,128)(2,1)S(1)}, bf16[96,1600]{1,0:T(8,128)(2,1)S(1)}, u32[]{:S(2)}, u32[]{:S(2)}) collective-permute-start(bf16[96,1600]{1,0:T(8,128)(2,1)S(1)} %get-tuple-element.109.refs_6_), channel_id=1, source_target_pairs={{1,2},{2,1},{5,6},{6,5},{9,10},{10,9},{13,14},{14,13},{17,18},{18,... | collective-permute-start | bytes 921608 | tf_op jit(solution)/shard_map/ppermute | solution.py:635
  39.5 13.5 %collective-permute-start.9 = (bf16[96,1600]{1,0:T(8,128)(2,1)S(1)}, bf16[96,1600]{1,0:T(8,128)(2,1)S(1)}, u32[]{:S(2)}, u32[]{:S(2)}) collective-permute-start(bf16[96,1600]{1,0:T(8,128)(2,1)S(1)} %get-tuple-element.110.refs_8_.refs_5_), channel_id=1, source_target_pairs={{0,1},{3,2},{4,5},{7,6},{8,9},{11,10},{12,13},{15,14},{16,17},{19,... | collective-permute-start | bytes 921608 | tf_op jit(solution)/shard_map/ppermute | solution.py:632
  46.0 13.9 %collective-permute-start.7 = (bf16[96,1600]{1,0:T(8,128)(2,1)S(1)}, bf16[96,1600]{1,0:T(8,128)(2,1)S(1)}, u32[]{:S(2)}, u32[]{:S(2)}) collective-permute-start(bf16[96,1600]{1,0:T(8,128)(2,1)S(1)} %get-tuple-element.112.refs_9_), channel_id=1, source_target_pairs={{0,1},{3,2},{1,0},{2,3},{4,5},{7,6},{5,4},{6,7},{8,9},{11,10},{9,8... | collective-permute-start | bytes 921608 | tf_op jit(solution)/shard_map/ppermute | solution.py:630
  46.1 13.8 %collective-permute-start.8 = (bf16[96,1600]{1,0:T(8,128)(2,1)S(1)}, bf16[96,1600]{1,0:T(8,128)(2,1)S(1)}, u32[]{:S(2)}, u32[]{:S(2)}) collective-permute-start(bf16[96,1600]{1,0:T(8,128)(2,1)S(1)} %get-tuple-element.113.refs_7_), channel_id=1, source_target_pairs={{1,2},{2,1},{5,6},{6,5},{9,10},{10,9},{13,14},{14,13},{17,18},{18,... | collective-permute-start | bytes 921608 | tf_op jit(solution)/shard_map/ppermute | solution.py:635
  55.5 15.3 %collective-permute-start.11 = (bf16[96,1600]{1,0:T(8,128)(2,1)}, bf16[96,1600]{1,0:T(8,128)(2,1)}, u32[]{:S(2)}, u32[]{:S(2)}) collective-permute-start(bf16[96,1600]{1,0:T(8,128)(2,1)} %get-tuple-element.118.refs_8_), channel_id=1, source_target_pairs={{0,1},{3,2},{1,0},{2,3},{4,5},{7,6},{5,4},{6,7},{8,9},{11,10},{9,8... | collective-permute-start | bytes 921608 | tf_op jit(solution)/shard_map/ppermute | solution.py:630
  58.0 12.8 %collective-permute-start.12 = (bf16[96,1600]{1,0:T(8,128)(2,1)}, bf16[96,1600]{1,0:T(8,128)(2,1)}, u32[]{:S(2)}, u32[]{:S(2)}) collective-permute-start(bf16[96,1600]{1,0:T(8,128)(2,1)} %get-tuple-element.119.refs_6_), channel_id=1, source_target_pairs={{1,2},{2,1},{5,6},{6,5},{9,10},{10,9},{13,14},{14,13},{17,18},{18,... | collective-permute-start | bytes 921608 | tf_op jit(solution)/shard_map/ppermute | solution.py:635
  64.2 14.7 %collective-permute-start.13 = (bf16[96,1600]{1,0:T(8,128)(2,1)}, bf16[96,1600]{1,0:T(8,128)(2,1)}, u32[]{:S(2)}, u32[]{:S(2)}) collective-permute-start(bf16[96,1600]{1,0:T(8,128)(2,1)} %get-tuple-element.122.refs_9_), channel_id=1, source_target_pairs={{0,1},{3,2},{1,0},{2,3},{4,5},{7,6},{5,4},{6,7},{8,9},{11,10},{9,8... | collective-permute-start | bytes 921608 | tf_op jit(solution)/shard_map/ppermute | solution.py:630
  66.7 12.2 %collective-permute-start.14 = (bf16[96,1600]{1,0:T(8,128)(2,1)}, bf16[96,1600]{1,0:T(8,128)(2,1)}, u32[]{:S(2)}, u32[]{:S(2)}) collective-permute-start(bf16[96,1600]{1,0:T(8,128)(2,1)} %get-tuple-element.123.refs_7_), channel_id=1, source_target_pairs={{1,2},{2,1},{5,6},{6,5},{9,10},{10,9},{13,14},{14,13},{17,18},{18,... | collective-permute-start | bytes 921608 | tf_op jit(solution)/shard_map/ppermute | solution.py:635
  81.5 12.1 %collective-permute-start.19 = (bf16[96,1600]{1,0:T(8,128)(2,1)S(1)}, bf16[96,1600]{1,0:T(8,128)(2,1)S(1)}, u32[]{:S(2)}, u32[]{:S(2)}) collective-permute-start(bf16[96,1600]{1,0:T(8,128)(2,1)S(1)} %get-tuple-element.132.refs_8_), channel_id=1, source_target_pairs={{0,1},{3,2},{1,0},{2,3},{4,5},{7,6},{5,4},{6,7},{8,9},{11,10},{9,8... | collective-permute-start | bytes 921608 | tf_op jit(solution)/shard_map/ppermute | solution.py:630
  85.8 13.6 %collective-permute-start.16 = (f32[4,512]{1,0:T(4,128)S(1)}, f32[4,512]{1,0:T(4,128)S(1)}, u32[]{:S(2)}, u32[]{:S(2)}) collective-permute-start(f32[4,512]{1,0:T(4,128)S(1)} %get-tuple-element.127.refs_0_), channel_id=1, source_target_pairs={{0,2},{1,3},{2,0},{3,1},{4,6},{5,7},{6,4},{7,5},{8,10},{9,11},{10,... | collective-permute-start | bytes 24584 | tf_op jit(solution)/shard_map/ppermute | solution.py:624
  89.9 16.0 %collective-permute-start.21 = (bf16[96,1600]{1,0:T(8,128)(2,1)S(1)}, bf16[96,1600]{1,0:T(8,128)(2,1)S(1)}, u32[]{:S(2)}, u32[]{:S(2)}) collective-permute-start(bf16[96,1600]{1,0:T(8,128)(2,1)S(1)} %get-tuple-element.140.refs_9_), channel_id=1, source_target_pairs={{0,1},{3,2},{1,0},{2,3},{4,5},{7,6},{5,4},{6,7},{8,9},{11,10},{9,8... | collective-permute-start | bytes 921608 | tf_op jit(solution)/shard_map/ppermute | solution.py:630
  91.8 14.0 %collective-permute-start.22 = (bf16[96,1600]{1,0:T(8,128)(2,1)S(1)}, bf16[96,1600]{1,0:T(8,128)(2,1)S(1)}, u32[]{:S(2)}, u32[]{:S(2)}) collective-permute-start(bf16[96,1600]{1,0:T(8,128)(2,1)S(1)} %get-tuple-element.141.refs_7_), channel_id=1, source_target_pairs={{1,2},{2,1},{5,6},{6,5},{9,10},{10,9},{13,14},{14,13},{17,18},{18,... | collective-permute-start | bytes 921608 | tf_op jit(solution)/shard_map/ppermute | solution.py:635
  94.5 15.1 %collective-permute-start.25 = (bf16[96,1600]{1,0:T(8,128)(2,1)S(1)}, bf16[96,1600]{1,0:T(8,128)(2,1)S(1)}, u32[]{:S(2)}, u32[]{:S(2)}) collective-permute-start(bf16[96,1600]{1,0:T(8,128)(2,1)S(1)} %get-tuple-element.146.refs_5_), channel_id=1, source_target_pairs={{0,1},{3,2},{1,0},{2,3},{4,5},{7,6},{5,4},{6,7},{8,9},{11,10},{9,8... | collective-permute-start | bytes 921608 | tf_op jit(solution)/shard_map/ppermute | solution.py:630
  110.5 14.1 %collective-permute-start.30 = (bf16[96,1600]{1,0:T(8,128)(2,1)S(1)}, bf16[96,1600]{1,0:T(8,128)(2,1)S(1)}, u32[]{:S(2)}, u32[]{:S(2)}) collective-permute-start(bf16[96,1600]{1,0:T(8,128)(2,1)S(1)} %get-tuple-element.158.refs_3_), channel_id=1, source_target_pairs={{1,0},{2,3},{5,4},{6,7},{9,8},{10,11},{13,12},{14,15},{17,16},{18,... | collective-permute-start | bytes 921608 | tf_op jit(solution)/shard_map/ppermute | solution.py:630
  115.8 16.7 %collective-permute-start.27 = (bf16[96,1600]{1,0:T(8,128)(2,1)S(1)}, bf16[96,1600]{1,0:T(8,128)(2,1)S(1)}, u32[]{:S(2)}, u32[]{:S(2)}) collective-permute-start(bf16[96,1600]{1,0:T(8,128)(2,1)S(1)} %get-tuple-element.149.refs_5_.refs_1_), channel_id=1, source_target_pairs={{1,2},{2,1},{5,6},{6,5},{9,10},{10,9},{13,14},{14,13},{17,18},{18,... | collective-permute-start | bytes 921608 | tf_op jit(solution)/shard_map/ppermute | solution.py:635
  116.5 17.1 %collective-permute-start.28 = (bf16[96,1600]{1,0:T(8,128)(2,1)S(1)}, bf16[96,1600]{1,0:T(8,128)(2,1)S(1)}, u32[]{:S(2)}, u32[]{:S(2)}) collective-permute-start(bf16[96,1600]{1,0:T(8,128)(2,1)S(1)} %get-tuple-element.150.refs_3_), channel_id=1, source_target_pairs={{1,0},{2,3},{5,4},{6,7},{9,8},{10,11},{13,12},{14,15},{17,16},{18,... | collective-permute-start | bytes 921608 | tf_op jit(solution)/shard_map/ppermute | solution.py:630
  124.7 17.3 %collective-permute-start.31 = (bf16[96,1600]{1,0:T(8,128)(2,1)S(1)}, bf16[96,1600]{1,0:T(8,128)(2,1)S(1)}, u32[]{:S(2)}, u32[]{:S(2)}) collective-permute-start(bf16[96,1600]{1,0:T(8,128)(2,1)S(1)} %get-tuple-element.159.refs_20_.refs_1_), channel_id=1, source_target_pairs={{1,0},{2,3},{5,4},{6,7},{9,8},{10,11},{13,12},{14,15},{17,16},{18,... | collective-permute-start | bytes 921608 | tf_op jit(solution)/shard_map/ppermute | solution.py:630
  135.0 16.8 %collective-permute-start.34 = (bf16[2,128,1024]{2,1,0:T(8,128)(2,1)S(1)}, bf16[2,128,1024]{2,1,0:T(8,128)(2,1)S(1)}, u32[]{:S(2)}, u32[]{:S(2)}) collective-permute-start(bf16[2,128,1024]{2,1,0:T(8,128)(2,1)S(1)} %get-tuple-element.187), channel_id=1, source_target_pairs={{0,8},{4,12},{8,0},{12,4},{1,9},{5,13},{9,1},{13,5},{2,10},{6,14},... | collective-permute-start | bytes 1572872 | tf_op jit(solution)/shard_map/ppermute | solution.py:406
  142.0 14.4 %collective-permute-start.35 = (bf16[2,128,1024]{2,1,0:T(8,128)(2,1)S(1)}, bf16[2,128,1024]{2,1,0:T(8,128)(2,1)S(1)}, u32[]{:S(2)}, u32[]{:S(2)}) collective-permute-start(bf16[2,128,1024]{2,1,0:T(8,128)(2,1)S(1)} %get-tuple-element.188), channel_id=1, source_target_pairs={{0,12},{4,8},{8,4},{12,0},{1,13},{5,9},{9,5},{13,1},{2,14},{6,10},... | collective-permute-start | bytes 1572872 | tf_op jit(solution)/shard_map/ppermute | solution.py:406
  (77 other events, 730.5 us)

commit v5 on v4

--- a/solution.py
+++ b/solution.py
@@ -282,7 +282,7 @@
     sources = len(picks)
     cap = rows // sources
     width = hidden_width if share % 128 else share
-    tile = min(256, features)
+    tile = min(512, features)
     tokens = picks[0].shape[1]
 
     def fixed(value):

time: 160 us -> 158 us (0.988)
  Pallas kernels: 60.3 us -> 56.1 us
  waiting for transfers between devices: 25 us -> 28.2 us
    pallas_call x4, Pallas kernels: 25.1 us -> 20.9 us  [run_back(): pl.pallas_call(body, grid=(features // tile,), in_specs=specs, out_specs=...]
    ppermute x12, waiting for transfers between devices: 13.8 us -> 15.7 us  [shards(): near[t] = lax.ppermute(carried[t], 'dp', way)]
  transfers between devices with their start and end apart: 39 -> 39, of which waited for: 9 -> 9; matrix products, arithmetic and copies ran while one was open for 1% -> 1% of each run, Pallas kernels for 32% -> 29%
where the time goes in v5:
time: 158 us; the launch traced here: 157 us
  Pallas kernels  56.1 us (36%)
  starting transfers between devices  55.5 us (35%)
  waiting for transfers between devices  28.2 us (18%)
  local copies, waits for them, and re-layouts  12.6 us (8%)
  between operations  1.92 us (1%)
    ppermute x12, starting transfers between devices, shards(): near[t] = lax.ppermute(carried[t], 'dp', way)  22.5 us
    pallas_call x4, Pallas kernels, run_back(): pl.pallas_call(body, grid=(features // tile,), in_specs=specs, out_specs=...  20.9 us
    pallas_call x21, Pallas kernels, call(): pl.pallas_call(kernel, grid=(1,) if piped else (), in_specs=[smem if a.dt...  18.5 us
    pallas_call x3, Pallas kernels, dequantize(): pl.pallas_call(functools.partial(dequantize_kernel, field=field), grid=(f...  16.7 us
    ppermute x12, waiting for transfers between devices, shards(): near[t] = lax.ppermute(carried[t], 'dp', way)  15.7 us
    ppermute x4, starting transfers between devices, shards(): near[t] = lax.ppermute(new, 'dp', INWARD)  12 us
    unnamed x124, local copies, waits for them, and re-layouts  11.4 us
    ppermute x12, starting transfers between devices, shards(): far[t] = lax.ppermute(inner[t], 'dp', MIDDLE)  9.52 us
  transfers between devices with their start and end apart: 39, of which 9 were waited for; matrix products, arithmetic and copies ran while one was open for 1% of the time, Pallas kernels for 29%

profile of v5, /device:TPU:0, one launch (start us, length us, event | category | flops | bytes accessed | tf_op | source)
XLA Modules:
  0.0 156.6 jit_solution(3345853373696164725)
XLA Ops:
  2.4 8.0 %shard_map.189.refs_3_.refs_10_.refs_14_ = bf16[1024,1536]{1,0:T(8,128)(2,1)} custom-call(s32[1024,1536]{1,0:T(8,128)} %bitcast.47, f32[3,24,1024]{2,1,0:T(8,128)} %bitcast.78, f32[8,128]{1,0:T(8,128)} %constant.23.clone.level_ref, bf16[24,1536]{1,0:T(8,128)(2,1)} %constant.24.clone.spread_ref), custom_call_target="tpu_custom_call" | custom-call | tf_op jit(solution)/shard_map/pallas_call | solution.py:88
  13.1 3.0 %collective-permute-start.1 = (bf16[144,2048]{1,0:T(8,128)(2,1)S(1)}, bf16[144,2048]{1,0:T(8,128)(2,1)S(1)}, u32[]{:S(2)}, u32[]{:S(2)}) collective-permute-start(bf16[144,2048]{1,0:T(8,128)(2,1)S(1)} %get-tuple-element.104.refs_2_.refs_12_.refs_4_), channel_id=1, source_target_pairs={{0,8},{4,12},{8,0},{12,4},{1,9},{5,13},{9,1},{13,5},{2,10},{6,14},... | collective-permute-start | bytes 1769480 | tf_op jit(solution)/shard_map/ppermute | solution.py:406
  16.1 3.5 %collective-permute-start.4 = (bf16[96,1600]{1,0:T(8,128)(2,1)S(1)}, bf16[96,1600]{1,0:T(8,128)(2,1)S(1)}, u32[]{:S(2)}, u32[]{:S(2)}) collective-permute-start(bf16[96,1600]{1,0:T(8,128)(2,1)S(1)} %get-tuple-element.106.refs_0_.refs_4_.refs_5_), channel_id=1, source_target_pairs={{0,1},{3,2},{4,5},{7,6},{8,9},{11,10},{12,13},{15,14},{16,17},{19,... | collective-permute-start | bytes 921608 | tf_op jit(solution)/shard_map/ppermute | solution.py:632
  19.7 4.4 %shard_map.191.refs_2_.refs_11_.refs_15_ = bf16[1024,1536]{1,0:T(8,128)(2,1)S(1)} custom-call(s32[1024,1536]{1,0:T(8,128)S(1)} %bitcast.48, f32[3,24,1024]{2,1,0:T(8,128)S(1)} %bitcast.79, f32[8,128]{1,0:T(8,128)S(1)} %copy-done.50, bf16[24,1536]{1,0:T(8,128)(2,1)S(1)} %copy-done.34, bf16[96,1600]{1,0:T(8,128)(2,1)S(1)} %get-tuple-element.106.refs_0_.refs_4_.refs_5_), custom_call_target="tpu_custom_call" | custom-call | tf_op jit(solution)/shard_map/pallas_call | solution.py:88
  26.3 4.3 %shard_map.193.refs_3_.refs_12_.refs_16_ = bf16[1024,1536]{1,0:T(8,128)(2,1)S(1)} custom-call(s32[1024,1536]{1,0:T(8,128)S(1)} %bitcast.49, f32[3,24,1024]{2,1,0:T(8,128)S(1)} %bitcast.80, f32[8,128]{1,0:T(8,128)S(1)} %copy-done.50, bf16[24,1536]{1,0:T(8,128)(2,1)S(1)} %copy-done.34, bf16[96,1600]{1,0:T(8,128)(2,1)S(1)} %shard_map.192.refs_0_.refs_7_.refs_5_), custom_call_target="tpu_custom_call" | custom-call | tf_op jit(solution)/shard_map/pallas_call | solution.py:88
  39.5 5.6 %collective-permute-start.9 = (bf16[96,1600]{1,0:T(8,128)(2,1)S(1)}, bf16[96,1600]{1,0:T(8,128)(2,1)S(1)}, u32[]{:S(2)}, u32[]{:S(2)}) collective-permute-start(bf16[96,1600]{1,0:T(8,128)(2,1)S(1)} %get-tuple-element.110.refs_8_.refs_5_), channel_id=1, source_target_pairs={{0,1},{3,2},{4,5},{7,6},{8,9},{11,10},{12,13},{15,14},{16,17},{19,... | collective-permute-start | bytes 921608 | tf_op jit(solution)/shard_map/ppermute | solution.py:632
  46.8 6.3 %collective-permute-done.9.refs_6_ = bf16[96,1600]{1,0:T(8,128)(2,1)S(1)} collective-permute-done((bf16[96,1600]{1,0:T(8,128)(2,1)S(1)}, bf16[96,1600]{1,0:T(8,128)(2,1)S(1)}, u32[]{:S(2)}, u32[]{:S(2)}) %collective-permute-start.9) | collective-permute-done | bytes 307232 | tf_op jit(solution)/shard_map/ppermute | solution.py:632
  55.5 2.5 %collective-permute-start.11 = (bf16[96,1600]{1,0:T(8,128)(2,1)}, bf16[96,1600]{1,0:T(8,128)(2,1)}, u32[]{:S(2)}, u32[]{:S(2)}) collective-permute-start(bf16[96,1600]{1,0:T(8,128)(2,1)} %get-tuple-element.118.refs_8_), channel_id=1, source_target_pairs={{0,1},{3,2},{1,0},{2,3},{4,5},{7,6},{5,4},{6,7},{8,9},{11,10},{9,8... | collective-permute-start | bytes 921608 | tf_op jit(solution)/shard_map/ppermute | solution.py:630
  59.9 2.1 %shard_map.198 = (bf16[96,1024]{1,0:T(8,128)(2,1)S(1)}, bf16[96,1600]{1,0:T(8,128)(2,1)S(1)}, bf16[96,1600]{1,0:T(8,128)(2,1)}, bf16[96,1600]{1,0:T(8,128)(2,1)}...) custom-call(s32[1]{0:T(128)} %bitcast.1.refs_0_, bf16[96,128]{1,0:T(8,128)(2,1)S(1)} %fusion.3.refs_1_.refs_15_, ...), custom_call_target="tpu_custom_call" | custom-call | tf_op jit(solution)/shard_map/pallas_call | solution.py:118
  64.2 2.5 %collective-permute-start.13 = (bf16[96,1600]{1,0:T(8,128)(2,1)}, bf16[96,1600]{1,0:T(8,128)(2,1)}, u32[]{:S(2)}, u32[]{:S(2)}) collective-permute-start(bf16[96,1600]{1,0:T(8,128)(2,1)} %get-tuple-element.122.refs_9_), channel_id=1, source_target_pairs={{0,1},{3,2},{1,0},{2,3},{4,5},{7,6},{5,4},{6,7},{8,9},{11,10},{9,8... | collective-permute-start | bytes 921608 | tf_op jit(solution)/shard_map/ppermute | solution.py:630
  68.6 2.1 %collective-permute-start.15 = (f32[4,512]{1,0:T(4,128)S(1)}, f32[4,512]{1,0:T(4,128)S(1)}, u32[]{:S(2)}, u32[]{:S(2)}) collective-permute-start(f32[4,512]{1,0:T(4,128)S(1)} %get-tuple-element.124.refs_11_), channel_id=1, source_target_pairs={{0,1},{1,0},{2,3},{3,2},{4,5},{5,4},{6,7},{7,6},{8,9},{9,8},{10,11... | collective-permute-start | bytes 24584 | tf_op jit(solution)/shard_map/ppermute | solution.py:621
  75.5 2.3 %shard_map.199 = (bf16[96,1600]{1,0:T(8,128)(2,1)S(1)}, bf16[96,1600]{1,0:T(8,128)(2,1)S(1)}, bf16[96,1600]{1,0:T(8,128)(2,1)S(1)}, bf16[96,1600]{1,0:T(8,128)(2,1)S(1)}) custom-call(s32[1]{0:T(128)} %bitcast.1.refs_0_, bf16[96,1024]{1,0:T(8,128)(2,1)S(1)} %copy-done.30, bf16[1024,1536]{1,0:T(8,128)(2,1)S(1)} %copy-done.5, ...), custom_call_target="tpu_custom_call" | custom-call | tf_op jit(solution)/shard_map/pallas_call | solution.py:118
  79.0 2.5 %shard_map.200 = (bf16[96,1024]{1,0:T(8,128)(2,1)S(1)}, bf16[96,1600]{1,0:T(8,128)(2,1)S(1)}, bf16[96,1600]{1,0:T(8,128)(2,1)S(1)}, bf16[96,1600]{1,0:T(8,128)(2...) custom-call(s32[1]{0:T(128)} %bitcast.1.refs_0_, bf16[96,128]{1,0:T(8,128)(2,1)S(1)} %copy-done.39, ...), custom_call_target="tpu_custom_call" | custom-call | tf_op jit(solution)/shard_map/pallas_call | solution.py:118
  81.5 3.6 %collective-permute-start.19 = (bf16[96,1600]{1,0:T(8,128)(2,1)S(1)}, bf16[96,1600]{1,0:T(8,128)(2,1)S(1)}, u32[]{:S(2)}, u32[]{:S(2)}) collective-permute-start(bf16[96,1600]{1,0:T(8,128)(2,1)S(1)} %get-tuple-element.132.refs_8_), channel_id=1, source_target_pairs={{0,1},{3,2},{1,0},{2,3},{4,5},{7,6},{5,4},{6,7},{8,9},{11,10},{9,8... | collective-permute-start | bytes 921608 | tf_op jit(solution)/shard_map/ppermute | solution.py:630
  85.8 3.0 %collective-permute-start.16 = (f32[4,512]{1,0:T(4,128)S(1)}, f32[4,512]{1,0:T(4,128)S(1)}, u32[]{:S(2)}, u32[]{:S(2)}) collective-permute-start(f32[4,512]{1,0:T(4,128)S(1)} %get-tuple-element.127.refs_0_), channel_id=1, source_target_pairs={{0,2},{1,3},{2,0},{3,1},{4,6},{5,7},{6,4},{7,5},{8,10},{9,11},{10,... | collective-permute-start | bytes 24584 | tf_op jit(solution)/shard_map/ppermute | solution.py:624
  94.5 4.3 %collective-permute-start.25 = (bf16[96,1600]{1,0:T(8,128)(2,1)S(1)}, bf16[96,1600]{1,0:T(8,128)(2,1)S(1)}, u32[]{:S(2)}, u32[]{:S(2)}) collective-permute-start(bf16[96,1600]{1,0:T(8,128)(2,1)S(1)} %get-tuple-element.146.refs_5_), channel_id=1, source_target_pairs={{0,1},{3,2},{1,0},{2,3},{4,5},{7,6},{5,4},{6,7},{8,9},{11,10},{9,8... | collective-permute-start | bytes 921608 | tf_op jit(solution)/shard_map/ppermute | solution.py:630
  99.6 5.2 %shard_map.204 = (bf16[2,128,1024]{2,1,0:T(8,128)(2,1)S(1)}, f32[2,64,1024]{2,1,0:T(8,128)S(1)}, f32[2,64,384]{2,1,0:T(8,128)S(1)}, f32[64,384]{1,0:T(8,128)S(1)...) custom-call(s32[1]{0:T(128)} %bitcast.refs_0_, bf16[96,1600]{1,0:T(8,128)(2,1)S(1)} %copy-done.44, ...), custom_call_target="tpu_custom_call" | custom-call | tf_op jit(solution)/shard_map/pallas_call | solution.py:361
  110.7 2.7 %collective-permute-done.23.refs_2_.refs_6_ = bf16[96,1600]{1,0:T(8,128)(2,1)S(1)} collective-permute-done((bf16[96,1600]{1,0:T(8,128)(2,1)S(1)}, bf16[96,1600]{1,0:T(8,128)(2,1)S(1)}, u32[]{:S(2)}, u32[]{:S(2)}) %collective-permute-start.23) | collective-permute-done | bytes 307232 | tf_op jit(solution)/shard_map/ppermute | solution.py:630
  115.6 7.3 %collective-permute-done.30.refs_4_ = bf16[96,1600]{1,0:T(8,128)(2,1)S(1)} collective-permute-done((bf16[96,1600]{1,0:T(8,128)(2,1)S(1)}, bf16[96,1600]{1,0:T(8,128)(2,1)S(1)}, u32[]{:S(2)}, u32[]{:S(2)}) %collective-permute-start.30) | collective-permute-done | bytes 307232 | tf_op jit(solution)/shard_map/ppermute | solution.py:630
  124.4 5.3 %shard_map.209 = (bf16[2,128,1024]{2,1,0:T(8,128)(2,1)S(1)}, f32[2,64,1024]{2,1,0:T(8,128)S(1)}, f32[2,64,384]{2,1,0:T(8,128)S(1)}, f32[64,384]{1,0:T(8,128)S(1)...) custom-call(s32[1]{0:T(128)} %bitcast.refs_0_, bf16[96,1600]{1,0:T(8,128)(2,1)S(1)} %get-tuple-element.151.refs_1_, ...), custom_call_target="tpu_custom_call" | custom-call | tf_op jit(solution)/shard_map/pallas_call | solution.py:361
  129.8 2.5 %collective-permute-done.28.refs_4_ = bf16[96,1600]{1,0:T(8,128)(2,1)S(1)} collective-permute-done((bf16[96,1600]{1,0:T(8,128)(2,1)S(1)}, bf16[96,1600]{1,0:T(8,128)(2,1)S(1)}, u32[]{:S(2)}, u32[]{:S(2)}) %collective-permute-start.28) | collective-permute-done | bytes 307232 | tf_op jit(solution)/shard_map/ppermute | solution.py:630
  134.2 5.3 %shard_map.211 = (bf16[2,128,1024]{2,1,0:T(8,128)(2,1)S(1)}, f32[2,64,1024]{2,1,0:T(8,128)S(1)}, f32[2,64,384]{2,1,0:T(8,128)S(1)}, f32[64,384]{1,0:T(8,128)S(1)...) custom-call(s32[1]{0:T(128)} %bitcast.refs_0_, bf16[96,1600]{1,0:T(8,128)(2,1)S(1)} %get-tuple-element.162.refs_1_, ...), custom_call_target="tpu_custom_call" | custom-call | tf_op jit(solution)/shard_map/pallas_call | solution.py:361
  142.5 5.1 %shard_map.215 = (bf16[2,128,1024]{2,1,0:T(8,128)(2,1)S(1)}, f32[2,64,1024]{2,1,0:T(8,128)}, f32[2,64,384]{2,1,0:T(8,128)}, f32[64,384]{1,0:T(8,128)}, f32[64,1024]{1,0:T(8,128)}) custom-call(s32[1]{0:T(128)} %bitcast.refs_0_, bf16[96,1536]{1,0:T(8,128)(2,1)S(1)} %get-tuple-element.171.refs_1_.refs_24_, bf16[96,1536]{1,0:T(8,128)(2,1)S(1)} %get-tuple-element.172.refs_2_, ...), custom_call_target="tpu_custom_call" | custom-call | flops 6000000000 | bytes 16000000 | tf_op jit(solution)/shard_map/pallas_call | solution.py:361
  149.7 4.5 %collective-permute-done.37.refs_10_ = f32[4,128]{1,0:T(4,128)S(1)} collective-permute-done((f32[4,128]{1,0:T(4,128)S(1)}, f32[4,128]{1,0:T(4,128)S(1)}, u32[]{:S(2)}, u32[]{:S(2)}) %collective-permute-start.37) | collective-permute-done | bytes 2080 | tf_op jit(solution)/shard_map/ppermute | solution.py:406
  (229 shorter events, 56.6 us)
Async XLA Ops:
  13.1 21.3 %collective-permute-start.1 = (bf16[144,2048]{1,0:T(8,128)(2,1)S(1)}, bf16[144,2048]{1,0:T(8,128)(2,1)S(1)}, u32[]{:S(2)}, u32[]{:S(2)}) collective-permute-start(bf16[144,2048]{1,0:T(8,128)(2,1)S(1)} %get-tuple-element.104.refs_2_.refs_12_.refs_4_), channel_id=1, source_target_pairs={{0,8},{4,12},{8,0},{12,4},{1,9},{5,13},{9,1},{13,5},{2,10},{6,14},... | collective-permute-start | bytes 1769480 | tf_op jit(solution)/shard_map/ppermute | solution.py:406
  16.1 14.6 %collective-permute-start.4 = (bf16[96,1600]{1,0:T(8,128)(2,1)S(1)}, bf16[96,1600]{1,0:T(8,128)(2,1)S(1)}, u32[]{:S(2)}, u32[]{:S(2)}) collective-permute-start(bf16[96,1600]{1,0:T(8,128)(2,1)S(1)} %get-tuple-element.106.refs_0_.refs_4_.refs_5_), channel_id=1, source_target_pairs={{0,1},{3,2},{4,5},{7,6},{8,9},{11,10},{12,13},{15,14},{16,17},{19,... | collective-permute-start | bytes 921608 | tf_op jit(solution)/shard_map/ppermute | solution.py:632
  19.6 15.4 %collective-permute-start = (bf16[144,2048]{1,0:T(8,128)(2,1)S(1)}, bf16[144,2048]{1,0:T(8,128)(2,1)S(1)}, u32[]{:S(2)}, u32[]{:S(2)}) collective-permute-start(bf16[144,2048]{1,0:T(8,128)(2,1)S(1)} %get-tuple-element.104.refs_2_.refs_12_.refs_4_), channel_id=1, source_target_pairs={{0,4},{4,0},{8,12},{12,8},{1,5},{5,1},{9,13},{13,9},{2,6},{6,2},{1... | collective-permute-start | bytes 1769480 | tf_op jit(solution)/shard_map/ppermute | solution.py:406
  24.8 13.1 %collective-permute-start.3 = (bf16[96,1600]{1,0:T(8,128)(2,1)S(1)}, bf16[96,1600]{1,0:T(8,128)(2,1)S(1)}, u32[]{:S(2)}, u32[]{:S(2)}) collective-permute-start(bf16[96,1600]{1,0:T(8,128)(2,1)S(1)} %shard_map.192.refs_0_.refs_7_.refs_5_), channel_id=1, source_target_pairs={{0,1},{3,2},{4,5},{7,6},{8,9},{11,10},{12,13},{15,14},{16,17},{19,... | collective-permute-start | bytes 921608 | tf_op jit(solution)/shard_map/ppermute | solution.py:632
  32.3 12.9 %collective-permute-start.5 = (bf16[96,1600]{1,0:T(8,128)(2,1)S(1)}, bf16[96,1600]{1,0:T(8,128)(2,1)S(1)}, u32[]{:S(2)}, u32[]{:S(2)}) collective-permute-start(bf16[96,1600]{1,0:T(8,128)(2,1)S(1)} %get-tuple-element.107.refs_7_.refs_4_), channel_id=1, source_target_pairs={{0,1},{3,2},{4,5},{7,6},{8,9},{11,10},{12,13},{15,14},{16,17},{19,... | collective-permute-start | bytes 921608 | tf_op jit(solution)/shard_map/ppermute | solution.py:632
  33.7 11.5 %collective-permute-start.6 = (bf16[96,1600]{1,0:T(8,128)(2,1)S(1)}, bf16[96,1600]{1,0:T(8,128)(2,1)S(1)}, u32[]{:S(2)}, u32[]{:S(2)}) collective-permute-start(bf16[96,1600]{1,0:T(8,128)(2,1)S(1)} %get-tuple-element.109.refs_6_), channel_id=1, source_target_pairs={{1,2},{2,1},{5,6},{6,5},{9,10},{10,9},{13,14},{14,13},{17,18},{18,... | collective-permute-start | bytes 921608 | tf_op jit(solution)/shard_map/ppermute | solution.py:635
  39.5 13.5 %collective-permute-start.9 = (bf16[96,1600]{1,0:T(8,128)(2,1)S(1)}, bf16[96,1600]{1,0:T(8,128)(2,1)S(1)}, u32[]{:S(2)}, u32[]{:S(2)}) collective-permute-start(bf16[96,1600]{1,0:T(8,128)(2,1)S(1)} %get-tuple-element.110.refs_8_.refs_5_), channel_id=1, source_target_pairs={{0,1},{3,2},{4,5},{7,6},{8,9},{11,10},{12,13},{15,14},{16,17},{19,... | collective-permute-start | bytes 921608 | tf_op jit(solution)/shard_map/ppermute | solution.py:632
  46.0 13.9 %collective-permute-start.7 = (bf16[96,1600]{1,0:T(8,128)(2,1)S(1)}, bf16[96,1600]{1,0:T(8,128)(2,1)S(1)}, u32[]{:S(2)}, u32[]{:S(2)}) collective-permute-start(bf16[96,1600]{1,0:T(8,128)(2,1)S(1)} %get-tuple-element.112.refs_9_), channel_id=1, source_target_pairs={{0,1},{3,2},{1,0},{2,3},{4,5},{7,6},{5,4},{6,7},{8,9},{11,10},{9,8... | collective-permute-start | bytes 921608 | tf_op jit(solution)/shard_map/ppermute | solution.py:630
  46.1 13.8 %collective-permute-start.8 = (bf16[96,1600]{1,0:T(8,128)(2,1)S(1)}, bf16[96,1600]{1,0:T(8,128)(2,1)S(1)}, u32[]{:S(2)}, u32[]{:S(2)}) collective-permute-start(bf16[96,1600]{1,0:T(8,128)(2,1)S(1)} %get-tuple-element.113.refs_7_), channel_id=1, source_target_pairs={{1,2},{2,1},{5,6},{6,5},{9,10},{10,9},{13,14},{14,13},{17,18},{18,... | collective-permute-start | bytes 921608 | tf_op jit(solution)/shard_map/ppermute | solution.py:635
  55.5 15.3 %collective-permute-start.11 = (bf16[96,1600]{1,0:T(8,128)(2,1)}, bf16[96,1600]{1,0:T(8,128)(2,1)}, u32[]{:S(2)}, u32[]{:S(2)}) collective-permute-start(bf16[96,1600]{1,0:T(8,128)(2,1)} %get-tuple-element.118.refs_8_), channel_id=1, source_target_pairs={{0,1},{3,2},{1,0},{2,3},{4,5},{7,6},{5,4},{6,7},{8,9},{11,10},{9,8... | collective-permute-start | bytes 921608 | tf_op jit(solution)/shard_map/ppermute | solution.py:630
  58.0 12.8 %collective-permute-start.12 = (bf16[96,1600]{1,0:T(8,128)(2,1)}, bf16[96,1600]{1,0:T(8,128)(2,1)}, u32[]{:S(2)}, u32[]{:S(2)}) collective-permute-start(bf16[96,1600]{1,0:T(8,128)(2,1)} %get-tuple-element.119.refs_6_), channel_id=1, source_target_pairs={{1,2},{2,1},{5,6},{6,5},{9,10},{10,9},{13,14},{14,13},{17,18},{18,... | collective-permute-start | bytes 921608 | tf_op jit(solution)/shard_map/ppermute | solution.py:635
  64.2 14.7 %collective-permute-start.13 = (bf16[96,1600]{1,0:T(8,128)(2,1)}, bf16[96,1600]{1,0:T(8,128)(2,1)}, u32[]{:S(2)}, u32[]{:S(2)}) collective-permute-start(bf16[96,1600]{1,0:T(8,128)(2,1)} %get-tuple-element.122.refs_9_), channel_id=1, source_target_pairs={{0,1},{3,2},{1,0},{2,3},{4,5},{7,6},{5,4},{6,7},{8,9},{11,10},{9,8... | collective-permute-start | bytes 921608 | tf_op jit(solution)/shard_map/ppermute | solution.py:630
  66.7 12.2 %collective-permute-start.14 = (bf16[96,1600]{1,0:T(8,128)(2,1)}, bf16[96,1600]{1,0:T(8,128)(2,1)}, u32[]{:S(2)}, u32[]{:S(2)}) collective-permute-start(bf16[96,1600]{1,0:T(8,128)(2,1)} %get-tuple-element.123.refs_7_), channel_id=1, source_target_pairs={{1,2},{2,1},{5,6},{6,5},{9,10},{10,9},{13,14},{14,13},{17,18},{18,... | collective-permute-start | bytes 921608 | tf_op jit(solution)/shard_map/ppermute | solution.py:635
  81.5 12.1 %collective-permute-start.19 = (bf16[96,1600]{1,0:T(8,128)(2,1)S(1)}, bf16[96,1600]{1,0:T(8,128)(2,1)S(1)}, u32[]{:S(2)}, u32[]{:S(2)}) collective-permute-start(bf16[96,1600]{1,0:T(8,128)(2,1)S(1)} %get-tuple-element.132.refs_8_), channel_id=1, source_target_pairs={{0,1},{3,2},{1,0},{2,3},{4,5},{7,6},{5,4},{6,7},{8,9},{11,10},{9,8... | collective-permute-start | bytes 921608 | tf_op jit(solution)/shard_map/ppermute | solution.py:630
  85.8 13.6 %collective-permute-start.16 = (f32[4,512]{1,0:T(4,128)S(1)}, f32[4,512]{1,0:T(4,128)S(1)}, u32[]{:S(2)}, u32[]{:S(2)}) collective-permute-start(f32[4,512]{1,0:T(4,128)S(1)} %get-tuple-element.127.refs_0_), channel_id=1, source_target_pairs={{0,2},{1,3},{2,0},{3,1},{4,6},{5,7},{6,4},{7,5},{8,10},{9,11},{10,... | collective-permute-start | bytes 24584 | tf_op jit(solution)/shard_map/ppermute | solution.py:624
  89.9 14.9 %collective-permute-start.21 = (bf16[96,1600]{1,0:T(8,128)(2,1)S(1)}, bf16[96,1600]{1,0:T(8,128)(2,1)S(1)}, u32[]{:S(2)}, u32[]{:S(2)}) collective-permute-start(bf16[96,1600]{1,0:T(8,128)(2,1)S(1)} %get-tuple-element.140.refs_9_), channel_id=1, source_target_pairs={{0,1},{3,2},{1,0},{2,3},{4,5},{7,6},{5,4},{6,7},{8,9},{11,10},{9,8... | collective-permute-start | bytes 921608 | tf_op jit(solution)/shard_map/ppermute | solution.py:630
  91.8 13.0 %collective-permute-start.22 = (bf16[96,1600]{1,0:T(8,128)(2,1)S(1)}, bf16[96,1600]{1,0:T(8,128)(2,1)S(1)}, u32[]{:S(2)}, u32[]{:S(2)}) collective-permute-start(bf16[96,1600]{1,0:T(8,128)(2,1)S(1)} %get-tuple-element.141.refs_7_), channel_id=1, source_target_pairs={{1,2},{2,1},{5,6},{6,5},{9,10},{10,9},{13,14},{14,13},{17,18},{18,... | collective-permute-start | bytes 921608 | tf_op jit(solution)/shard_map/ppermute | solution.py:635
  94.5 14.1 %collective-permute-start.25 = (bf16[96,1600]{1,0:T(8,128)(2,1)S(1)}, bf16[96,1600]{1,0:T(8,128)(2,1)S(1)}, u32[]{:S(2)}, u32[]{:S(2)}) collective-permute-start(bf16[96,1600]{1,0:T(8,128)(2,1)S(1)} %get-tuple-element.146.refs_5_), channel_id=1, source_target_pairs={{0,1},{3,2},{1,0},{2,3},{4,5},{7,6},{5,4},{6,7},{8,9},{11,10},{9,8... | collective-permute-start | bytes 921608 | tf_op jit(solution)/shard_map/ppermute | solution.py:630
  109.4 13.6 %collective-permute-start.30 = (bf16[96,1600]{1,0:T(8,128)(2,1)S(1)}, bf16[96,1600]{1,0:T(8,128)(2,1)S(1)}, u32[]{:S(2)}, u32[]{:S(2)}) collective-permute-start(bf16[96,1600]{1,0:T(8,128)(2,1)S(1)} %get-tuple-element.158.refs_3_), channel_id=1, source_target_pairs={{1,0},{2,3},{5,4},{6,7},{9,8},{10,11},{13,12},{14,15},{17,16},{18,... | collective-permute-start | bytes 921608 | tf_op jit(solution)/shard_map/ppermute | solution.py:630
  113.6 16.1 %collective-permute-start.27 = (bf16[96,1600]{1,0:T(8,128)(2,1)S(1)}, bf16[96,1600]{1,0:T(8,128)(2,1)S(1)}, u32[]{:S(2)}, u32[]{:S(2)}) collective-permute-start(bf16[96,1600]{1,0:T(8,128)(2,1)S(1)} %get-tuple-element.149.refs_5_.refs_1_), channel_id=1, source_target_pairs={{1,2},{2,1},{5,6},{6,5},{9,10},{10,9},{13,14},{14,13},{17,18},{18,... | collective-permute-start | bytes 921608 | tf_op jit(solution)/shard_map/ppermute | solution.py:635
  114.3 17.9 %collective-permute-start.28 = (bf16[96,1600]{1,0:T(8,128)(2,1)S(1)}, bf16[96,1600]{1,0:T(8,128)(2,1)S(1)}, u32[]{:S(2)}, u32[]{:S(2)}) collective-permute-start(bf16[96,1600]{1,0:T(8,128)(2,1)S(1)} %get-tuple-element.150.refs_3_), channel_id=1, source_target_pairs={{1,0},{2,3},{5,4},{6,7},{9,8},{10,11},{13,12},{14,15},{17,16},{18,... | collective-permute-start | bytes 921608 | tf_op jit(solution)/shard_map/ppermute | solution.py:630
  123.1 16.5 %collective-permute-start.31 = (bf16[96,1600]{1,0:T(8,128)(2,1)S(1)}, bf16[96,1600]{1,0:T(8,128)(2,1)S(1)}, u32[]{:S(2)}, u32[]{:S(2)}) collective-permute-start(bf16[96,1600]{1,0:T(8,128)(2,1)S(1)} %get-tuple-element.159.refs_20_.refs_1_), channel_id=1, source_target_pairs={{1,0},{2,3},{5,4},{6,7},{9,8},{10,11},{13,12},{14,15},{17,16},{18,... | collective-permute-start | bytes 921608 | tf_op jit(solution)/shard_map/ppermute | solution.py:630
  133.6 15.1 %collective-permute-start.34 = (bf16[2,128,1024]{2,1,0:T(8,128)(2,1)S(1)}, bf16[2,128,1024]{2,1,0:T(8,128)(2,1)S(1)}, u32[]{:S(2)}, u32[]{:S(2)}) collective-permute-start(bf16[2,128,1024]{2,1,0:T(8,128)(2,1)S(1)} %get-tuple-element.187), channel_id=1, source_target_pairs={{0,8},{4,12},{8,0},{12,4},{1,9},{5,13},{9,1},{13,5},{2,10},{6,14},... | collective-permute-start | bytes 1572872 | tf_op jit(solution)/shard_map/ppermute | solution.py:406
  139.5 14.7 %collective-permute-start.35 = (bf16[2,128,1024]{2,1,0:T(8,128)(2,1)S(1)}, bf16[2,128,1024]{2,1,0:T(8,128)(2,1)S(1)}, u32[]{:S(2)}, u32[]{:S(2)}) collective-permute-start(bf16[2,128,1024]{2,1,0:T(8,128)(2,1)S(1)} %get-tuple-element.188), channel_id=1, source_target_pairs={{0,12},{4,8},{8,4},{12,0},{1,13},{5,9},{9,5},{13,1},{2,14},{6,10},... | collective-permute-start | bytes 1572872 | tf_op jit(solution)/shard_map/ppermute | solution.py:406
  (77 other events, 725.2 us)
